TPU v7x, 32 devices: a whole 2x2x4 slice. The times are simulated.
32 devices in a mesh: dp: 4 (over z), fsdp: 8 (over y, x, core).
Axes of the slice: x: 2, y: 2, z: 4, core: 2. Of those that a mesh axis runs over, the one named last changes fastest.
Arguments:
- tokens: bfloat16 [8192, 2048], P(('dp', 'fsdp')), may hold values from -6 to 6
- positions: int32 [8192], P(('dp', 'fsdp')), may hold values from -1 to 255, as said below
- cotangent: bfloat16 [8192, 2048], P(('dp', 'fsdp')), may hold values from -6 to 6
- entry_weight: float32 [3, 2048, 2048], P(None, ('dp', 'fsdp')), may hold values from -0.125 to 0.125
- mixing_weight: float32 [1, 2048, 2048], P(None, ('dp', 'fsdp')), may hold values from -0.5 to 0.5
- attention_gain: float32 [1, 2048], P(None, ('dp', 'fsdp')), may hold values from 0.5 to 1.5
- expand_weight: float32 [2, 8192, 2048], P(None, ('dp', 'fsdp')), may hold values from -0.125 to 0.125
- shrink_weight: float32 [1, 2048, 8192], P(None, ('dp', 'fsdp')), may hold values from -0.0625 to 0.0625
- feedforward_gain: float32 [1, 2048], P(None, ('dp', 'fsdp')), may hold values from 0.5 to 1.5
- entry_moment: float32 [3, 2048, 2048], P(None, ('dp', 'fsdp'))
- entry_square: float32 [3, 2048, 2048], P(None, ('dp', 'fsdp')), may hold values from 1024 to 4096
- mixing_moment: float32 [1, 2048, 2048], P(None, ('dp', 'fsdp'))
- mixing_square: float32 [1, 2048, 2048], P(None, ('dp', 'fsdp')), may hold values from 10 to 42
- attention_moment: float32 [1, 2048], P(None, ('dp', 'fsdp'))
- attention_square: float32 [1, 2048], P(None, ('dp', 'fsdp')), may hold values from 512 to 2048
- expand_moment: float32 [2, 8192, 2048], P(None, ('dp', 'fsdp'))
- expand_square: float32 [2, 8192, 2048], P(None, ('dp', 'fsdp')), may hold values from 10 to 42
- shrink_moment: float32 [1, 2048, 8192], P(None, ('dp', 'fsdp'))
- shrink_square: float32 [1, 2048, 8192], P(None, ('dp', 'fsdp')), may hold values from 51 to 204
- feedforward_moment: float32 [1, 2048], P(None, ('dp', 'fsdp'))
- feedforward_square: float32 [1, 2048], P(None, ('dp', 'fsdp')), may hold values from 102 to 409
Outputs:
- layer_output: bfloat16 [8192, 2048], P(('dp', 'fsdp'))
- input_gradient: float32 [8192, 2048], P(('dp', 'fsdp'))
- entry_gradient: float32 [3, 2048, 2048], P(None, ('dp', 'fsdp'))
- mixing_gradient: float32 [1, 2048, 2048], P(None, ('dp', 'fsdp'))
- attention_gradient: float32 [1, 2048], P(None, ('dp', 'fsdp'))
- expand_gradient: float32 [2, 8192, 2048], P(None, ('dp', 'fsdp'))
- shrink_gradient: float32 [1, 2048, 8192], P(None, ('dp', 'fsdp'))
- feedforward_gradient: float32 [1, 2048], P(None, ('dp', 'fsdp'))
- entry_updated: float32 [3, 2048, 2048], P(None, ('dp', 'fsdp'))
- mixing_updated: float32 [1, 2048, 2048], P(None, ('dp', 'fsdp'))
- attention_updated: float32 [1, 2048], P(None, ('dp', 'fsdp'))
- expand_updated: float32 [2, 8192, 2048], P(None, ('dp', 'fsdp'))
- shrink_updated: float32 [1, 2048, 8192], P(None, ('dp', 'fsdp'))
- feedforward_updated: float32 [1, 2048], P(None, ('dp', 'fsdp'))
- entry_momentum: float32 [3, 2048, 2048], P(None, ('dp', 'fsdp'))
- entry_variance: float32 [3, 2048, 2048], P(None, ('dp', 'fsdp'))
- mixing_momentum: float32 [1, 2048, 2048], P(None, ('dp', 'fsdp'))
- mixing_variance: float32 [1, 2048, 2048], P(None, ('dp', 'fsdp'))
- attention_momentum: float32 [1, 2048], P(None, ('dp', 'fsdp'))
- attention_variance: float32 [1, 2048], P(None, ('dp', 'fsdp'))
- expand_momentum: float32 [2, 8192, 2048], P(None, ('dp', 'fsdp'))
- expand_variance: float32 [2, 8192, 2048], P(None, ('dp', 'fsdp'))
- shrink_momentum: float32 [1, 2048, 8192], P(None, ('dp', 'fsdp'))
- shrink_variance: float32 [1, 2048, 8192], P(None, ('dp', 'fsdp'))
- feedforward_momentum: float32 [1, 2048], P(None, ('dp', 'fsdp'))
- feedforward_variance: float32 [1, 2048], P(None, ('dp', 'fsdp'))
Inputs may be any that keep to these rules, and one draw needn't show every extreme that they name: Each device's 256 slots hold whole sequences packed from its first slot, positions counting 0, 1, 2 within each; the remaining slots are -1. Some device holds a single sequence of all 256 slots; every other device has at least one empty slot.
All inputs are finite; a program needn't handle non-finite values.
Results may differ from a plain program's by a relative error of at most 0.015.
The roundings to bfloat16 on the way count: a program that leaves them out, or rounds other values in their place, can miss the bound.
Values may be sent and summed in bfloat16 or wider, within the bound.
No kernel may reach another device: no remote copies, remote signals or barrier semaphores. Data moves between devices by JAX's collectives and lax.ppermute only.
A program may use at most 576 MiB of HBM per device.

v0:
```python
import jax
import jax.numpy as jnp
from jax import lax
from jax.sharding import PartitionSpec as P

HEADS = 32
HEAD = 64
STEP = 3


EPS = 1e-05
THETA = 130000.0
RATE = 0.01
MIXING_RATE = 0.04
GAIN_RATE = 0.3
BETA_ONE = 0.9
BETA_TWO = 0.95
ADAM_EPS = 1e-08
DECAY = 0.1


def contract_last(left, right):
    return lax.dot_general(
        left, right, (((1,), (1,)), ((), ())), preferred_element_type=jnp.float32
    )


def contract_first(left, right):
    return lax.dot_general(
        left, right, (((0,), (0,)), ((), ())), preferred_element_type=jnp.float32
    )


def plain_product(left, right):
    return jnp.dot(left, right, preferred_element_type=jnp.float32)


def rope_tables(positions):
    half = HEAD // 2
    freq = THETA ** (-2.0 * jnp.arange(half, dtype=jnp.float32) / HEAD)
    angle = positions.astype(jnp.float32)[:, None] * freq[None, :]
    return (jnp.cos(angle), jnp.sin(angle))


def rotate(value, cosine, sine):
    half = HEAD // 2
    shaped = value.reshape(value.shape[0], HEADS, HEAD)
    first = shaped[..., :half]
    second = shaped[..., half:]
    cos_rows = cosine[:, None, :]
    sin_rows = sine[:, None, :]
    joined = jnp.concatenate(
        [first * cos_rows - second * sin_rows, second * cos_rows + first * sin_rows], axis=-1
    )
    return joined.reshape(value.shape)


def unrotate(grad, cosine, sine):
    half = HEAD // 2
    shaped = grad.reshape(grad.shape[0], HEADS, HEAD)
    first = shaped[..., :half]
    second = shaped[..., half:]
    cos_rows = cosine[:, None, :]
    sin_rows = sine[:, None, :]
    joined = jnp.concatenate(
        [first * cos_rows + second * sin_rows, second * cos_rows - first * sin_rows], axis=-1
    )
    return joined.reshape(grad.shape)


def norm_back(value, scale, gain, grad):
    weighted = grad * gain
    inner = jnp.mean(weighted * value, axis=-1, keepdims=True)
    back = scale * weighted - value * (scale * scale * scale) * inner
    return (back, jnp.sum(grad * value * scale, axis=0))


def adamw(weight, gradient, moment, square, rate, decay):
    moment_new = BETA_ONE * moment + (1.0 - BETA_ONE) * gradient
    square_new = BETA_TWO * square + (1.0 - BETA_TWO) * gradient * gradient
    corrected = moment_new / (1.0 - BETA_ONE**STEP)
    spread = jnp.sqrt(square_new / (1.0 - BETA_TWO**STEP)) + ADAM_EPS
    return (weight - rate * (corrected / spread + decay * weight), moment_new, square_new)


def gather_attention(entry, mixing, gain):
    return (
        lax.all_gather(entry, ("dp", "fsdp"), axis=1, tiled=True),
        lax.all_gather(mixing, ("dp", "fsdp"), axis=1, tiled=True),
        lax.all_gather(gain, ("dp", "fsdp"), axis=1, tiled=True),
    )


def gather_feedforward(expand, shrink, gain):
    return (
        lax.all_gather(expand, ("dp", "fsdp"), axis=1, tiled=True),
        lax.all_gather(shrink, ("dp", "fsdp"), axis=1, tiled=True),
        lax.all_gather(gain, ("dp", "fsdp"), axis=1, tiled=True),
    )


def reduce_attention(entry, mixing, shrink, gain):
    return (
        lax.psum_scatter(entry, ("dp", "fsdp"), scatter_dimension=1, tiled=True),
        lax.psum_scatter(mixing, ("dp", "fsdp"), scatter_dimension=1, tiled=True),
        lax.psum_scatter(shrink, ("dp", "fsdp"), scatter_dimension=1, tiled=True),
        lax.psum_scatter(gain, ("dp", "fsdp"), scatter_dimension=1, tiled=True),
    )


def reduce_feedforward(expand, gain):
    return (
        lax.psum_scatter(expand, ("dp", "fsdp"), scatter_dimension=1, tiled=True),
        lax.psum_scatter(gain, ("dp", "fsdp"), scatter_dimension=1, tiled=True),
    )


def local(
    tokens,
    positions,
    cotangent,
    entry_weight,
    mixing_weight,
    attention_gain,
    expand_weight,
    shrink_weight,
    feedforward_gain,
    entry_moment,
    entry_square,
    mixing_moment,
    mixing_square,
    attention_moment,
    attention_square,
    expand_moment,
    expand_square,
    shrink_moment,
    shrink_square,
    feedforward_moment,
    feedforward_square,
):
    rows = tokens.shape[0]
    width = tokens.shape[1]
    hidden_width = shrink_weight.shape[2]
    factor = HEAD ** (-0.5)
    inputs = tokens.astype(jnp.float32)
    live = (positions >= 0).astype(jnp.float32)[:, None]
    cosine, sine = rope_tables(positions)
    slots = jnp.arange(rows, dtype=jnp.int32)
    same = positions[:, None] - positions[None, :] == slots[:, None] - slots[None, :]
    visible = same & (slots[None, :] <= slots[:, None])
    entry_low = entry_weight.astype(jnp.bfloat16)
    mixing_low = mixing_weight.astype(jnp.bfloat16)
    attention_low = attention_gain.astype(jnp.bfloat16)
    expand_low = expand_weight.astype(jnp.bfloat16)
    shrink_low = shrink_weight.astype(jnp.bfloat16)
    feedforward_low = feedforward_gain.astype(jnp.bfloat16)
    entry_all, mixing_all, gain_first = gather_attention(entry_low, mixing_low, attention_low)
    gain_one = gain_first[0].astype(jnp.float32)
    scale_one = lax.rsqrt(jnp.mean(inputs * inputs, axis=-1, keepdims=True) + EPS)
    normed = (inputs * scale_one * gain_one).astype(jnp.bfloat16)
    mixed = contract_last(normed, entry_all.reshape(3 * width, width))
    query = rotate(mixed[:, :width], cosine, sine).astype(jnp.bfloat16)
    keys = rotate(mixed[:, width : 2 * width], cosine, sine).astype(jnp.bfloat16)
    values = mixed[:, 2 * width :].astype(jnp.bfloat16)
    query_heads = query.reshape(rows, HEADS, HEAD)
    key_heads = keys.reshape(rows, HEADS, HEAD)
    value_heads = values.reshape(rows, HEADS, HEAD)

    def masked_scores():
        raw = (
            jnp.einsum("qhd,khd->hqk", query_heads, key_heads, preferred_element_type=jnp.float32)
            * factor
        )
        return jnp.where(visible[None], raw, -1e30)

    scores = masked_scores()
    top = jnp.max(scores, axis=-1, keepdims=True)
    weights = jnp.exp(scores - top)
    total = jnp.sum(weights, axis=-1, keepdims=True)
    logsum = top + jnp.log(total)
    probs = (weights / total).astype(jnp.bfloat16)
    attended = (
        jnp.einsum("hqk,khd->qhd", probs, value_heads, preferred_element_type=jnp.float32)
        .reshape(rows, width)
        .astype(jnp.bfloat16)
    )
    middle = inputs + contract_last(attended, mixing_all[0])
    expand_all, shrink_all, gain_second = gather_feedforward(
        expand_low, shrink_low, feedforward_low
    )
    gain_two = gain_second[0].astype(jnp.float32)
    scale_two = lax.rsqrt(jnp.mean(middle * middle, axis=-1, keepdims=True) + EPS)
    normed_two = (middle * scale_two * gain_two).astype(jnp.bfloat16)
    both = contract_last(normed_two, expand_all.reshape(2 * hidden_width, width))
    gate = both[:, :hidden_width]
    upward = both[:, hidden_width:]
    sigma = jax.nn.sigmoid(gate)
    swish = gate * sigma
    hidden = (swish * upward).astype(jnp.bfloat16)
    output = middle + contract_last(hidden, shrink_all[0])
    layer_output = output.astype(jnp.bfloat16)
    grad_out = cotangent.astype(jnp.float32) * live
    grad_low = grad_out.astype(jnp.bfloat16)
    expand_back, shrink_back, gain_second_back = gather_feedforward(
        expand_low, shrink_low, feedforward_low
    )
    hidden_grad = plain_product(grad_low, shrink_back[0])
    gate_grad = hidden_grad * upward * (sigma * (1.0 + gate * (1.0 - sigma)))
    upward_grad = hidden_grad * swish
    both_grad = jnp.concatenate([gate_grad, upward_grad], axis=1).astype(jnp.bfloat16)
    normed_two_grad = plain_product(both_grad, expand_back.reshape(2 * hidden_width, width))
    middle_back, gain_two_grad = norm_back(
        middle, scale_two, gain_second_back[0].astype(jnp.float32), normed_two_grad
    )
    middle_grad = grad_out + middle_back
    expand_grad = contract_first(both_grad, normed_two)
    expand_gradient, feedforward_gradient = reduce_feedforward(
        expand_grad.reshape(2, hidden_width, width), gain_two_grad[None]
    )
    entry_back, mixing_back, gain_first_back = gather_attention(
        entry_low, mixing_low, attention_low
    )
    branch_low = middle_grad.astype(jnp.bfloat16)
    mixing_grad = contract_first(branch_low, attended)
    attended_grad = (
        plain_product(branch_low, mixing_back[0]).astype(jnp.bfloat16).reshape(rows, HEADS, HEAD)
    )
    probs_full = jnp.exp(masked_scores() - logsum)
    prob_grad = jnp.einsum(
        "qhd,khd->hqk", attended_grad, value_heads, preferred_element_type=jnp.float32
    )
    delta = jnp.sum(probs_full * prob_grad, axis=-1, keepdims=True)
    score_grad = (probs_full * (prob_grad - delta)).astype(jnp.bfloat16)
    value_grad = jnp.einsum(
        "hqk,qhd->khd",
        probs_full.astype(jnp.bfloat16),
        attended_grad,
        preferred_element_type=jnp.float32,
    ).reshape(rows, width)
    query_grad = (
        jnp.einsum(
            "hqk,khd->qhd", score_grad, key_heads, preferred_element_type=jnp.float32
        ).reshape(rows, width)
        * factor
    )
    key_grad = (
        jnp.einsum(
            "hqk,qhd->khd", score_grad, query_heads, preferred_element_type=jnp.float32
        ).reshape(rows, width)
        * factor
    )
    mixed_grad = jnp.concatenate(
        [unrotate(query_grad, cosine, sine), unrotate(key_grad, cosine, sine), value_grad], axis=1
    ).astype(jnp.bfloat16)
    entry_grad = contract_first(mixed_grad, normed)
    normed_grad = plain_product(mixed_grad, entry_back.reshape(3 * width, width))
    input_back, gain_one_grad = norm_back(
        inputs, scale_one, gain_first_back[0].astype(jnp.float32), normed_grad
    )
    input_gradient = middle_grad + input_back
    shrink_grad = contract_first(grad_low, hidden)
    entry_gradient, mixing_gradient, shrink_gradient, attention_gradient = reduce_attention(
        entry_grad.reshape(3, width, width),
        mixing_grad[None],
        shrink_grad[None],
        gain_one_grad[None],
    )
    entry_new = adamw(entry_weight, entry_gradient, entry_moment, entry_square, RATE, DECAY)
    mixing_new = adamw(
        mixing_weight, mixing_gradient, mixing_moment, mixing_square, MIXING_RATE, DECAY
    )
    attention_new = adamw(
        attention_gain, attention_gradient, attention_moment, attention_square, GAIN_RATE, 0.0
    )
    expand_new = adamw(expand_weight, expand_gradient, expand_moment, expand_square, RATE, DECAY)
    shrink_new = adamw(shrink_weight, shrink_gradient, shrink_moment, shrink_square, RATE, DECAY)
    feedforward_new = adamw(
        feedforward_gain,
        feedforward_gradient,
        feedforward_moment,
        feedforward_square,
        GAIN_RATE,
        0.0,
    )
    return (
        layer_output,
        input_gradient,
        entry_gradient,
        mixing_gradient,
        attention_gradient,
        expand_gradient,
        shrink_gradient,
        feedforward_gradient,
        entry_new[0],
        mixing_new[0],
        attention_new[0],
        expand_new[0],
        shrink_new[0],
        feedforward_new[0],
        entry_new[1],
        entry_new[2],
        mixing_new[1],
        mixing_new[2],
        attention_new[1],
        attention_new[2],
        expand_new[1],
        expand_new[2],
        shrink_new[1],
        shrink_new[2],
        feedforward_new[1],
        feedforward_new[2],
    )


def solution(mesh):
    placed = (
        P(("dp", "fsdp"), None),
        P(("dp", "fsdp")),
        P(("dp", "fsdp"), None),
        P(None, ("dp", "fsdp"), None),
        P(None, ("dp", "fsdp"), None),
        P(None, ("dp", "fsdp")),
        P(None, ("dp", "fsdp"), None),
        P(None, ("dp", "fsdp"), None),
        P(None, ("dp", "fsdp")),
        P(None, ("dp", "fsdp"), None),
        P(None, ("dp", "fsdp"), None),
        P(None, ("dp", "fsdp"), None),
        P(None, ("dp", "fsdp"), None),
        P(None, ("dp", "fsdp")),
        P(None, ("dp", "fsdp")),
        P(None, ("dp", "fsdp"), None),
        P(None, ("dp", "fsdp"), None),
        P(None, ("dp", "fsdp"), None),
        P(None, ("dp", "fsdp"), None),
        P(None, ("dp", "fsdp")),
        P(None, ("dp", "fsdp")),
    )
    return jax.shard_map(
        local,
        mesh=mesh,
        in_specs=placed,
        out_specs=(
            P(("dp", "fsdp"), None),
            P(("dp", "fsdp"), None),
            P(None, ("dp", "fsdp"), None),
            P(None, ("dp", "fsdp"), None),
            P(None, ("dp", "fsdp")),
            P(None, ("dp", "fsdp"), None),
            P(None, ("dp", "fsdp"), None),
            P(None, ("dp", "fsdp")),
            P(None, ("dp", "fsdp"), None),
            P(None, ("dp", "fsdp"), None),
            P(None, ("dp", "fsdp")),
            P(None, ("dp", "fsdp"), None),
            P(None, ("dp", "fsdp"), None),
            P(None, ("dp", "fsdp")),
            P(None, ("dp", "fsdp"), None),
            P(None, ("dp", "fsdp"), None),
            P(None, ("dp", "fsdp"), None),
            P(None, ("dp", "fsdp"), None),
            P(None, ("dp", "fsdp")),
            P(None, ("dp", "fsdp")),
            P(None, ("dp", "fsdp"), None),
            P(None, ("dp", "fsdp"), None),
            P(None, ("dp", "fsdp"), None),
            P(None, ("dp", "fsdp"), None),
            P(None, ("dp", "fsdp")),
            P(None, ("dp", "fsdp")),
        ),
        check_vma=False,
    )
```

profile of v0, /device:TPU:0, one launch (start us, length us, event | category | flops | bytes accessed | tf_op | source)
XLA Modules:
  0.0 4014.7 jit_solution(10972297825933986984)
XLA Ops:
  16.4 43.2 %all-reduce.2 = (bf16[2048]{0:T(1024)(128)(2,1)S(1)}, bf16[2048]{0:T(1024)(128)(2,1)S(1)}) all-reduce(bf16[2048]{0:T(1024)(128)(2,1)S(1)} %dynamic-update-slice, bf16[2048]{0:T(1024)(128)(2,1)S(1)} %dynamic-update-slice.1), channel_id=1, replica_groups=mesh['dp'=4,'fsdp'=8] {'dp','fsdp'}, use_global_device_ids=true, to_apply=%add | all-reduce | flops 4096 | bytes 16384
  60.8 109.3 %all-gather.5.cloned.1.call-done = bf16[3,2048,2048]{2,1,0:T(8,128)(2,1)} async-done(((bf16[3,64,2048]{2,1,0:T(8,128)(2,1)}), bf16[3,2048,2048]{2,1,0:T(8,128)(2,1)}) %all-gather.5.cloned.1.call-update) | async-done | bytes 25165840 | tf_op jit(solution)/shard_map/all_gather | solution.py:88
  170.1 13.4 fusion.55
  209.0 40.2 %all-gather.7.cloned.1.call-done = bf16[1,2048,2048]{2,1,0:T(8,128)(2,1)} async-done(((bf16[1,64,2048]{2,1,0:T(8,128)(2,1)}), bf16[1,2048,2048]{2,1,0:T(8,128)(2,1)}) %all-gather.7.cloned.1.call-update) | async-done | bytes 8388624 | tf_op jit(solution)/shard_map/all_gather | solution.py:89
  255.5 352.0 %all-gather.9.cloned.1.call-done = bf16[2,8192,2048]{2,1,0:T(8,128)(2,1)} async-done(((bf16[2,256,2048]{2,1,0:T(8,128)(2,1)}), bf16[2,8192,2048]{2,1,0:T(8,128)(2,1)}) %all-gather.9.cloned.1.call-update) | async-done | bytes 67108880 | tf_op jit(solution)/shard_map/all_gather | solution.py:96
  607.5 33.0 fusion.71
  640.5 163.2 %all-gather.11.cloned.1.call-done = bf16[1,2048,8192]{2,1,0:T(8,128)(2,1)} async-done(((bf16[1,64,8192]{2,1,0:T(8,128)(2,1)}), bf16[1,2048,8192]{2,1,0:T(8,128)(2,1)}) %all-gather.11.cloned.1.call-update) | async-done | bytes 33554448 | tf_op jit(solution)/shard_map/all_gather | solution.py:97
  803.8 24.6 multiply_convert_fusion.2
  828.3 29.4 multiply_reduce_fusion.1
  861.0 7.4 fusion.27
  870.7 6.7 fusion.43
  896.1 13.5 fusion.39
  911.1 9.4 convolution_bitcast_fusion.1
  922.1 20.8 fusion.46
  944.1 25.5 convolution_bitcast_fusion
  971.2 47.4 %fusion.11 = f32[16384,2048]{1,0:T(8,128)} fusion(bf16[256,8192]{1,0:T(8,128)(2,1)} %get-tuple-element.51, bf16[256,8192]{1,0:T(8,128)(2,1)} %get-tuple-element.50, f32[256,2048]{1,0:T(8,128)S(1)} %copy-done.5, f32[2048]{0:T(1024)S(1)} %mul.644, f32[256]{0:T(256)S(1)} %get-tuple-element.72), kind=kOutput, calls=%fused_computation.25 | convolution fusion | flops 17198219264 | bytes 144712704 | tf_op jit(solution)/shard_map/dot_general | solution.py:29
  1023.7 17.5 fusion.24
  1042.0 116.3 %reduce-scatter.19.cloned.1.call-done = f32[64,1]{1,0:T(8,128)} async-done(((f32[2048,1]{1,0:T(8,128)}), f32[64,1]{1,0:T(8,128)}) %reduce-scatter.19.cloned.1.call-update) | async-done | bytes 272
  1160.3 179.7 %reduce-scatter.13.cloned.1.call-done = f32[1,64,2048]{2,1,0:T(8,128)} async-done(((f32[1,2048,2048]{2,1,0:T(8,128)}), f32[1,64,2048]{2,1,0:T(8,128)}) %reduce-scatter.13.cloned.1.call-update) | async-done | bytes 524304 | tf_op jit(solution)/shard_map/reduce_scatter | solution.py:105
  1342.5 530.2 %reduce-scatter.11.cloned.1.call-done = f32[3,64,2048]{2,1,0:T(8,128)} async-done(((f32[3,2048,2048]{2,1,0:T(8,128)}), f32[3,64,2048]{2,1,0:T(8,128)}) %reduce-scatter.11.cloned.1.call-update) | async-done | bytes 1572880 | tf_op jit(solution)/shard_map/reduce_scatter | solution.py:104
  1878.6 708.3 %reduce-scatter.17.cloned.1.call-done = f32[1,64,8192]{2,1,0:T(8,128)} async-done(((f32[1,2048,8192]{2,1,0:T(8,128)}), f32[1,64,8192]{2,1,0:T(8,128)}) %reduce-scatter.17.cloned.1.call-update) | async-done | bytes 2097168 | tf_op jit(solution)/shard_map/reduce_scatter | solution.py:106
  2586.9 6.6 multiply_subtract_fusion.1
  2593.5 1403.0 %reduce-scatter.15.cloned.1.call-done = f32[2,256,2048]{2,1,0:T(8,128)} async-done(((f32[2,8192,2048]{2,1,0:T(8,128)}), f32[2,256,2048]{2,1,0:T(8,128)}) %reduce-scatter.15.cloned.1.call-update) | async-done | bytes 4194320 | tf_op jit(solution)/shard_map/reduce_scatter | solution.py:113
  3996.5 10.9 multiply_subtract_fusion
  (176 shorter events, 87.9 us)
Async XLA Ops:
  7.2 162.9 %all-gather.5.cloned.1.call-start = ((), (), s32[]{:S(2)}) async-start(), calls=%async_computation.6 | async-start | bytes 25952256 | tf_op jit(solution)/shard_map/all_gather | solution.py:88
  9.7 239.5 %all-gather.7.cloned.1.call-start = ((), (), s32[]{:S(2)}) async-start(), calls=%async_computation.7 | async-start | bytes 8650752 | tf_op jit(solution)/shard_map/all_gather | solution.py:89
  10.6 596.9 %all-gather.9.cloned.1.call-start = ((), (), s32[]{:S(2)}) async-start(), calls=%async_computation.8 | async-start | bytes 69206016 | tf_op jit(solution)/shard_map/all_gather | solution.py:96
  14.6 789.1 %all-gather.11.cloned.1.call-start = ((), (), s32[]{:S(2)}) async-start(), calls=%async_computation.9 | async-start | bytes 34603008 | tf_op jit(solution)/shard_map/all_gather | solution.py:97
  15.8 1025.4 %reduce-scatter.21.cloned.1.call-start = ((), (), s32[]{:S(2)}) async-start(), calls=%async_computation.15 | async-start | bytes 1081344
  60.6 137.4 %copy-start.29 = (f32[256,32]{0,1:T(8,128)}, f32[256,32]{0,1:T(8,128)S(1)}, u32[]{:S(2)}) copy-start(f32[256,32]{0,1:T(8,128)S(1)} %get-tuple-element.67) | copy-start | bytes 98308
  60.7 137.4 %copy-start.31 = (f32[256,32]{0,1:T(8,128)}, f32[256,32]{0,1:T(8,128)S(1)}, u32[]{:S(2)}) copy-start(f32[256,32]{0,1:T(8,128)S(1)} %get-tuple-element.68) | copy-start | bytes 98308
  255.5 572.9 %copy-start.4 = (f32[256,2048]{1,0:T(8,128)}, f32[256,2048]{1,0:T(8,128)S(1)}, u32[]{:S(2)}) copy-start(f32[256,2048]{1,0:T(8,128)S(1)} %get-tuple-element.76) | copy-start | bytes 6291460
  891.7 266.6 %reduce-scatter.19.cloned.1.call-start = ((), (), s32[]{:S(2)}) async-start(), calls=%async_computation.14 | async-start | bytes 1081344
  911.0 429.0 %reduce-scatter.13.cloned.1.call-start = ((), (), s32[]{:S(2)}) async-start(), calls=%async_computation.11 | async-start | bytes 17301504 | tf_op jit(solution)/shard_map/reduce_scatter | solution.py:105
  920.5 952.1 %reduce-scatter.11.cloned.1.call-start = ((), (), s32[]{:S(2)}) async-start(), calls=%async_computation.10 | async-start | bytes 51904512 | tf_op jit(solution)/shard_map/reduce_scatter | solution.py:104
  942.9 1644.1 %reduce-scatter.17.cloned.1.call-start = ((), (), s32[]{:S(2)}) async-start(), calls=%async_computation.13 | async-start | bytes 69206016 | tf_op jit(solution)/shard_map/reduce_scatter | solution.py:106
  969.6 3026.9 %reduce-scatter.15.cloned.1.call-start = ((), (), s32[]{:S(2)}) async-start(), calls=%async_computation.12 | async-start | bytes 138412032 | tf_op jit(solution)/shard_map/reduce_scatter | solution.py:113
  1023.6 135.6 %copy-start.44 = (f32[1,64]{1,0:T(1,128)S(1)}, f32[1,64]{1,0:T(1,128)}, u32[]{:S(2)}) copy-start(f32[1,64]{1,0:T(1,128)} %param.40) | copy-start | bytes 772
  1023.6 135.6 %copy-start.45 = (f32[1,64]{1,0:T(1,128)S(1)}, f32[1,64]{1,0:T(1,128)}, u32[]{:S(2)}) copy-start(f32[1,64]{1,0:T(1,128)} %param.41) | copy-start | bytes 772
  1023.6 136.1 %copy-start.47 = (f32[1,64]{1,0:T(1,128)S(1)}, f32[1,64]{1,0:T(1,128)}, u32[]{:S(2)}) copy-start(f32[1,64]{1,0:T(1,128)} %param.26) | copy-start | bytes 772
  1023.6 136.1 %copy-start.48 = (f32[1,64]{1,0:T(1,128)S(1)}, f32[1,64]{1,0:T(1,128)}, u32[]{:S(2)}) copy-start(f32[1,64]{1,0:T(1,128)} %param.34) | copy-start | bytes 772
  1023.6 136.1 %copy-start.49 = (f32[1,64]{1,0:T(1,128)S(1)}, f32[1,64]{1,0:T(1,128)}, u32[]{:S(2)}) copy-start(f32[1,64]{1,0:T(1,128)} %param.35) | copy-start | bytes 772
  1023.6 316.4 %copy-start.25 = (f32[1,64,2048]{2,1,0:T(8,128)S(1)}, f32[1,64,2048]{2,1,0:T(8,128)}, u32[]{:S(2)}) copy-start(f32[1,64,2048]{2,1,0:T(8,128)} %param.25) | copy-start | bytes 1572868
  1023.7 316.4 %copy-start.27 = (f32[1,64,2048]{2,1,0:T(8,128)S(1)}, f32[1,64,2048]{2,1,0:T(8,128)}, u32[]{:S(2)}) copy-start(f32[1,64,2048]{2,1,0:T(8,128)} %param.32) | copy-start | bytes 1572868
  1023.7 316.3 %copy-start.28 = (f32[1,64,2048]{2,1,0:T(8,128)S(1)}, f32[1,64,2048]{2,1,0:T(8,128)}, u32[]{:S(2)}) copy-start(f32[1,64,2048]{2,1,0:T(8,128)} %param.33) | copy-start | bytes 1572868
  1042.0 836.6 %copy-start.39 = (f32[1,64]{1,0:T(1,128)}, f32[1,64]{1,0:T(1,128)S(1)}, u32[]{:S(2)}) copy-start(f32[1,64]{1,0:T(1,128)S(1)} %copy.82) | copy-start | bytes 772
  1159.2 719.4 %copy-start.40 = (f32[1,64]{1,0:T(1,128)}, f32[1,64]{1,0:T(1,128)S(1)}, u32[]{:S(2)}) copy-start(f32[1,64]{1,0:T(1,128)S(1)} %copy.80) | copy-start | bytes 772
  1342.5 1244.5 %copy-start.7 = (f32[1,64,8192]{2,1,0:T(8,128)S(1)}, f32[1,64,8192]{2,1,0:T(8,128)}, u32[]{:S(2)}) copy-start(f32[1,64,8192]{2,1,0:T(8,128)} %param.28) | copy-start | bytes 6291460
  (38 other events, 593.3 us)
Sparse Core Ops, SparseCore 0:
  11.5 158.5 all-gather.4
  173.5 75.6 all-gather.6
  252.7 354.7 all-gather.8
  610.8 192.9 all-gather.10
  891.8 132.9 reduce-scatter.20
  1027.6 130.6 reduce-scatter.18
  1161.2 178.7 reduce-scatter.12
  1342.9 529.7 reduce-scatter.10
  1875.6 711.2 reduce-scatter.16
  2589.7 1406.7 reduce-scatter.14
where the time goes:
time: 4030 us; the launch traced here: 4010 us
  waiting for transfers between devices  3600 us (89%)
  matrix products  270 us (7%)
  other arithmetic  52.8 us (1%)
  blocking collectives  43.2 us (1%)
    reduce_scatter x1, waiting for transfers between devices, reduce_feedforward(): lax.psum_scatter(expand, ('dp', 'fsdp'), scatter_dimension=1, tiled=True)  1400 us
    reduce_scatter x1, waiting for transfers between devices, reduce_attention(): lax.psum_scatter(shrink, ('dp', 'fsdp'), scatter_dimension=1, tiled=True)  708 us
    reduce_scatter x1, waiting for transfers between devices, reduce_attention(): lax.psum_scatter(entry, ('dp', 'fsdp'), scatter_dimension=1, tiled=True)  530 us
    all_gather x1, waiting for transfers between devices, gather_feedforward(): lax.all_gather(expand, ('dp', 'fsdp'), axis=1, tiled=True)  352 us
    reduce_scatter x1, waiting for transfers between devices, reduce_attention(): lax.psum_scatter(mixing, ('dp', 'fsdp'), scatter_dimension=1, tiled=True)  180 us
    all_gather x1, waiting for transfers between devices, gather_feedforward(): lax.all_gather(shrink, ('dp', 'fsdp'), axis=1, tiled=True)  163 us
    unnamed x12, waiting for transfers between devices  116 us
    all_gather x1, waiting for transfers between devices, gather_attention(): lax.all_gather(entry, ('dp', 'fsdp'), axis=1, tiled=True)  109 us
  transfers between devices with their start and end apart: 10, of which 9 were waited for; matrix products, arithmetic and copies ran while one was open for 6% of the time, Pallas kernels for 0%

commit v1 on v0

v1 whole, which is shorter than its diff:
```python
import functools
import jax
import jax.numpy as jnp
from jax import lax
from jax.sharding import PartitionSpec as P

HEADS = 32
HEAD = 64
STEP = 3


EPS = 1e-05
THETA = 130000.0
RATE = 0.01
MIXING_RATE = 0.04
GAIN_RATE = 0.3
BETA_ONE = 0.9
BETA_TWO = 0.95
ADAM_EPS = 1e-08
DECAY = 0.1


def contract_last(left, right):
    return lax.dot_general(
        left, right, (((1,), (1,)), ((), ())), preferred_element_type=jnp.float32
    )


def contract_first(left, right):
    return lax.dot_general(
        left, right, (((0,), (0,)), ((), ())), preferred_element_type=jnp.float32
    )


def plain_product(left, right):
    return jnp.dot(left, right, preferred_element_type=jnp.float32)


def rope_tables(positions):
    half = HEAD // 2
    freq = THETA ** (-2.0 * jnp.arange(half, dtype=jnp.float32) / HEAD)
    angle = positions.astype(jnp.float32)[:, None] * freq[None, :]
    return (jnp.cos(angle), jnp.sin(angle))


def rotate(value, cosine, sine):
    half = HEAD // 2
    shaped = value.reshape(value.shape[0], -1, HEAD)
    first = shaped[..., :half]
    second = shaped[..., half:]
    cos_rows = cosine[:, None, :]
    sin_rows = sine[:, None, :]
    joined = jnp.concatenate(
        [first * cos_rows - second * sin_rows, second * cos_rows + first * sin_rows], axis=-1
    )
    return joined.reshape(value.shape)


def unrotate(grad, cosine, sine):
    half = HEAD // 2
    shaped = grad.reshape(grad.shape[0], -1, HEAD)
    first = shaped[..., :half]
    second = shaped[..., half:]
    cos_rows = cosine[:, None, :]
    sin_rows = sine[:, None, :]
    joined = jnp.concatenate(
        [first * cos_rows + second * sin_rows, second * cos_rows - first * sin_rows], axis=-1
    )
    return joined.reshape(grad.shape)


def norm_back(value, scale, gain, grad):
    weighted = grad * gain
    inner = jnp.mean(weighted * value, axis=-1, keepdims=True)
    back = scale * weighted - value * (scale * scale * scale) * inner
    return (back, jnp.sum(grad * value * scale, axis=0))


def adamw(weight, gradient, moment, square, rate, decay):
    moment_new = BETA_ONE * moment + (1.0 - BETA_ONE) * gradient
    square_new = BETA_TWO * square + (1.0 - BETA_TWO) * gradient * gradient
    corrected = moment_new / (1.0 - BETA_ONE**STEP)
    spread = jnp.sqrt(square_new / (1.0 - BETA_TWO**STEP)) + ADAM_EPS
    return (weight - rate * (corrected / spread + decay * weight), moment_new, square_new)


AXES = ("dp", "fsdp")
BF16 = jnp.bfloat16
F32 = jnp.float32


def add_low(*values):
    return sum(value.astype(F32) for value in values).astype(BF16)


class Plan:
    def __init__(self, dp, fsdp):
        self.dp, self.fsdp = dp, fsdp
        self.clock = None
        self.bits = [1 << k for k in range(1, (fsdp - 1).bit_length())] + [1]
        self.short = fsdp == 8

    def tie(self, values):
        if self.clock is None:
            return tuple(values)
        return lax.optimization_barrier((tuple(values), self.clock))[0]

    def step(self, work, *values):
        found = work(*self.tie(values))
        self.clock = jax.tree.leaves(found)[0]
        return found

    def window(self, sends, *works):
        values = self.tie([value for value, _ in sends])
        came = []
        for value, (_, mask) in zip(values, sends):
            axis, count = ("fsdp", self.fsdp) if mask > 0 else ("dp", self.dp)
            pairs = [(i, i ^ abs(mask)) for i in range(count)]
            came.append(lax.ppermute(value, axis, pairs))
        gave = [work() for work in works]
        came, self.clock = lax.optimization_barrier((came, self.clock))
        return came, gave

    def wait(self, value):
        value, self.clock = lax.optimization_barrier((value, self.clock))
        return value

    def spread(self, block, marks=None, works=((), (), ())):
        small = marks is not None
        gave = []
        if self.short:
            half = block.shape[0] // 2
            (beside, above, other, *got), found = self.window(
                [(block, 2), (block, 4), (block, 1)] + [(marks, 2)] * small, *works[0]
            )
            gave += found
            if small:
                marks = self.step(lambda a, b: jnp.concatenate([a, b]), marks, *got)
            upper, lower, pair = self.step(
                lambda a, b: (a[:half], b[half:], jnp.concatenate([b, a])), above, beside
            )
            (first, second, pair, *got), found = self.window(
                [(upper, 2), (lower, 4), (pair, 1)] + [(marks, 4)] * small, *works[1]
            )
            gave += found
            across = self.step(lambda a, b: jnp.concatenate([a, b]), first, second)
            if small:
                marks = self.step(lambda a, b: jnp.concatenate([a, b]), marks, *got)
            near = [block, beside, above, across]
            (far, *got), found = self.window(
                [(across, 1)] + [(marks, 1)] * small, *[functools.partial(w, near) for w in works[2]]
            )
            size = block.shape[0]
            return near, [other, pair[:size], pair[size:], far], (marks, *got), gave + found
        near = [block]
        for bit in self.bits[:-1]:
            got, _ = self.window([(piece, bit) for piece in near] + [(marks, bit)] * small)
            if small:
                marks = jnp.concatenate([marks, got[-1]])
            near = near + got[: len(near)]
        for work in [*works[0], *works[1]]:
            gave.append(work())
        got, found = self.window(
            [(piece, 1) for piece in near] + [(marks, 1)] * small,
            *[functools.partial(w, near) for w in works[2]],
        )
        return near, got[: len(near)], (marks, *got[len(near) :]), gave + found

    def settle(self, near, far, rows, works=((), (), ()), small=None):
        gave = []

        def sends(bit):
            return [] if small is None else [(small[bit:], bit)]

        def sum_small(got, bit):
            if got:
                return self.step(lambda a, b: a[:bit] + b, small, *got)
            return None

        if not self.short:
            terms = jnp.concatenate([near(), far])
            for work in [*works[0], *works[1], *works[2]]:
                gave.append(work())
            for bit in reversed(self.bits):
                size = terms.shape[0] // 2
                (got,), _ = self.window([(terms[size:], bit)])
                terms = self.step(add_low, terms[:size], got)
            if small is not None:
                for bit in sorted(self.bits, reverse=True):
                    small = sum_small(self.window(sends(bit))[0], bit)
            return (terms, jnp.zeros_like(terms), jnp.zeros_like(terms)), gave, small
        half = rows // 2
        (got, *more), (near, *found) = self.window([(far, 1)] + sends(4), near, *works[0])
        gave += found
        small = sum_small(more, 4)
        sums = self.step(add_low, near, got)
        across = sums[3 * rows :]
        (first, second, *more), found = self.window(
            [(across[:half], 2), (across[half:], 4)] + sends(2), *works[1]
        )
        gave += found
        small = sum_small(more, 2)

        def merge(sums, first, second):
            beside, above = sums[rows : 2 * rows], sums[2 * rows : 3 * rows]
            return (
                jnp.concatenate([beside[:half], add_low(beside[half:], second)]),
                jnp.concatenate([add_low(above[:half], first), above[half:]]),
            )

        beside, above = self.step(merge, sums, first, second)
        (beside, above, *more), found = self.window([(beside, 2), (above, 4)] + sends(1), *works[2])
        small = sum_small(more, 1)
        return (sums[:rows], beside, above), gave + found, small

    def columns_out(self, shard):
        rows, columns = shard.shape
        width = columns // (self.dp * self.fsdp)
        blocks = shard.reshape(rows, self.dp, self.fsdp, width).transpose(2, 0, 1, 3)
        return lax.all_to_all(
            blocks.reshape(self.fsdp, rows, self.dp * width), "fsdp", 0, 0, tiled=True
        )

    def columns_back(self, blocks):
        rows = blocks.shape[0] // self.fsdp
        width = blocks.shape[1] // self.dp
        blocks = lax.all_to_all(
            blocks.reshape(self.fsdp, rows, self.dp * width), "fsdp", 0, 0, tiled=True
        )
        blocks = blocks.reshape(self.fsdp, rows, self.dp, width).transpose(1, 2, 0, 3)
        return blocks.reshape(rows, self.dp * self.fsdp * width)


def local(
    dp,
    fsdp,
    tokens,
    positions,
    cotangent,
    entry_weight,
    mixing_weight,
    attention_gain,
    expand_weight,
    shrink_weight,
    feedforward_gain,
    entry_moment,
    entry_square,
    mixing_moment,
    mixing_square,
    attention_moment,
    attention_square,
    expand_moment,
    expand_square,
    shrink_moment,
    shrink_square,
    feedforward_moment,
    feedforward_square,
):
    plan = Plan(dp, fsdp)
    step, window, wait = plan.step, plan.window, plan.wait
    rows = tokens.shape[0]
    width = tokens.shape[1]
    group = fsdp // 2
    whole_heads = entry_weight.shape[1] == HEAD
    heads = HEADS // fsdp
    span = heads * HEAD
    factor = HEAD ** (-0.5)
    state = {}

    def work(call, *values):
        return lambda *_: step(call, *values)

    def store(name, call, *values):
        def run(*_):
            state[name] = step(call, *values)

        return run

    def low_of(value):
        return value.astype(BF16)

    join = lambda *a: jnp.concatenate(a)
    product_last = lambda a, b: contract_last(a, b).astype(BF16)
    product_plain = lambda a, b: plain_product(a, b).astype(BF16)

    def product_pairs(a, b, c, d):
        return (contract_first(a, b) + contract_first(c, d)).astype(BF16)

    entry_low = step(low_of, entry_weight)
    role = lax.axis_index("fsdp")
    if whole_heads:
        entry_role = lax.all_gather(entry_low, "dp", axis=1, tiled=True)
    else:
        entry_all = lax.all_gather(entry_low, AXES, axis=1, tiled=True)
        entry_role = lax.dynamic_slice_in_dim(entry_all, role * span, span, axis=1)

    def gains_dp():
        gains = jnp.concatenate([attention_gain, feedforward_gain]).astype(BF16)[:, None]
        return lax.all_gather(gains, "dp", axis=1, tiled=True)

    def gains_fsdp(gains):
        gains = lax.all_gather(gains[:, :, None], "fsdp", axis=2, tiled=True)
        return gains.reshape(2, width).astype(F32)

    def columns_work(shrink_low, mixing_low):
        return plan.columns_out(shrink_low), plan.columns_out(mixing_low)

    def norm_group(gain, places, *blocks):
        group_tokens = jnp.concatenate(blocks)
        group_inputs = group_tokens.astype(F32)
        scale = lax.rsqrt(jnp.mean(group_inputs * group_inputs, axis=-1, keepdims=True) + EPS)
        return (group_inputs * scale * gain).astype(BF16), group_tokens, scale

    def norm_near(near):
        state["near"] = step(norm_group, state["gains"][0], None, *near)

    spread_tokens, far_tokens, (near_places, far_places), _ = plan.spread(
        tokens,
        positions[None],
        (
            [
                store("gate_low", lambda a: a[0].astype(BF16), expand_weight),
                store("gains_dp", gains_dp),
                store("up_low", lambda a: a[1].astype(BF16), expand_weight),
            ],
            [
                lambda: state.update(gains=step(gains_fsdp, state["gains_dp"])),
                store("mixing_low", low_of, mixing_weight[0]),
                store("shrink_low", low_of, shrink_weight[0]),
            ],
            [lambda near: state.update(columns=step(columns_work, state["shrink_low"], state["mixing_low"])), norm_near],
        ),
    )
    gain_one, gain_two = state["gains"][0], state["gains"][1]
    shrink_blocks, mixing_blocks = state["columns"]
    gate_role = lax.all_gather(state["gate_low"], "dp", axis=0, tiled=True)
    if whole_heads:
        mixing_role = lax.all_gather(mixing_blocks, "dp", axis=0, tiled=True).reshape(width, span)
    else:
        mixing_all = lax.all_gather(state["mixing_low"], AXES, axis=0, tiled=True)
        mixing_role = lax.dynamic_slice_in_dim(mixing_all, role * span, span, axis=1)
    up_role = lax.all_gather(state["up_low"], "dp", axis=0, tiled=True)
    shrink_role = lax.all_gather(shrink_blocks, "dp", axis=0, tiled=True).reshape(width, -1)

    def heads_of(value):
        return value.reshape(group, rows, heads, HEAD)

    def project(normed, entry_role, places):
        cosine, sine = rope_tables(places.reshape(-1))
        mixed = contract_last(normed, entry_role)
        return (
            rotate(mixed[:, :span], cosine, sine).astype(BF16),
            rotate(mixed[:, span : 2 * span], cosine, sine).astype(BF16),
            mixed[:, 2 * span :].astype(BF16),
            cosine,
            sine,
        )

    def attend(query, keys, values, places):
        slots = jnp.arange(rows, dtype=jnp.int32)
        same = places[:, :, None] - places[:, None, :] == slots[:, None] - slots[None, :]
        visible = (same & (slots[None, :] <= slots[:, None]))[:, None]
        raw = jnp.einsum(
            "bqhd,bkhd->bhqk", heads_of(query), heads_of(keys), preferred_element_type=F32
        )
        scores = jnp.where(visible, raw * factor, -1e30)
        top = jnp.max(scores, axis=-1, keepdims=True)
        weights = jnp.exp(scores - top)
        probs_full = weights / jnp.sum(weights, axis=-1, keepdims=True)
        attended = (
            jnp.einsum(
                "bhqk,bkhd->bqhd",
                probs_full.astype(BF16),
                heads_of(values),
                preferred_element_type=F32,
            )
            .reshape(group * rows, span)
            .astype(BF16)
        )
        return attended, probs_full

    inputs = tokens.astype(F32)
    live = (positions >= 0).astype(F32)[:, None]
    grad_out = cotangent.astype(F32) * live
    grad_low = step(low_of, grad_out)
    state["far"] = step(norm_group, gain_one, None, *far_tokens)
    entry_role = wait(entry_role).reshape(3 * span, width)

    def project_work(name, places):
        def run(*_):
            state["qkv " + name] = step(project, state[name][0], entry_role, places)

        return run

    def attend_work(name, places):
        def run(*_):
            state["attend " + name] = step(attend, *state["qkv " + name][:3], places)

        return run

    near_grad, far_grad, _, _ = plan.spread(
        grad_low,
        None,
        (
            [project_work("far", far_places), project_work("near", near_places)],
            [attend_work("far", far_places)],
            [attend_work("near", near_places)],
        ),
    )
    gate_role = wait(gate_role)
    mixing_role = wait(mixing_role)
    far = step(product_last, state["attend far"][0], mixing_role)
    near = work(product_last, state["attend near"][0], mixing_role)
    parts, _, _ = plan.settle(
        near, far, rows, ([], [store("grad near", join, *near_grad)], [store("grad far", join, *far_grad)])
    )

    def norm_middle(inputs, gain, own, beside, above):
        middle = inputs + own.astype(F32) + beside.astype(F32) + above.astype(F32)
        scale = lax.rsqrt(jnp.mean(middle * middle, axis=-1, keepdims=True) + EPS)
        return (middle * scale * gain).astype(BF16), middle, scale

    low_two, middle, scale_two = step(norm_middle, inputs, gain_two, *parts)

    def expand(normed, gate_role, up_role):
        gate = contract_last(normed, gate_role)
        upward = contract_last(normed, up_role)
        return gate, upward, (gate * jax.nn.sigmoid(gate) * upward).astype(BF16)

    def expand_near(near):
        state["two near"] = step(join, *near)
        state["up near"] = step(expand, state["two near"], gate_role, wait(up_role))

    _, far_two, _, _ = plan.spread(low_two, None, ([], [], [expand_near]))
    state["two far"] = step(join, *far_two)
    state["up far"] = step(expand, state["two far"], gate_role, up_role)
    shrink_grad = step(
        product_pairs, state["grad near"], state["up near"][2], state["grad far"], state["up far"][2]
    )
    shrink_summed = lax.psum_scatter(shrink_grad, "dp", scatter_dimension=0, tiled=True)
    shrink_role = wait(shrink_role)

    def back(gate, upward, grad_group, shrink_role):
        sigma = jax.nn.sigmoid(gate)
        swish = gate * sigma
        hidden_grad = plain_product(grad_group, shrink_role)
        gate_grad = hidden_grad * upward * (sigma * (1.0 + gate * (1.0 - sigma)))
        upward_grad = hidden_grad * swish
        return gate_grad.astype(BF16), upward_grad.astype(BF16)

    def back_terms(gate_grad, up_grad, gate_role, up_role):
        return (plain_product(gate_grad, gate_role) + plain_product(up_grad, up_role)).astype(BF16)

    far_back = step(back, *state["up far"][:2], state["grad far"], shrink_role)
    far = step(back_terms, *far_back, gate_role, up_role)
    near_back = step(back, *state["up near"][:2], state["grad near"], shrink_role)

    def expand_grad(index):
        return work(
            product_pairs, near_back[index], state["two near"], far_back[index], state["two far"]
        )

    parts, (gate_grad, up_grad), _ = plan.settle(
        work(back_terms, *near_back, gate_role, up_role),
        far,
        rows,
        ([], [expand_grad(0)], [expand_grad(1)]),
    )
    gate_summed = lax.psum_scatter(gate_grad, "dp", scatter_dimension=0, tiled=True)
    up_summed = lax.psum_scatter(up_grad, "dp", scatter_dimension=0, tiled=True)

    shrink_summed = wait(shrink_summed)

    def shrink_update(summed, *values):
        gradient = plan.columns_back(summed)[None].astype(F32)
        return gradient, *adamw(values[0], gradient, *values[1:], RATE, DECAY)

    def expand_update(gate, up, weight, moment, square):
        gradient = jnp.stack([gate, up]).astype(F32)
        return gradient, *adamw(weight, gradient, moment, square, RATE, DECAY)

    def back_two(middle, scale, gain, grad_out, own, beside, above):
        grad = own.astype(F32) + beside.astype(F32) + above.astype(F32)
        middle_back, gain_grad = norm_back(middle, scale, gain, grad)
        middle_grad = grad_out + middle_back
        return middle_grad.astype(BF16), middle_grad, gain_grad

    branch_low, middle_grad, gain_two_grad = step(
        back_two, middle, scale_two, gain_two, grad_out, *parts
    )

    def branch_near(near):
        state["branch near"] = step(join, *near)
        state["do near"] = step(product_plain, state["branch near"], mixing_role)

    _, far_branch, _, (far_output, near_output, *_) = plan.spread(
        branch_low,
        None,
        (
            [
                work(product_last, state["up far"][2], shrink_role),
                work(product_last, state["up near"][2], shrink_role),
            ],
            [store("shrink", shrink_update, shrink_summed, shrink_weight, shrink_moment, shrink_square)],
            [branch_near],
        ),
    )
    state["branch far"] = step(join, *far_branch)
    state["do far"] = step(product_plain, state["branch far"], mixing_role)

    gate_summed = wait(gate_summed)

    def attend_back(query, keys, values, cosine, sine, probs_full, attended_grad):
        query_heads, key_heads, value_heads = heads_of(query), heads_of(keys), heads_of(values)
        attended_grad = heads_of(attended_grad)
        prob_grad = jnp.einsum(
            "bqhd,bkhd->bhqk", attended_grad, value_heads, preferred_element_type=F32
        )
        delta = jnp.sum(probs_full * prob_grad, axis=-1, keepdims=True)
        score_grad = (probs_full * (prob_grad - delta)).astype(BF16)
        value_grad = jnp.einsum(
            "bhqk,bqhd->bkhd", probs_full.astype(BF16), attended_grad, preferred_element_type=F32
        ).reshape(group * rows, span)
        query_grad = (
            jnp.einsum(
                "bhqk,bkhd->bqhd", score_grad, key_heads, preferred_element_type=F32
            ).reshape(group * rows, span)
            * factor
        )
        key_grad = (
            jnp.einsum(
                "bhqk,bqhd->bkhd", score_grad, query_heads, preferred_element_type=F32
            ).reshape(group * rows, span)
            * factor
        )
        return jnp.concatenate(
            [unrotate(query_grad, cosine, sine), unrotate(key_grad, cosine, sine), value_grad],
            axis=1,
        ).astype(BF16)

    def attend_back_work(name):
        return store(
            "mixed " + name,
            attend_back,
            *state["qkv " + name],
            state["attend " + name][1],
            state["do " + name],
        )

    parts, (mixing_grad, *_), _ = plan.settle(
        lambda: near_output,
        far_output,
        rows,
        (
            [
                work(
                    product_pairs,
                    state["branch near"],
                    state["attend near"][0],
                    state["branch far"],
                    state["attend far"][0],
                )
            ],
            [attend_back_work("far")],
            [attend_back_work("near")],
        ),
    )
    if whole_heads:
        mixing_summed = lax.psum_scatter(mixing_grad, "dp", scatter_dimension=0, tiled=True)
    layer_output = step(
        lambda *a: sum((value.astype(F32) for value in a[1:]), a[0]).astype(BF16), middle, *parts
    )
    up_summed = wait(up_summed)

    def back_one(mixed_grad, entry_role, group_tokens, scale):
        part = plain_product(mixed_grad, entry_role)
        gain_grad = jnp.sum(part * group_tokens.astype(F32) * scale, axis=0)
        return part.astype(BF16), gain_grad

    far, far_gain = step(back_one, state["mixed far"], entry_role, *state["far"][1:])
    near, near_gain = step(back_one, state["mixed near"], entry_role, *state["near"][1:])

    def order_gains(far_gain, near_gain, gain_two_grad):
        gains = jnp.stack([far_gain + near_gain, gain_two_grad])
        gains = gains.reshape(2, dp, fsdp, width // (dp * fsdp)).transpose(2, 1, 0, 3)
        return jnp.take(gains, jnp.arange(fsdp) ^ role, axis=0)

    gains = step(order_gains, far_gain, near_gain, gain_two_grad)
    parts, (entry_grad, *_), gains = plan.settle(
        lambda: near,
        far,
        rows,
        (
            [
                work(
                    product_pairs,
                    state["mixed near"],
                    state["near"][0],
                    state["mixed far"],
                    state["far"][0],
                )
            ],
            [],
            [
                store(
                    "expand",
                    expand_update,
                    gate_summed,
                    up_summed,
                    expand_weight,
                    expand_moment,
                    expand_square,
                )
            ],
        ),
        gains,
    )
    shrink_gradient, *shrink_new = state["shrink"]
    expand_gradient, *expand_new = state["expand"]
    if whole_heads:
        entry_gradient = lax.psum_scatter(
            entry_grad.reshape(3, dp * HEAD, width), "dp", scatter_dimension=1, tiled=True
        )
    else:
        entry_full = lax.dynamic_update_slice_in_dim(
            jnp.zeros((3, width, width), BF16),
            entry_grad.reshape(3, span, width),
            role * span,
            axis=1,
        )
        mixing_full = lax.dynamic_update_slice_in_dim(
            jnp.zeros((width, width), BF16), mixing_grad, role * span, axis=1
        )
        entry_gradient = lax.psum_scatter(entry_full, AXES, scatter_dimension=1, tiled=True)
        mixing_gradient = lax.psum_scatter(mixing_full, AXES, scatter_dimension=0, tiled=True)

    def back_input(inputs, gain, middle_grad, *parts):
        scale = lax.rsqrt(jnp.mean(inputs * inputs, axis=-1, keepdims=True) + EPS)
        grad = sum(value.astype(F32) for value in parts)
        return middle_grad + norm_back(inputs, scale, gain, grad)[0]

    input_gradient = step(back_input, inputs, gain_one, middle_grad, *parts)

    def order_dp(gains):
        return jnp.take(gains[0], jnp.arange(dp) ^ lax.axis_index("dp"), axis=0)

    gains = step(order_dp, gains)
    for bit in reversed([1 << k for k in range((dp - 1).bit_length())]):
        (got,), _ = window([(gains[bit:], -bit)])
        gains = step(lambda a, b: a[:bit] + b, gains, got)
    gain_grads = gains[0]
    attention_gradient, feedforward_gradient = gain_grads[:1], gain_grads[1:]

    if whole_heads:
        mixing_gradient = step(plan.columns_back, mixing_summed)
    mixing_gradient = mixing_gradient[None].astype(F32)
    entry_gradient = entry_gradient.astype(F32)
    entry_new = adamw(entry_weight, entry_gradient, entry_moment, entry_square, RATE, DECAY)
    mixing_new = adamw(
        mixing_weight, mixing_gradient, mixing_moment, mixing_square, MIXING_RATE, DECAY
    )
    attention_new = adamw(
        attention_gain, attention_gradient, attention_moment, attention_square, GAIN_RATE, 0.0
    )
    feedforward_new = adamw(
        feedforward_gain,
        feedforward_gradient,
        feedforward_moment,
        feedforward_square,
        GAIN_RATE,
        0.0,
    )
    return (
        layer_output,
        input_gradient,
        entry_gradient,
        mixing_gradient,
        attention_gradient,
        expand_gradient,
        shrink_gradient,
        feedforward_gradient,
        entry_new[0],
        mixing_new[0],
        attention_new[0],
        expand_new[0],
        shrink_new[0],
        feedforward_new[0],
        entry_new[1],
        entry_new[2],
        mixing_new[1],
        mixing_new[2],
        attention_new[1],
        attention_new[2],
        expand_new[1],
        expand_new[2],
        shrink_new[1],
        shrink_new[2],
        feedforward_new[1],
        feedforward_new[2],
    )


def solution(mesh):
    placed = (
        P(("dp", "fsdp"), None),
        P(("dp", "fsdp")),
        P(("dp", "fsdp"), None),
        P(None, ("dp", "fsdp"), None),
        P(None, ("dp", "fsdp"), None),
        P(None, ("dp", "fsdp")),
        P(None, ("dp", "fsdp"), None),
        P(None, ("dp", "fsdp"), None),
        P(None, ("dp", "fsdp")),
        P(None, ("dp", "fsdp"), None),
        P(None, ("dp", "fsdp"), None),
        P(None, ("dp", "fsdp"), None),
        P(None, ("dp", "fsdp"), None),
        P(None, ("dp", "fsdp")),
        P(None, ("dp", "fsdp")),
        P(None, ("dp", "fsdp"), None),
        P(None, ("dp", "fsdp"), None),
        P(None, ("dp", "fsdp"), None),
        P(None, ("dp", "fsdp"), None),
        P(None, ("dp", "fsdp")),
        P(None, ("dp", "fsdp")),
    )
    return jax.shard_map(
        functools.partial(local, mesh.shape["dp"], mesh.shape["fsdp"]),
        mesh=mesh,
        in_specs=placed,
        out_specs=(
            P(("dp", "fsdp"), None),
            P(("dp", "fsdp"), None),
            P(None, ("dp", "fsdp"), None),
            P(None, ("dp", "fsdp"), None),
            P(None, ("dp", "fsdp")),
            P(None, ("dp", "fsdp"), None),
            P(None, ("dp", "fsdp"), None),
            P(None, ("dp", "fsdp")),
            P(None, ("dp", "fsdp"), None),
            P(None, ("dp", "fsdp"), None),
            P(None, ("dp", "fsdp")),
            P(None, ("dp", "fsdp"), None),
            P(None, ("dp", "fsdp"), None),
            P(None, ("dp", "fsdp")),
            P(None, ("dp", "fsdp"), None),
            P(None, ("dp", "fsdp"), None),
            P(None, ("dp", "fsdp"), None),
            P(None, ("dp", "fsdp"), None),
            P(None, ("dp", "fsdp")),
            P(None, ("dp", "fsdp")),
            P(None, ("dp", "fsdp"), None),
            P(None, ("dp", "fsdp"), None),
            P(None, ("dp", "fsdp"), None),
            P(None, ("dp", "fsdp"), None),
            P(None, ("dp", "fsdp")),
            P(None, ("dp", "fsdp")),
        ),
        check_vma=False,
    )
```

time: 4030 us -> 763 us (0.19)
  waiting for transfers between devices: 3600 us -> 209 us
  local copies, waits for them, and re-layouts: 30.2 us -> 137 us
  matrix products: 270 us -> 197 us
  starting transfers between devices: 0.41 us -> 57 us
  other arithmetic: 52.8 us -> 105 us
    reduce_scatter x4 -> x5, waiting for transfers between devices: 2820 us -> 0.01 us  [the longest x1 0.01 us: local(): lax.psum_scatter(shrink_grad, 'dp', scatter_dimension=0, tiled=True)]
    all_gather x4 -> x5, waiting for transfers between devices: 665 us -> 12.7 us  [the longest x1 12.7 us: local(): lax.all_gather(shrink_blocks, 'dp', axis=0, tiled=True).reshape(width, -1)]
    ppermute x0 -> x56, waiting for transfers between devices: none -> 183 us  [window(): came.append(lax.ppermute(value, axis, pairs))]
    unnamed x12 -> x10, waiting for transfers between devices: 116 us -> 0.17 us
    dot_general x4 -> x10, matrix products: 103 us -> 53 us  [contract_first(): lax.dot_general(left, right, (((0,), (0,)), ((), ())), preferred_element_...]
    ppermute x0 -> x56, starting transfers between devices: none -> 44.2 us  [window(): came.append(lax.ppermute(value, axis, pairs))]
    unnamed x1 -> x0, blocking collectives: 43.2 us -> none
  transfers between devices with their start and end apart: 10 -> 69, of which waited for: 9 -> 33; matrix products, arithmetic and copies ran while one was open for 6% -> 54% of each run, Pallas kernels for 0% -> 0%
where the time goes in v1:
time: 763 us; the launch traced here: 753 us
  waiting for transfers between devices  209 us (27%)
  matrix products  197 us (26%)
  local copies, waits for them, and re-layouts  137 us (18%)
  other arithmetic  105 us (14%)
  starting transfers between devices  57 us (7%)
  blocking collectives  31.6 us (4%)
  between operations  16.9 us (2%)
    ppermute x56, waiting for transfers between devices, window(): came.append(lax.ppermute(value, axis, pairs))  183 us
    dot_general x10, matrix products, plain_product(): return jnp.dot(left, right, preferred_element_type=jnp.float32)  64.4 us
    dot_general x10, matrix products, contract_last(): lax.dot_general(left, right, (((1,), (1,)), ((), ())), preferred_element_...  56.9 us
    dot_general x10, matrix products, contract_first(): lax.dot_general(left, right, (((0,), (0,)), ((), ())), preferred_element_...  53 us
    ppermute x56, starting transfers between devices, window(): came.append(lax.ppermute(value, axis, pairs))  44.2 us
    unnamed x319, local copies, waits for them, and re-layouts  42.5 us
    reshape x16, local copies, waits for them, and re-layouts, heads_of(): return value.reshape(group, rows, heads, HEAD)  26.9 us
    sub x5, other arithmetic, adamw(): weight - rate * (corrected / spread + decay * weight)  24.5 us
  transfers between devices with their start and end apart: 69, of which 33 were waited for; matrix products, arithmetic and copies ran while one was open for 54% of the time, Pallas kernels for 0%

profile of v1, /device:TPU:0, one launch (start us, length us, event | category | flops | bytes accessed | tf_op | source)
XLA Modules:
  0.0 753.2 jit_solution(17407314693950654807)
XLA Ops:
  14.8 21.4 %collective-permute-done.3 = s32[1,256]{1,0:T(1,128)S(1)} collective-permute-done((s32[1,256]{1,0:T(1,128)}, s32[1,256]{1,0:T(1,128)S(1)}, u32[]{:S(2)}, u32[]{:S(2)}) %collective-permute-start.3) | collective-permute-done | bytes 1056 | tf_op jit(solution)/shard_map/ppermute | solution.py:119
  42.3 10.9 %collective-permute-done.7 = s32[2,256]{1,0:T(2,128)S(1)} collective-permute-done((s32[2,256]{1,0:T(2,128)S(1)}, s32[2,256]{1,0:T(2,128)S(1)}, u32[]{:S(2)}, u32[]{:S(2)}) %collective-permute-start.7) | collective-permute-done | bytes 2080 | tf_op jit(solution)/shard_map/ppermute | solution.py:119
  55.9 10.7 %all_to_all.20 = bf16[8,64,256]{2,1,0:T(8,128)(2,1)} all-to-all(bf16[8,64,256]{2,1,0:T(8,128)(2,1)S(1)} %reshape.688), channel_id=1, replica_groups=mesh['dp'=4,'fsdp'=8] {'fsdp'}, dimensions={0} | all-to-all | bytes 524288 | tf_op jit(solution)/shard_map/all_to_all | solution.py:220
  82.6 11.3 %all_gather.21 = bf16[2,4,64]{2,0,1:T(2,128)(2,1)S(1)} all-gather(bf16[2,1,64]{2,0,1:T(2,128)(2,1)S(1)} %copy.191), channel_id=1, replica_groups=mesh['dp'=4,'fsdp'=8] {'dp'}, dimensions={1}, use_global_device_ids=true | all-gather | bytes 1280 | tf_op jit(solution)/shard_map/all_gather | solution.py:299
  94.1 9.6 %all-gather = bf16[2,4,512]{1,0,2:T(2,128)(2,1)S(1)} all-gather(bf16[2,4,64]{1,0,2:T(2,128)(2,1)S(1)} %copy.192), channel_id=2, replica_groups=mesh['dp'=4,'fsdp'=8] {'fsdp'}, dimensions={2}, use_global_device_ids=true | all-gather | bytes 9216 | tf_op jit(solution)/shard_map/all_gather | solution.py:302
  140.3 16.2 %collective-permute-done.10 = bf16[256,2048]{1,0:T(8,128)(2,1)S(1)} collective-permute-done((bf16[256,2048]{1,0:T(8,128)(2,1)}, bf16[256,2048]{1,0:T(8,128)(2,1)S(1)}, u32[]{:S(2)}, u32[]{:S(2)}) %collective-permute-start.10) | collective-permute-done | bytes 1048608 | tf_op jit(solution)/shard_map/ppermute | solution.py:119
  221.9 9.7 %collective-permute-done.17 = bf16[128,2048]{1,0:T(8,128)(2,1)S(1)} collective-permute-done((bf16[128,2048]{1,0:T(8,128)(2,1)S(1)}, bf16[128,2048]{1,0:T(8,128)(2,1)S(1)}, u32[]{:S(2)}, u32[]{:S(2)}) %collective-permute-start.17) | collective-permute-done | bytes 524320 | tf_op jit(solution)/shard_map/ppermute | solution.py:119
  239.0 18.2 %collective-permute-done.19 = bf16[256,2048]{1,0:T(8,128)(2,1)S(1)} collective-permute-done((bf16[256,2048]{1,0:T(8,128)(2,1)S(1)}, bf16[256,2048]{1,0:T(8,128)(2,1)S(1)}, u32[]{:S(2)}, u32[]{:S(2)}) %collective-permute-start.19) | collective-permute-done | bytes 1048608 | tf_op jit(solution)/shard_map/ppermute | solution.py:119
  260.6 20.6 %collective-permute-done.22 = bf16[256,2048]{1,0:T(8,128)(2,1)S(1)} collective-permute-done((bf16[256,2048]{1,0:T(8,128)(2,1)S(1)}, bf16[256,2048]{1,0:T(8,128)(2,1)S(1)}, u32[]{:S(2)}, u32[]{:S(2)}) %collective-permute-start.22) | collective-permute-done | bytes 1048608 | tf_op jit(solution)/shard_map/ppermute | solution.py:119
  287.5 12.5 %collective-permute-done.25 = bf16[128,2048]{1,0:T(8,128)(2,1)} collective-permute-done((bf16[128,2048]{1,0:T(8,128)(2,1)}, bf16[128,2048]{1,0:T(8,128)(2,1)}, u32[]{:S(2)}, u32[]{:S(2)}) %collective-permute-start.25) | collective-permute-done | bytes 524320 | tf_op jit(solution)/shard_map/ppermute | solution.py:119
  307.0 8.2 %fusion.109 = f32[1024,1024]{1,0:T(8,128)S(1)} fusion(bf16[1024,2048]{1,0:T(8,128)(2,1)} %constant_dynamic-update-slice_fusion.22, bf16[1024,2048]{1,0:T(8,128)(2,1)} %bitcast.277), kind=kOutput, calls=%fused_computation.303 | convolution fusion | flops 4294967296 | bytes 12582912 | tf_op jit(solution)/shard_map/dot_general | solution.py:24
  315.2 10.3 %multiply_convert_fusion.7 = (bf16[1024,1024]{1,0:T(8,128)(2,1)S(1)}, f32[1024,1024]{1,0:T(8,128)}) fusion(f32[1024,1024]{1,0:T(8,128)S(1)} %fusion.109, bf16[1024,2048]{1,0:T(8,128)(2,1)} %constant_dynamic-update-slice_fusion.22, bf16[1024,2048]{1,0:T(8,128)(2,1)S(1)} %bitcast.281), kind=kOutput, calls=%fused_computation.41 | convolution fusion | flops 4301258752 | bytes 18874368 | tf_op jit(solution)/shard_map/dot_general | solution.py:24
  353.0 12.7 %all-gather.13.cloned.1.call-done = bf16[32,64,1024]{2,1,0:T(8,128)(2,1)} async-done(((bf16[8,64,1024]{2,1,0:T(8,128)(2,1)}), bf16[32,64,1024]{2,1,0:T(8,128)(2,1)}) %all-gather.13.cloned.1.call-update) | async-done | bytes 4194320 | tf_op jit(solution)/shard_map/all_gather | solution.py:343
  365.6 11.8 %multiply_convert_fusion.4 = (bf16[1024,1024]{1,0:T(8,128)(2,1)S(1)}, bf16[1024,1024]{1,0:T(8,128)(2,1)S(1)}) fusion(f32[1024,1024]{1,0:T(8,128)} %copy-done.132, f32[1024,1024]{1,0:T(8,128)} %get-tuple-element.511, bf16[1024,2048]{1,0:T(8,128)(2,1)} %copy-done.91, bf16[2048,1024]{1,0:T(8,128)(2,1)} %bitcast.285), kind=kOutput, calls=%fused_computation.37 | convolution fusion | flops 4308598784 | bytes 20971520 | tf_op jit(solution)/shard_map/dot_general | solution.py:36
  377.5 6.9 fusion.112
  384.4 7.1 add_convert_fusion.6
  391.6 9.3 %multiply_convert_fusion.2 = (bf16[1024,1024]{1,0:T(8,128)(2,1)}, bf16[1024,1024]{1,0:T(8,128)(2,1)S(1)}) fusion(f32[1024,1024]{1,0:T(8,128)} %copy-done.131, f32[1024,1024]{1,0:T(8,128)} %get-tuple-element.519, bf16[1024,2048]{1,0:T(8,128)(2,1)S(1)} %copy-done.90, bf16[2048,1024]{1,0:T(8,128)(2,1)S(1)} %bitcast.286), kind=kOutput, calls=%fused_computation.34 | convolution fusion | flops 4308598784 | bytes 20971520 | tf_op jit(solution)/shard_map/dot_general | solution.py:36
  409.0 7.0 add_convert_fusion.5
  456.4 10.2 %collective-permute-done.32 = bf16[256,2048]{1,0:T(8,128)(2,1)} collective-permute-done((bf16[256,2048]{1,0:T(8,128)(2,1)}, bf16[256,2048]{1,0:T(8,128)(2,1)}, u32[]{:S(2)}, u32[]{:S(2)}) %collective-permute-start.32) | collective-permute-done | bytes 1048608 | tf_op jit(solution)/shard_map/ppermute | solution.py:119
  488.2 8.7 %collective-permute-done.34 = bf16[256,2048]{1,0:T(8,128)(2,1)S(1)} collective-permute-done((bf16[256,2048]{1,0:T(8,128)(2,1)S(1)}, bf16[256,2048]{1,0:T(8,128)(2,1)S(1)}, u32[]{:S(2)}, u32[]{:S(2)}) %collective-permute-start.34) | collective-permute-done | bytes 1048608 | tf_op jit(solution)/shard_map/ppermute | solution.py:119
  508.9 12.5 %all-to-all-done.2 = bf16[8,64,1024]{2,1,0:T(8,128)(2,1)} async-done(((bf16[8,64,1024]{2,1,0:T(8,128)(2,1)}), bf16[8,64,1024]{2,1,0:T(8,128)(2,1)}, u32[]{:S(2)}, u32[]{:S(2)}) %all-to-all-start.2) | async-done | bytes 1048608 | tf_op jit(solution)/shard_map/all_to_all | solution.py:227
  647.1 13.0 %collective-permute-done.44 = bf16[256,2048]{1,0:T(8,128)(2,1)S(1)} collective-permute-done((bf16[256,2048]{1,0:T(8,128)(2,1)}, bf16[256,2048]{1,0:T(8,128)(2,1)S(1)}, u32[]{:S(2)}, u32[]{:S(2)}) %collective-permute-start.44) | collective-permute-done | bytes 1048608 | tf_op jit(solution)/shard_map/ppermute | solution.py:119
  690.1 9.3 %multiply_subtract_fusion = (f32[2,256,2048]{2,1,0:T(8,128)}, f32[2,256,2048]{2,1,0:T(8,128)}, f32[2,256,2048]{2,1,0:T(8,128)}, f32[2,256,2048]{2,1,0:T(8,128)}) fusion(f32[2,256,2048]{2,1,0:T(8,128)S(1)} %copy-done.21, f32[2,256,2048]{2,1,0:T(8,128)S(1)} %copy-done.39, f32[2,256,2048]{2,1,0:T(8,128)} %param.37, bf16[1,256,2048]{2,1,0:T(8,128)(2,1)S(1)} %bitcast.258, ...), kind=kLoop, calls=%fused_computation.28 | loop fusion | flops 17825792 | bytes 31457280 | tf_op jit(solution)/shard_map/sub | solution.py:84
  699.4 11.8 %collective-permute-done.51 = bf16[256,2048]{1,0:T(8,128)(2,1)S(1)} collective-permute-done((bf16[256,2048]{1,0:T(8,128)(2,1)S(1)}, bf16[256,2048]{1,0:T(8,128)(2,1)S(1)}, u32[]{:S(2)}, u32[]{:S(2)}) %collective-permute-start.51) | collective-permute-done | bytes 1048608 | tf_op jit(solution)/shard_map/ppermute | solution.py:119
  (681 shorter events, 456.5 us)
Async XLA Ops:
  7.2 115.6 %all-gather.9.cloned.1.call-start = ((), (), s32[]{:S(2)}) async-start(), calls=%async_computation.9 | async-start | bytes 3932160 | tf_op jit(solution)/shard_map/all_gather | solution.py:292
  9.7 130.6 %all-gather.11.cloned.1.call-start = ((), (), s32[]{:S(2)}) async-start(), calls=%async_computation.10 | async-start | bytes 1310720 | tf_op jit(solution)/shard_map/all_gather | solution.py:338
  9.7 26.4 %collective-permute-start = (bf16[256,2048]{1,0:T(8,128)(2,1)}, bf16[256,2048]{1,0:T(8,128)(2,1)S(1)}, u32[]{:S(2)}, u32[]{:S(2)}) collective-permute-start(bf16[256,2048]{1,0:T(8,128)(2,1)} %param.21), channel_id=1, source_target_pairs={{0,2},{1,3},{2,0},{3,1},{4,6},{5,7},{6,4},{7,5},{8,10},{9,11},{10,... | collective-permute-start | bytes 3145736 | tf_op jit(solution)/shard_map/ppermute | solution.py:119
  12.7 24.8 %collective-permute-start.1 = (bf16[256,2048]{1,0:T(8,128)(2,1)}, bf16[256,2048]{1,0:T(8,128)(2,1)S(1)}, u32[]{:S(2)}, u32[]{:S(2)}) collective-permute-start(bf16[256,2048]{1,0:T(8,128)(2,1)} %param.21), channel_id=1, source_target_pairs={{0,4},{1,5},{2,6},{3,7},{4,0},{5,1},{6,2},{7,3},{8,12},{9,13},{10,... | collective-permute-start | bytes 3145736 | tf_op jit(solution)/shard_map/ppermute | solution.py:119
  66.6 220.9 %all-gather.15.cloned.1.call-start = ((), (), s32[]{:S(2)}) async-start(), calls=%async_computation.17 | async-start | bytes 5242880 | tf_op jit(solution)/shard_map/all_gather | solution.py:336
  77.2 31.4 %all-to-all-start = ((bf16[8,64,1024]{2,1,0:T(8,128)(2,1)}), bf16[8,64,1024]{2,1,0:T(8,128)(2,1)}, u32[]{:S(2)}, u32[]{:S(2)}) async-start(bf16[8,64,1024]{2,1,0:T(8,128)(2,1)} %reshape.675), calls=%async_computation | async-start | bytes 2097152 | tf_op jit(solution)/shard_map/all_to_all | solution.py:220
  81.4 225.5 %all-gather.17.cloned.1.call-start = ((), (), s32[]{:S(2)}) async-start(), calls=%async_computation.18 | async-start | bytes 5242880 | tf_op jit(solution)/shard_map/all_gather | solution.py:342
  130.8 25.7 %collective-permute-start.10 = (bf16[256,2048]{1,0:T(8,128)(2,1)}, bf16[256,2048]{1,0:T(8,128)(2,1)S(1)}, u32[]{:S(2)}, u32[]{:S(2)}) collective-permute-start(bf16[256,2048]{1,0:T(8,128)(2,1)} %convert_element_type.423), channel_id=1, source_target_pairs={{0,2},{1,3},{2,0},{3,1},{4,6},{5,7},{6,4},{7,5},{8,10},{9,11},{10,... | collective-permute-start | bytes 3145736 | tf_op jit(solution)/shard_map/ppermute | solution.py:119
  132.4 25.3 %collective-permute-start.11 = (bf16[256,2048]{1,0:T(8,128)(2,1)}, bf16[256,2048]{1,0:T(8,128)(2,1)S(1)}, u32[]{:S(2)}, u32[]{:S(2)}) collective-permute-start(bf16[256,2048]{1,0:T(8,128)(2,1)} %convert_element_type.423), channel_id=1, source_target_pairs={{0,4},{1,5},{2,6},{3,7},{4,0},{5,1},{6,2},{7,3},{8,12},{9,13},{10,... | collective-permute-start | bytes 3145736 | tf_op jit(solution)/shard_map/ppermute | solution.py:119
  164.4 27.9 %collective-permute-start.15 = (bf16[512,2048]{1,0:T(8,128)(2,1)}, bf16[512,2048]{1,0:T(8,128)(2,1)}, u32[]{:S(2)}, u32[]{:S(2)}) collective-permute-start(bf16[512,2048]{1,0:T(8,128)(2,1)} %pad_maximum_fusion.1), channel_id=1, source_target_pairs={{0,1},{1,0},{2,3},{3,2},{4,5},{5,4},{6,7},{7,6},{8,9},{9,8},{10,11... | collective-permute-start | bytes 6291464 | tf_op jit(solution)/shard_map/ppermute | solution.py:119
  177.5 33.7 %collective-permute-start.16 = (bf16[1024,2048]{1,0:T(8,128)(2,1)}, bf16[1024,2048]{1,0:T(8,128)(2,1)}, u32[]{:S(2)}, u32[]{:S(2)}) collective-permute-start(bf16[1024,2048]{1,0:T(8,128)(2,1)} %convolution_convert_fusion.1), channel_id=1, source_target_pairs={{0,1},{1,0},{2,3},{3,2},{4,5},{5,4},{6,7},{7,6},{8,9},{9,8},{10,11... | collective-permute-start | bytes 12582920 | tf_op jit(solution)/shard_map/ppermute | solution.py:119
  182.7 182.9 %all-gather.13.cloned.1.call-start = ((), (), s32[]{:S(2)}) async-start(), calls=%async_computation.11 | async-start | bytes 5242880 | tf_op jit(solution)/shard_map/all_gather | solution.py:343
  208.9 28.5 %collective-permute-start.21 = (bf16[256,2048]{1,0:T(8,128)(2,1)}, bf16[256,2048]{1,0:T(8,128)(2,1)S(1)}, u32[]{:S(2)}, u32[]{:S(2)}) collective-permute-start(bf16[256,2048]{1,0:T(8,128)(2,1)} %constant_dynamic-update-slice_fusion.10), channel_id=1, source_target_pairs={{0,1},{1,0},{2,3},{3,2},{4,5},{5,4},{6,7},{7,6},{8,9},{9,8},{10,11... | collective-permute-start | bytes 3145736 | tf_op jit(solution)/shard_map/ppermute | solution.py:119
  287.5 213.7 %reduce-scatter.8.cloned.1.call-start = ((), (), s32[]{:S(2)}) async-start(), calls=%async_computation.13 | async-start | bytes 5242880 | tf_op jit(solution)/shard_map/reduce_scatter | solution.py:440
  352.9 190.7 %reduce-scatter.6.cloned.1.call-start = ((), (), s32[]{:S(2)}) async-start(), calls=%async_computation.12 | async-start | bytes 5242880 | tf_op jit(solution)/shard_map/reduce_scatter | solution.py:469
  441.5 25.1 %collective-permute-start.32 = (bf16[256,2048]{1,0:T(8,128)(2,1)}, bf16[256,2048]{1,0:T(8,128)(2,1)}, u32[]{:S(2)}, u32[]{:S(2)}) collective-permute-start(bf16[256,2048]{1,0:T(8,128)(2,1)} %pad_maximum_fusion.8), channel_id=1, source_target_pairs={{0,2},{1,3},{2,0},{3,1},{4,6},{5,7},{6,4},{7,5},{8,10},{9,11},{10,... | collective-permute-start | bytes 3145736 | tf_op jit(solution)/shard_map/ppermute | solution.py:119
  501.2 30.0 %collective-permute-start.39 = (bf16[512,2048]{1,0:T(8,128)(2,1)}, bf16[512,2048]{1,0:T(8,128)(2,1)}, u32[]{:S(2)}, u32[]{:S(2)}) collective-permute-start(bf16[512,2048]{1,0:T(8,128)(2,1)} %pad_maximum_fusion.3), channel_id=1, source_target_pairs={{0,1},{1,0},{2,3},{3,2},{4,5},{5,4},{6,7},{7,6},{8,9},{9,8},{10,11... | collective-permute-start | bytes 6291464 | tf_op jit(solution)/shard_map/ppermute | solution.py:119
  505.5 170.3 %reduce-scatter.10.cloned.1.call-start = ((), (), s32[]{:S(2)}) async-start(), calls=%async_computation.14 | async-start | bytes 5242880 | tf_op jit(solution)/shard_map/reduce_scatter | solution.py:470
  505.5 25.7 %collective-permute-start.37 = (bf16[128,2048]{1,0:T(8,128)(2,1)}, bf16[128,2048]{1,0:T(8,128)(2,1)}, u32[]{:S(2)}, u32[]{:S(2)}) collective-permute-start(bf16[128,2048]{1,0:T(8,128)(2,1)} %slice.339), channel_id=1, source_target_pairs={{0,2},{1,3},{2,0},{3,1},{4,6},{5,7},{6,4},{7,5},{8,10},{9,11},{10,... | collective-permute-start | bytes 1572872 | tf_op jit(solution)/shard_map/ppermute | solution.py:119
  544.1 179.4 %reduce-scatter.14.cloned.1.call-start = ((), (), s32[]{:S(2)}) async-start(), calls=%async_computation.16 | async-start | bytes 1310720 | tf_op jit(solution)/shard_map/reduce_scatter | solution.py:569
  633.1 27.9 %collective-permute-start.46 = (bf16[1024,2048]{1,0:T(8,128)(2,1)}, bf16[1024,2048]{1,0:T(8,128)(2,1)}, u32[]{:S(2)}, u32[]{:S(2)}) collective-permute-start(bf16[1024,2048]{1,0:T(8,128)(2,1)} %get-tuple-element.639), channel_id=1, source_target_pairs={{0,1},{1,0},{2,3},{3,2},{4,5},{5,4},{6,7},{7,6},{8,9},{9,8},{10,11... | collective-permute-start | bytes 12582920 | tf_op jit(solution)/shard_map/ppermute | solution.py:119
  633.2 107.7 %reduce-scatter.12.cloned.1.call-start = ((), (), s32[]{:S(2)}) async-start(), calls=%async_computation.15 | async-start | bytes 3932160 | tf_op jit(solution)/shard_map/reduce_scatter | solution.py:621
  634.3 25.8 %collective-permute-start.44 = (bf16[256,2048]{1,0:T(8,128)(2,1)}, bf16[256,2048]{1,0:T(8,128)(2,1)S(1)}, u32[]{:S(2)}, u32[]{:S(2)}) collective-permute-start(bf16[256,2048]{1,0:T(8,128)(2,1)} %pad_maximum_fusion.10), channel_id=1, source_target_pairs={{0,2},{1,3},{2,0},{3,1},{4,6},{5,7},{6,4},{7,5},{8,10},{9,11},{10,... | collective-permute-start | bytes 3145736 | tf_op jit(solution)/shard_map/ppermute | solution.py:119
  635.1 25.8 %collective-permute-start.45 = (bf16[256,2048]{1,0:T(8,128)(2,1)}, bf16[256,2048]{1,0:T(8,128)(2,1)}, u32[]{:S(2)}, u32[]{:S(2)}) collective-permute-start(bf16[256,2048]{1,0:T(8,128)(2,1)} %pad_maximum_fusion.11), channel_id=1, source_target_pairs={{0,4},{1,5},{2,6},{3,7},{4,0},{5,1},{6,2},{7,3},{8,12},{9,13},{10,... | collective-permute-start | bytes 3145736 | tf_op jit(solution)/shard_map/ppermute | solution.py:119
  (188 other events, 1998.6 us)
Sparse Core Ops, SparseCore 0:
  10.2 66.1 all-gather.8
  77.9 26.6 all-gather.10
  106.8 80.2 all-gather.14
  189.1 79.2 all-gather.16
  287.6 77.9 all-gather.12
  367.8 75.2 reduce-scatter.7
  445.5 77.2 reduce-scatter.5
  544.2 74.2 reduce-scatter.9
  633.3 25.0 reduce-scatter.13
  660.5 58.9 reduce-scatter.11

commit v2 on v1

v2 whole, which is shorter than its diff:
```python
import functools

import jax
import jax.numpy as jnp
from jax import lax
from jax.experimental import pallas as pl
from jax.experimental.pallas import tpu as pltpu
from jax.sharding import PartitionSpec as P

HEADS = 32
HEAD = 64
STEP = 3


EPS = 1e-05
THETA = 130000.0
RATE = 0.01
MIXING_RATE = 0.04
GAIN_RATE = 0.3
BETA_ONE = 0.9
BETA_TWO = 0.95
ADAM_EPS = 1e-08
DECAY = 0.1


def contract_last(left, right):
    return lax.dot_general(
        left, right, (((1,), (1,)), ((), ())), preferred_element_type=jnp.float32
    )


def contract_first(left, right):
    return lax.dot_general(
        left, right, (((0,), (0,)), ((), ())), preferred_element_type=jnp.float32
    )


def plain_product(left, right):
    return jnp.dot(left, right, preferred_element_type=jnp.float32)


def rope_tables(positions):
    half = HEAD // 2
    freq = THETA ** (-2.0 * jnp.arange(half, dtype=jnp.float32) / HEAD)
    angle = positions.astype(jnp.float32)[:, None] * freq[None, :]
    return (jnp.cos(angle), jnp.sin(angle))


def norm_back(value, scale, gain, grad):
    weighted = grad * gain
    inner = jnp.mean(weighted * value, axis=-1, keepdims=True)
    back = scale * weighted - value * (scale * scale * scale) * inner
    return (back, jnp.sum(grad * value * scale, axis=0))


def adamw(weight, gradient, moment, square, rate, decay):
    moment_new = BETA_ONE * moment + (1.0 - BETA_ONE) * gradient
    square_new = BETA_TWO * square + (1.0 - BETA_TWO) * gradient * gradient
    corrected = moment_new / (1.0 - BETA_ONE**STEP)
    spread = jnp.sqrt(square_new / (1.0 - BETA_TWO**STEP)) + ADAM_EPS
    return (weight - rate * (corrected / spread + decay * weight), moment_new, square_new)


AXES = ("dp", "fsdp")
VMEM_BYTES = 56 * 2**20
BF16 = jnp.bfloat16
F32 = jnp.float32


def add_low(*values):
    return sum(value.astype(F32) for value in values).astype(BF16)


def probs_of(left, right, places_down, places_across, turned):
    rows = right.shape[0]
    down = lax.broadcasted_iota(jnp.int32, (rows, rows), 0)
    across = lax.broadcasted_iota(jnp.int32, (rows, rows), 1)
    earlier = down <= across if turned else across <= down
    visible = (places_down - places_across == down - across) & earlier
    raw = contract_last(left, right).reshape(-1, rows, rows)
    scores = jnp.where(visible[None], raw * (HEAD ** (-0.5)), -1e30)
    axis = 1 if turned else 2
    weights = jnp.exp(scores - jnp.max(scores, axis=axis, keepdims=True))
    return weights * (1.0 / jnp.sum(weights, axis=axis, keepdims=True))


def by_head(value):
    head = lax.broadcasted_iota(jnp.int32, value.shape, 1) // HEAD
    none = jnp.zeros_like(value)
    return jnp.concatenate(
        [jnp.where(head == h, value, none) for h in range(value.shape[1] // HEAD)]
    )


def own_columns(value, rows):
    head = lax.broadcasted_iota(jnp.int32, (rows, value.shape[1]), 1) // HEAD
    total = value[:rows]
    for h in range(1, value.shape[1] // HEAD):
        total = jnp.where(head == h, value[h * rows : (h + 1) * rows], total)
    return total


def swap_halves(value):
    columns = value.shape[1]
    half = HEAD // 2
    lane = lax.broadcasted_iota(jnp.int32, value.shape, 1) % HEAD
    return jnp.where(
        lane < half, pltpu.roll(value, columns - half, 1), pltpu.roll(value, half, 1)
    )


def attend_kernel(group, *refs):
    blocks, refs = refs[:group], refs[group:]
    gain, weight, cosine, sine, down, across, normed, joint, attended, held = refs
    for k in range(group):

        @pl.when(pl.program_id(0) == k)
        def _():
            held[...] = blocks[k][...]

    value = held[...].astype(F32)
    scale = lax.rsqrt(jnp.mean(value * value, axis=-1, keepdims=True) + EPS)
    normed[...] = (value * scale * gain[...]).astype(BF16)
    mixed = contract_last(normed[...], weight[...])
    span = mixed.shape[1] // 3
    for part in range(2):
        piece = mixed[:, part * span : (part + 1) * span]
        joint[:, part * span : (part + 1) * span] = (
            piece * cosine[...] + swap_halves(piece) * sine[...]
        ).astype(BF16)
    joint[:, 2 * span :] = mixed[:, 2 * span :].astype(BF16)
    query, keys, values = (joint[:, part * span : (part + 1) * span] for part in range(3))
    rows = query.shape[0]
    probs = probs_of(by_head(query), keys, down[0], across[0], False).astype(BF16)
    found = plain_product(probs.reshape(-1, rows), values)
    attended[...] = own_columns(found, rows).astype(BF16)


def attend_blocks(blocks, gain, weight, cosine, sine, places):
    group = len(blocks)
    rows, width = blocks[0].shape
    span = weight.shape[0] // 3
    whole = lambda *shape: pl.BlockSpec(shape, lambda i: (0,) * len(shape))
    by_row = lambda columns: pl.BlockSpec((rows, columns), lambda i: (i, 0))
    return pl.pallas_call(
        functools.partial(attend_kernel, group),
        grid=(group,),
        in_specs=[whole(rows, width)] * group
        + [whole(1, width), whole(3 * span, width), by_row(span), by_row(span)]
        + [
            pl.BlockSpec((1, rows, 1), lambda i: (i, 0, 0)),
            pl.BlockSpec((1, 1, rows), lambda i: (i, 0, 0)),
        ],
        out_specs=[by_row(width), by_row(3 * span), by_row(span)],
        out_shape=[
            jax.ShapeDtypeStruct((group * rows, columns), BF16)
            for columns in (width, 3 * span, span)
        ],
        scratch_shapes=[pltpu.VMEM((rows, width), BF16)],
        compiler_params=pltpu.CompilerParams(vmem_limit_bytes=VMEM_BYTES),
    )(*blocks, gain[None], weight, cosine, sine, places[:, :, None], places[:, None, :])


def attend_back_kernel(group, first, *refs):
    grads, blocks, refs = refs[:group], refs[group : 2 * group], refs[2 * group :]
    mixing, weight, joint, attended, normed, cosine, sine, down, across = refs[:9]
    earlier, refs = (None, refs[9:]) if first else (refs[9:12], refs[12:])
    terms, entry_sum, mixing_sum, gain_sum, held, tokens, back = refs
    step = pl.program_id(0)
    for k in range(group):

        @pl.when(step == k)
        def _():
            held[...] = grads[k][...]
            tokens[...] = blocks[k][...]

    @pl.when(step == 0)
    def _():
        for k, sums in ((1, mixing_sum), (2, gain_sum)):
            sums[...] = jnp.zeros_like(sums) if first else earlier[k][...]

    rows = held.shape[0]
    here = pl.ds(pl.multiple_of(step * rows, rows), rows)
    span = joint.shape[1] // 3
    query, keys, values = (joint[:, part * span : (part + 1) * span] for part in range(3))
    grad = plain_product(held[...], mixing[...]).astype(BF16)
    key_heads = by_head(keys)
    probs = probs_of(key_heads, query, down[0], across[0], True)
    prob_grad = contract_last(by_head(values), grad).reshape(probs.shape)
    delta = jnp.sum(probs * prob_grad, axis=1, keepdims=True)
    score_grad = (probs * (prob_grad - delta)).astype(BF16).reshape(-1, rows)
    query_grad = contract_first(score_grad, key_heads)
    key_grad = own_columns(plain_product(score_grad, query), rows)
    value_grad = own_columns(plain_product(probs.astype(BF16).reshape(-1, rows), grad), rows)
    for part, value in enumerate((query_grad, key_grad)):
        value = value * (HEAD ** (-0.5))
        back[here, part * span : (part + 1) * span] = (
            value * cosine[...] - swap_halves(value) * sine[...]
        ).astype(BF16)
    back[here, 2 * span :] = value_grad.astype(BF16)
    term = plain_product(back[here, :], weight[...])
    terms[...] = term.astype(BF16)
    value = tokens[...].astype(F32)
    scale = lax.rsqrt(jnp.mean(value * value, axis=-1, keepdims=True) + EPS)
    gain_sum[...] += jnp.sum(term * (value * scale), axis=0, keepdims=True)
    mixing_sum[...] += contract_first(attended[...], held[...])

    @pl.when(step == group - 1)
    def _():
        for part in range(3):
            part = slice(part * span, (part + 1) * span)
            found = contract_first(back[:, part], normed[...])
            entry_sum[part, :] = found if first else earlier[0][part, :] + found


def attend_back_blocks(grads, blocks, mixing, weight, joint, attended, normed, turn, places, earlier):
    group = len(blocks)
    rows, width = blocks[0].shape
    span = weight.shape[0] // 3
    whole = lambda *shape: pl.BlockSpec(shape, lambda i: (0,) * len(shape))
    by_row = lambda columns: pl.BlockSpec((rows, columns), lambda i: (i, 0))
    sums = [(3 * span, width), (span, width), (1, width)]
    return pl.pallas_call(
        functools.partial(attend_back_kernel, group, not earlier),
        grid=(group,),
        in_specs=[whole(rows, width)] * (2 * group)
        + [whole(width, span), whole(3 * span, width)]
        + [by_row(3 * span), by_row(span), whole(group * rows, width), by_row(span), by_row(span)]
        + [
            pl.BlockSpec((1, rows, 1), lambda i: (i, 0, 0)),
            pl.BlockSpec((1, 1, rows), lambda i: (i, 0, 0)),
        ]
        + [whole(*shape) for shape in sums if earlier],
        out_specs=[by_row(width)] + [whole(*shape) for shape in sums],
        out_shape=[jax.ShapeDtypeStruct((group * rows, width), BF16)]
        + [jax.ShapeDtypeStruct(shape, F32) for shape in sums],
        scratch_shapes=[
            pltpu.VMEM((rows, width), BF16),
            pltpu.VMEM((rows, width), BF16),
            pltpu.VMEM((group * rows, 3 * span), BF16),
        ],
        compiler_params=pltpu.CompilerParams(vmem_limit_bytes=VMEM_BYTES),
    )(
        *grads,
        *blocks,
        mixing,
        weight,
        joint,
        attended,
        normed,
        *turn,
        places[:, :, None],
        places[:, None, :],
        *earlier,
    )


def turn_tables(places, heads):
    cosine, sine = rope_tables(places.reshape(-1))
    return (
        jnp.tile(jnp.concatenate([cosine, cosine], axis=1), (1, heads)),
        jnp.tile(jnp.concatenate([-sine, sine], axis=1), (1, heads)),
    )


class Plan:
    def __init__(self, dp, fsdp):
        self.dp, self.fsdp = dp, fsdp
        self.clock = None
        self.bits = [1 << k for k in range(1, (fsdp - 1).bit_length())] + [1]
        self.short = fsdp == 8

    def tie(self, values):
        if self.clock is None:
            return tuple(values)
        return lax.optimization_barrier((tuple(values), self.clock))[0]

    def step(self, work, *values):
        found = work(*self.tie(values))
        self.clock = jax.tree.leaves(found)
        return found

    def window(self, sends, *works):
        values = self.tie([value for value, _ in sends])
        came = []
        for value, (_, mask) in zip(values, sends):
            axis, count = ("fsdp", self.fsdp) if mask > 0 else ("dp", self.dp)
            pairs = [(i, i ^ abs(mask)) for i in range(count)]
            came.append(lax.ppermute(value, axis, pairs))
        gave, done = [], []
        for work in works:
            gave.append(work())
            done += self.clock
        came, self.clock = lax.optimization_barrier((came, done or came))
        return came, gave

    def wait(self, value):
        self.clock = [*self.clock, value]
        return value

    def merge(self, rows, sums, first, second):
        half = rows // 2
        beside, above = sums[rows : 2 * rows], sums[2 * rows : 3 * rows]
        return (
            jnp.concatenate([beside[:half], add_low(beside[half:], second)]),
            jnp.concatenate([add_low(above[:half], first), above[half:]]),
        )

    def spread(self, block, marks=None, works=((), (), ()), extra=None):
        small = marks is not None
        gave, more = [], []

        def added(k):
            return [] if extra is None else extra(k, more)

        if self.short:
            half = block.shape[0] // 2
            (beside, above, other, *got), found = self.window(
                [(block, 2), (block, 4), (block, 1)] + [(marks, 2)] * small + added(0), *works[0]
            )
            gave += found
            more.append(got)
            if small:
                marks = self.step(lambda a, b: jnp.concatenate([a, b]), marks, *got)
            upper, lower, pair = self.step(
                lambda a, b: (a[:half], b[half:], jnp.concatenate([b, a])), above, beside
            )
            (first, second, pair, *got), found = self.window(
                [(upper, 2), (lower, 4), (pair, 1)] + [(marks, 4)] * small, *works[1]
            )
            gave += found
            across = self.step(lambda a, b: jnp.concatenate([a, b]), first, second)
            if small:
                marks = self.step(lambda a, b: jnp.concatenate([a, b]), marks, *got)
            near = [block, beside, above, across]
            (far, *got), found = self.window(
                [(across, 1)] + [(marks, 1)] * small + added(2),
                *[functools.partial(w, near) for w in works[2]],
            )
            more.append(got)
            size = block.shape[0]
            got = got if extra is None else more
            return near, [other, pair[:size], pair[size:], far], (marks, *got), gave + found
        near = [block]
        for bit in self.bits[:-1]:
            got, _ = self.window([(piece, bit) for piece in near] + [(marks, bit)] * small)
            if small:
                marks = jnp.concatenate([marks, got[-1]])
            near = near + got[: len(near)]
        for work in [*works[0], *works[1]]:
            gave.append(work())
        got, found = self.window(
            [(piece, 1) for piece in near] + [(marks, 1)] * small,
            *[functools.partial(w, near) for w in works[2]],
        )
        return near, got[: len(near)], (marks, *got[len(near) :]), gave + found

    def settle(self, near, far, rows, works=((), (), ()), small=None, got=None):
        gave = []

        def sends(bit):
            return [] if small is None else [(small[bit:], bit)]

        def sum_small(got, bit):
            if got:
                return self.step(lambda a, b: a[:bit] + b, small, *got)
            return None

        if not self.short:
            terms = jnp.concatenate([near(), far])
            for work in [*works[0], *works[1], *works[2]]:
                gave.append(work())
            for bit in reversed(self.bits):
                size = terms.shape[0] // 2
                if got is None:
                    (got,), _ = self.window([(terms[size:], bit)])
                terms = self.step(add_low, terms[:size], got)
                got = None
            if small is not None:
                for bit in sorted(self.bits, reverse=True):
                    small = sum_small(self.window(sends(bit))[0], bit)
            return (terms, jnp.zeros_like(terms), jnp.zeros_like(terms)), gave, small
        half = rows // 2
        if got is None:
            (got,), (near, *found) = self.window([(far, 1)], near, *works[0])
            gave += found
        else:
            near = near()
        sums = self.step(add_low, near, got)
        across = sums[3 * rows :]
        (first, second, *more), found = self.window(
            [(across[:half], 2), (across[half:], 4)] + sends(4), *works[1]
        )
        gave += found
        small = sum_small(more, 4)

        beside, above = self.step(functools.partial(self.merge, rows), sums, first, second)
        (beside, above, *more), found = self.window([(beside, 2), (above, 4)] + sends(2), *works[2])
        small = sum_small(more, 2)
        if small is not None:
            (more,), _ = self.window(sends(1))
            small = sum_small([more], 1)
        return (sums[:rows], beside, above), gave + found, small

    def columns_split(self, shard):
        rows, columns = shard.shape
        width = columns // (self.dp * self.fsdp)
        blocks = shard.reshape(rows, self.dp, self.fsdp, width).transpose(2, 0, 1, 3)
        return blocks.reshape(self.fsdp, rows, self.dp * width)

    def exchange(self, blocks):
        return lax.all_to_all(blocks, "fsdp", 0, 0, tiled=True)

    def columns_back(self, blocks):
        rows = blocks.shape[0] // self.fsdp
        width = blocks.shape[1] // self.dp
        blocks = lax.all_to_all(
            blocks.reshape(self.fsdp, rows, self.dp * width), "fsdp", 0, 0, tiled=True
        )
        blocks = blocks.reshape(self.fsdp, rows, self.dp, width).transpose(1, 2, 0, 3)
        return blocks.reshape(rows, self.dp * self.fsdp * width)


def local(
    dp,
    fsdp,
    tokens,
    positions,
    cotangent,
    entry_weight,
    mixing_weight,
    attention_gain,
    expand_weight,
    shrink_weight,
    feedforward_gain,
    entry_moment,
    entry_square,
    mixing_moment,
    mixing_square,
    attention_moment,
    attention_square,
    expand_moment,
    expand_square,
    shrink_moment,
    shrink_square,
    feedforward_moment,
    feedforward_square,
):
    plan = Plan(dp, fsdp)
    step, window, wait = plan.step, plan.window, plan.wait
    rows = tokens.shape[0]
    width = tokens.shape[1]
    group = fsdp // 2
    whole_heads = entry_weight.shape[1] == HEAD
    heads = HEADS // fsdp
    span = heads * HEAD
    factor = HEAD ** (-0.5)
    state = {}

    def work(call, *values):
        return lambda *_: step(call, *values)

    def store(name, call, *values):
        def run(*_):
            state[name] = step(call, *values)

        return run

    def low_of(value):
        return value.astype(BF16)

    join = lambda *a: jnp.concatenate(a)
    product_last = lambda a, b: contract_last(a, b).astype(BF16)
    product_plain = lambda a, b: plain_product(a, b).astype(BF16)

    def product_pairs(a, b, c, d):
        return (contract_first(a, b) + contract_first(c, d)).astype(BF16)

    entry_low = step(low_of, entry_weight)
    role = lax.axis_index("fsdp")
    if whole_heads:
        entry_role = lax.all_gather(entry_low, "dp", axis=1, tiled=True)
    else:
        entry_all = lax.all_gather(entry_low, AXES, axis=1, tiled=True)
        entry_role = lax.dynamic_slice_in_dim(entry_all, role * span, span, axis=1)

    def gains_dp(*gains):
        gains = jnp.concatenate(gains).astype(BF16)[:, None]
        return lax.all_gather(gains, "dp", axis=1, tiled=True)

    def gains_fsdp(gains):
        gains = lax.all_gather(gains[:, :, None], "fsdp", axis=2, tiled=True)
        return gains.reshape(2, width).astype(F32)

    def columns_work(shrink_low, mixing_low):
        blocks = plan.exchange(
            jnp.concatenate([plan.columns_split(shrink_low), plan.columns_split(mixing_low)], -1)
        )
        size = shrink_low.shape[1] // fsdp
        return blocks[..., :size], blocks[..., size:]

    spread_tokens, far_tokens, (near_places, far_places), _ = plan.spread(
        tokens,
        positions[None],
        (
            [
                store("mixing_low", low_of, mixing_weight[0]),
                store("shrink_low", low_of, shrink_weight[0]),
                store("gains_dp", gains_dp, attention_gain, feedforward_gain),
                lambda: state.update(
                    columns=step(columns_work, state["shrink_low"], state["mixing_low"])
                ),
            ],
            [
                store("gate_low", lambda a: a[0].astype(BF16), expand_weight),
                store("up_low", lambda a: a[1].astype(BF16), expand_weight),
                lambda: state.update(gains=step(gains_fsdp, state["gains_dp"])),
            ],
            [],
        ),
    )
    gain_one, gain_two = state["gains"][0], state["gains"][1]
    shrink_blocks, mixing_blocks = state["columns"]
    gate_role = lax.all_gather(state["gate_low"], "dp", axis=0, tiled=True)
    if whole_heads:
        mixing_role = lax.all_gather(mixing_blocks, "dp", axis=0, tiled=True).reshape(width, span)
    else:
        mixing_all = lax.all_gather(state["mixing_low"], AXES, axis=0, tiled=True)
        mixing_role = lax.dynamic_slice_in_dim(mixing_all, role * span, span, axis=1)
    up_role = lax.all_gather(state["up_low"], "dp", axis=0, tiled=True)
    shrink_role = lax.all_gather(shrink_blocks, "dp", axis=0, tiled=True).reshape(width, -1)

    inputs = tokens.astype(F32)
    live = (positions >= 0).astype(F32)[:, None]
    grad_out = cotangent.astype(F32) * live
    grad_low = step(low_of, grad_out)
    entry_role = wait(entry_role).reshape(3 * span, width)
    state["turn near"] = step(lambda a: turn_tables(a, heads), near_places)
    state["turn far"] = step(lambda a: turn_tables(a, heads), far_places)

    def attend_work(name, blocks, places):
        def run(*_):
            state["attend " + name] = step(
                attend_blocks, blocks, gain_one, entry_role, *state["turn " + name], places
            )

        return run

    near_grad, far_grad, _, _ = plan.spread(
        grad_low,
        None,
        (
            [attend_work("far", far_tokens, far_places)],
            [
                attend_work("near", spread_tokens, near_places),
                lambda: state.update(gate=wait(gate_role)),
            ],
            [],
        ),
    )
    mixing_role = wait(mixing_role)
    far = step(product_last, state["attend far"][2], mixing_role)
    near = work(product_last, state["attend near"][2], mixing_role)
    parts, _, _ = plan.settle(
        near, far, rows, ([], [store("grad near", join, *near_grad)], [store("grad far", join, *far_grad)])
    )

    def norm_middle(inputs, gain, own, beside, above):
        middle = inputs + own.astype(F32) + beside.astype(F32) + above.astype(F32)
        scale = lax.rsqrt(jnp.mean(middle * middle, axis=-1, keepdims=True) + EPS)
        return (middle * scale * gain).astype(BF16), middle, scale

    low_two, middle, scale_two = step(norm_middle, inputs, gain_two, *parts)

    def expand(normed, gate_role, up_role):
        gate = contract_last(normed, gate_role)
        upward = contract_last(normed, up_role)
        return gate, upward, (gate * jax.nn.sigmoid(gate) * upward).astype(BF16)

    def expand_near(near):
        state["two near"] = step(join, *near)
        state["up near"] = step(expand, state["two near"], gate_role, up_role)

    _, far_two, _, _ = plan.spread(low_two, None, ([], [lambda: wait(up_role)], [expand_near]))
    state["two far"] = step(join, *far_two)
    state["up far"] = step(expand, state["two far"], gate_role, up_role)
    shrink_grad = step(
        product_pairs, state["grad near"], state["up near"][2], state["grad far"], state["up far"][2]
    )
    shrink_summed = lax.psum_scatter(shrink_grad, "dp", scatter_dimension=0, tiled=True)
    shrink_role = wait(shrink_role)

    def back(gate, upward, grad_group, shrink_role):
        sigma = jax.nn.sigmoid(gate)
        swish = gate * sigma
        hidden_grad = plain_product(grad_group, shrink_role)
        gate_grad = hidden_grad * upward * (sigma * (1.0 + gate * (1.0 - sigma)))
        upward_grad = hidden_grad * swish
        return gate_grad.astype(BF16), upward_grad.astype(BF16)

    def back_terms(gate_grad, up_grad, gate_role, up_role):
        return (plain_product(gate_grad, gate_role) + plain_product(up_grad, up_role)).astype(BF16)

    far_back = step(back, *state["up far"][:2], state["grad far"], shrink_role)
    far = step(back_terms, *far_back, gate_role, up_role)

    def near_terms():
        state["back"] = step(back, *state["up near"][:2], state["grad near"], shrink_role)
        return step(back_terms, *state["back"], gate_role, up_role)

    def expand_grad(index):
        return lambda: step(
            product_pairs, state["back"][index], state["two near"], far_back[index], state["two far"]
        )

    parts, (gate_grad, up_grad, far_output, near_output), _ = plan.settle(
        near_terms,
        far,
        rows,
        (
            [],
            [expand_grad(0)],
            [
                expand_grad(1),
                work(product_last, state["up far"][2], shrink_role),
                work(product_last, state["up near"][2], shrink_role),
            ],
        ),
    )
    gate_summed = lax.psum_scatter(gate_grad, "dp", scatter_dimension=0, tiled=True)
    up_summed = lax.psum_scatter(up_grad, "dp", scatter_dimension=0, tiled=True)

    shrink_summed = wait(shrink_summed)

    def shrink_update(gradient, *values):
        gradient = gradient[None].astype(F32)
        return gradient, *adamw(values[0], gradient, *values[1:], RATE, DECAY)

    def shrink_work():
        state["shrink"] = step(
            shrink_update, state["shrink back"], shrink_weight, shrink_moment, shrink_square
        )

    def expand_update(gate, up, weight, moment, square):
        gradient = jnp.stack([gate, up]).astype(F32)
        return gradient, *adamw(weight, gradient, moment, square, RATE, DECAY)

    def back_two(middle, scale, gain, grad_out, own, beside, above):
        grad = own.astype(F32) + beside.astype(F32) + above.astype(F32)
        middle_back, gain_grad = norm_back(middle, scale, gain, grad)
        middle_grad = grad_out + middle_back
        return middle_grad.astype(BF16), middle_grad, gain_grad

    branch_low, middle_grad, gain_two_grad = step(
        back_two, middle, scale_two, gain_two, grad_out, *parts
    )

    def attend_back(name, grads, blocks, places, earlier):
        normed, joint, attended = state["attend " + name]
        return step(
            attend_back_blocks,
            grads,
            blocks,
            mixing_role,
            entry_role,
            joint,
            attended,
            normed,
            state["turn " + name],
            places,
            earlier,
        )

    def order_gains(gain_one_grad, gain_two_grad):
        gains = jnp.stack([gain_one_grad[0], gain_two_grad])
        gains = gains.reshape(2, dp, fsdp, width // (dp * fsdp)).transpose(2, 1, 0, 3)
        return jnp.take(gains, jnp.arange(fsdp) ^ role, axis=0)

    def extra_output(k, came):
        if k == 0:
            return [(far_output, 1)]
        if k == 1:
            return []
        state["sums"] = step(add_low, near_output, came[0][0])
        across = state["sums"][3 * rows :]
        return [(across[: rows // 2], 2), (across[rows // 2 :], 4)]

    def back_near(near_branch):
        state["near back"] = attend_back("near", near_branch, spread_tokens, near_places, [])

    def back_far():
        state["far back"] = attend_back(
            "far", far_branch, far_tokens, far_places, state["near back"][1:]
        )

    _, far_branch, came, _ = plan.spread(
        branch_low,
        None,
        ([], [], [back_near]),
        extra_output,
    )
    gate_summed = wait(gate_summed)
    if plan.short:
        beside, above = step(functools.partial(plan.merge, rows), state["sums"], *came[2])
        parts, _ = window([(beside, 2), (above, 4)], back_far)
        parts = [state["sums"][:rows], *parts]
    else:
        parts, _, _ = plan.settle(lambda: near_output, far_output, rows, ([], [back_far], []))
    layer_output = step(
        lambda *a: sum((value.astype(F32) for value in a[1:]), a[0]).astype(BF16), middle, *parts
    )
    near, far = state["near back"][0], state["far back"][0]
    up_summed = wait(up_summed)

    def lower_sums():
        _, entry_grad, mixing_grad, gain_grad = state["far back"]
        state["entry"], state["mixing"] = step(
            lambda a, b: (low_of(a), low_of(b.T)), entry_grad, mixing_grad
        )
        state["gain"] = step(order_gains, gain_grad, gain_two_grad)

    (got,), _ = window(
        [(far, 1)], lower_sums, store("shrink back", plan.columns_back, shrink_summed)
    )
    entry_grad, mixing_grad, gains = state["entry"], state["mixing"], state["gain"]
    if whole_heads:
        mixing_summed = lax.psum_scatter(mixing_grad, "dp", scatter_dimension=0, tiled=True)
        entry_gradient = lax.psum_scatter(
            entry_grad.reshape(3, dp * HEAD, width), "dp", scatter_dimension=1, tiled=True
        )
    else:
        entry_full = lax.dynamic_update_slice_in_dim(
            jnp.zeros((3, width, width), BF16),
            entry_grad.reshape(3, span, width),
            role * span,
            axis=1,
        )
        mixing_full = lax.dynamic_update_slice_in_dim(
            jnp.zeros((width, width), BF16), mixing_grad, role * span, axis=1
        )
        entry_gradient = lax.psum_scatter(entry_full, AXES, scatter_dimension=1, tiled=True)
        mixing_summed = lax.psum_scatter(mixing_full, AXES, scatter_dimension=0, tiled=True)

    def mixing_update(gradient, *values):
        if whole_heads:
            gradient = plan.columns_back(gradient)
        gradient = gradient[None].astype(F32)
        return gradient, *adamw(values[0], gradient, *values[1:], MIXING_RATE, DECAY)

    parts, _, gains = plan.settle(
        lambda: near,
        far,
        rows,
        (
            [],
            [lambda: shrink_work()],
            [
                store(
                    "expand",
                    expand_update,
                    gate_summed,
                    up_summed,
                    expand_weight,
                    expand_moment,
                    expand_square,
                ),
                store(
                    "mixing new",
                    mixing_update,
                    mixing_summed,
                    mixing_weight,
                    mixing_moment,
                    mixing_square,
                ),
            ],
        ),
        gains,
        got,
    )
    mixing_gradient, *mixing_new = state["mixing new"]
    def back_input(inputs, gain, middle_grad, *parts):
        scale = lax.rsqrt(jnp.mean(inputs * inputs, axis=-1, keepdims=True) + EPS)
        grad = sum(value.astype(F32) for value in parts)
        return middle_grad + norm_back(inputs, scale, gain, grad)[0]

    input_gradient = step(back_input, inputs, gain_one, middle_grad, *parts)

    def order_dp(gains):
        return jnp.take(gains[0], jnp.arange(dp) ^ lax.axis_index("dp"), axis=0)

    gains = step(order_dp, gains)
    for bit in reversed([1 << k for k in range((dp - 1).bit_length())]):
        (got,), _ = window([(gains[bit:], -bit)])
        gains = step(lambda a, b: a[:bit] + b, gains, got)
    gain_grads = gains[0]
    attention_gradient, feedforward_gradient = gain_grads[:1], gain_grads[1:]
    shrink_gradient, *shrink_new = state["shrink"]
    expand_gradient, *expand_new = state["expand"]
    entry_gradient = entry_gradient.astype(F32)
    entry_new = adamw(entry_weight, entry_gradient, entry_moment, entry_square, RATE, DECAY)
    attention_new = adamw(
        attention_gain, attention_gradient, attention_moment, attention_square, GAIN_RATE, 0.0
    )
    feedforward_new = adamw(
        feedforward_gain,
        feedforward_gradient,
        feedforward_moment,
        feedforward_square,
        GAIN_RATE,
        0.0,
    )
    return (
        layer_output,
        input_gradient,
        entry_gradient,
        mixing_gradient,
        attention_gradient,
        expand_gradient,
        shrink_gradient,
        feedforward_gradient,
        entry_new[0],
        mixing_new[0],
        attention_new[0],
        expand_new[0],
        shrink_new[0],
        feedforward_new[0],
        entry_new[1],
        entry_new[2],
        mixing_new[1],
        mixing_new[2],
        attention_new[1],
        attention_new[2],
        expand_new[1],
        expand_new[2],
        shrink_new[1],
        shrink_new[2],
        feedforward_new[1],
        feedforward_new[2],
    )


def solution(mesh):
    placed = (
        P(("dp", "fsdp"), None),
        P(("dp", "fsdp")),
        P(("dp", "fsdp"), None),
        P(None, ("dp", "fsdp"), None),
        P(None, ("dp", "fsdp"), None),
        P(None, ("dp", "fsdp")),
        P(None, ("dp", "fsdp"), None),
        P(None, ("dp", "fsdp"), None),
        P(None, ("dp", "fsdp")),
        P(None, ("dp", "fsdp"), None),
        P(None, ("dp", "fsdp"), None),
        P(None, ("dp", "fsdp"), None),
        P(None, ("dp", "fsdp"), None),
        P(None, ("dp", "fsdp")),
        P(None, ("dp", "fsdp")),
        P(None, ("dp", "fsdp"), None),
        P(None, ("dp", "fsdp"), None),
        P(None, ("dp", "fsdp"), None),
        P(None, ("dp", "fsdp"), None),
        P(None, ("dp", "fsdp")),
        P(None, ("dp", "fsdp")),
    )
    return jax.shard_map(
        functools.partial(local, mesh.shape["dp"], mesh.shape["fsdp"]),
        mesh=mesh,
        in_specs=placed,
        out_specs=(
            P(("dp", "fsdp"), None),
            P(("dp", "fsdp"), None),
            P(None, ("dp", "fsdp"), None),
            P(None, ("dp", "fsdp"), None),
            P(None, ("dp", "fsdp")),
            P(None, ("dp", "fsdp"), None),
            P(None, ("dp", "fsdp"), None),
            P(None, ("dp", "fsdp")),
            P(None, ("dp", "fsdp"), None),
            P(None, ("dp", "fsdp"), None),
            P(None, ("dp", "fsdp")),
            P(None, ("dp", "fsdp"), None),
            P(None, ("dp", "fsdp"), None),
            P(None, ("dp", "fsdp")),
            P(None, ("dp", "fsdp"), None),
            P(None, ("dp", "fsdp"), None),
            P(None, ("dp", "fsdp"), None),
            P(None, ("dp", "fsdp"), None),
            P(None, ("dp", "fsdp")),
            P(None, ("dp", "fsdp")),
            P(None, ("dp", "fsdp"), None),
            P(None, ("dp", "fsdp"), None),
            P(None, ("dp", "fsdp"), None),
            P(None, ("dp", "fsdp"), None),
            P(None, ("dp", "fsdp")),
            P(None, ("dp", "fsdp")),
        ),
        check_vma=False,
    )
```

time: 763 us -> 724 us (0.949)
  Pallas kernels: 0 us -> 83.1 us
  matrix products: 197 us -> 132 us
  local copies, waits for them, and re-layouts: 137 us -> 95 us
  waiting for transfers between devices: 209 us -> 231 us
  other arithmetic: 105 us -> 85.1 us
  blocking collectives: 31.6 us -> 21.3 us
    pallas_call x0 -> x4, Pallas kernels: none -> 83.1 us  [the longest x2 57.1 us: attend_back_blocks(): pl.pallas_call(functools.partial(attend_back_kernel, group, not earlier),...]
    reshape x21 -> x7, local copies, waits for them, and re-layouts: 31.9 us -> 4.28 us  [the longest x2 2.06 us: columns_back(): blocks.reshape(self.fsdp, rows, self.dp, width).transpose(1, 2, 0, 3)]
    dot_general x12 -> x0, matrix products: 22.9 us -> none  [the longest x2 6.08 us: attend_back(): jnp.einsum('bqhd,bkhd->bhqk', attended_grad, value_heads, preferred_eleme...]
    unnamed x319 -> x211, local copies, waits for them, and re-layouts: 42.5 us -> 21.3 us
    dot_general x10 -> x6, matrix products: 53 us -> 34.6 us  [contract_first(): lax.dot_general(left, right, (((0,), (0,)), ((), ())), preferred_element_...]
    optimization_barrier x1 -> x11, local copies, waits for them, and re-layouts: 0.12 us -> 16.8 us  [tie(): return lax.optimization_barrier((tuple(values), self.clock))[0]]
    all_to_all x1, waiting for transfers between devices: 0.01 us -> 14.7 us  [exchange(): return lax.all_to_all(blocks, 'fsdp', 0, 0, tiled=True)]
    ppermute x56, waiting for transfers between devices: 183 us -> 169 us  [window(): came.append(lax.ppermute(value, axis, pairs))]
  transfers between devices with their start and end apart: 69 -> 69, of which waited for: 33 -> 23; matrix products, arithmetic and copies ran while one was open for 54% -> 41% of each run, Pallas kernels for 0% -> 12%
where the time goes in v2:
time: 724 us; the launch traced here: 718 us
  waiting for transfers between devices  231 us (32%)
  matrix products  132 us (18%)
  local copies, waits for them, and re-layouts  95 us (13%)
  other arithmetic  85.1 us (12%)
  Pallas kernels  83.1 us (11%)
  starting transfers between devices  53.6 us (7%)
  blocking collectives  21.3 us (3%)
  between operations  16.4 us (2%)
    ppermute x56, waiting for transfers between devices, window(): came.append(lax.ppermute(value, axis, pairs))  169 us
    pallas_call x2, Pallas kernels, attend_back_blocks(): pl.pallas_call(functools.partial(attend_back_kernel, group, not earlier),...  57.1 us
    dot_general x6, matrix products, plain_product(): return jnp.dot(left, right, preferred_element_type=jnp.float32)  51.7 us
    dot_general x8, matrix products, contract_last(): lax.dot_general(left, right, (((1,), (1,)), ((), ())), preferred_element_...  45.9 us
    ppermute x56, starting transfers between devices, window(): came.append(lax.ppermute(value, axis, pairs))  41 us
    dot_general x6, matrix products, contract_first(): lax.dot_general(left, right, (((0,), (0,)), ((), ())), preferred_element_...  34.6 us
    pallas_call x2, Pallas kernels, attend_blocks(): pl.pallas_call(functools.partial(attend_kernel, group), grid=(group,), in...  25.9 us
    all_to_all x2, waiting for transfers between devices, columns_back(): lax.all_to_all(blocks.reshape(self.fsdp, rows, self.dp * width), 'fsdp',...  25.4 us
  transfers between devices with their start and end apart: 69, of which 23 were waited for; matrix products, arithmetic and copies ran while one was open for 41% of the time, Pallas kernels for 12%

profile of v2, /device:TPU:0, one launch (start us, length us, event | category | flops | bytes accessed | tf_op | source)
XLA Modules:
  0.0 717.7 jit_solution(14808723398813524804)
XLA Ops:
  11.1 12.6 %all_gather.21 = bf16[2,4,64]{2,0,1:T(2,128)(2,1)S(1)} all-gather(bf16[2,1,64]{2,0,1:T(2,128)(2,1)S(1)} %copy.128), channel_id=1, replica_groups=mesh['dp'=4,'fsdp'=8] {'dp'}, dimensions={1}, use_global_device_ids=true | all-gather | bytes 1280 | tf_op jit(solution)/shard_map/all_gather | solution.py:489
  35.7 14.7 %all-to-all-done = bf16[8,64,1280]{2,1,0:T(8,128)(2,1)} async-done(((bf16[8,64,1280]{2,1,0:T(8,128)(2,1)}), bf16[8,64,1280]{2,1,0:T(8,128)(2,1)}, u32[]{:S(2)}, u32[]{:S(2)}) %all-to-all-start) | async-done | bytes 1310752 | tf_op jit(solution)/shard_map/all_to_all | solution.py:412
  54.3 17.1 %collective-permute-done.3 = s32[1,256]{1,0:T(1,128)S(1)} collective-permute-done((s32[1,256]{1,0:T(1,128)S(1)}, s32[1,256]{1,0:T(1,128)S(1)}, u32[]{:S(2)}, u32[]{:S(2)}) %collective-permute-start.3) | collective-permute-done | bytes 1056 | tf_op jit(solution)/shard_map/ppermute | solution.py:289
  80.2 9.2 %collective-permute-done.7 = s32[2,256]{1,0:T(2,128)S(1)} collective-permute-done((s32[2,256]{1,0:T(2,128)S(1)}, s32[2,256]{1,0:T(2,128)S(1)}, u32[]{:S(2)}, u32[]{:S(2)}) %collective-permute-start.7) | collective-permute-done | bytes 2080 | tf_op jit(solution)/shard_map/ppermute | solution.py:289
  96.0 8.8 %all-gather = bf16[2,4,512]{1,0,2:T(2,128)(2,1)S(1)} all-gather(bf16[2,4,64]{1,0,2:T(2,128)(2,1)S(1)} %copy.131), channel_id=2, replica_groups=mesh['dp'=4,'fsdp'=8] {'fsdp'}, dimensions={2}, use_global_device_ids=true | all-gather | bytes 9216 | tf_op jit(solution)/shard_map/all_gather | solution.py:492
  116.7 12.9 %shard_map.404 = (bf16[1024,2048]{1,0:T(8,128)(2,1)}, bf16[1024,768]{1,0:T(8,128)(2,1)}, bf16[1024,256]{1,0:T(8,128)(2,1)}) custom-call(bf16[256,2048]{1,0:T(8,128)(2,1)} %collective-permute-done.2.refs_0_.refs_4_, bf16[256,2048]{1,0:T(8,128)(2,1)} %get-tuple-element.615.refs_1_.refs_5_, bf16[256,2048]{1,0:T(8,128)(2,1)} %get-tuple-element.616.refs_2_.refs_6_, ...), custom_call_target="tpu_custom_call" | custom-call | tf_op jit(solution)/shard_map/pallas_call | solution.py:145
  137.0 23.1 %collective-permute-done.10 = bf16[256,2048]{1,0:T(8,128)(2,1)S(1)} collective-permute-done((bf16[256,2048]{1,0:T(8,128)(2,1)S(1)}, bf16[256,2048]{1,0:T(8,128)(2,1)S(1)}, u32[]{:S(2)}, u32[]{:S(2)}) %collective-permute-start.10) | collective-permute-done | bytes 1048608 | tf_op jit(solution)/shard_map/ppermute | solution.py:289
  176.9 13.0 %shard_map.405 = (bf16[1024,2048]{1,0:T(8,128)(2,1)}, bf16[1024,768]{1,0:T(8,128)(2,1)}, bf16[1024,256]{1,0:T(8,128)(2,1)}) custom-call(bf16[256,2048]{1,0:T(8,128)(2,1)} %refs_4_, bf16[256,2048]{1,0:T(8,128)(2,1)} %copy-done.11, bf16[256,2048]{1,0:T(8,128)(2,1)} %copy-done.12, bf16[256,2048]{1,0:T(8,128)(2,1)} %copy-done.29, f32[1,2048]{1,0:T(1,128)} %bitcast.160, ...), custom_call_target="tpu_custom_call" | custom-call | tf_op jit(solution)/shard_map/pallas_call | solution.py:145
  205.6 11.2 %collective-permute-done.14 = bf16[128,2048]{1,0:T(8,128)(2,1)S(1)} collective-permute-done((bf16[128,2048]{1,0:T(8,128)(2,1)S(1)}, bf16[128,2048]{1,0:T(8,128)(2,1)S(1)}, u32[]{:S(2)}, u32[]{:S(2)}) %collective-permute-start.14) | collective-permute-done | bytes 524320 | tf_op jit(solution)/shard_map/ppermute | solution.py:289
  222.2 20.3 %collective-permute-done.19 = bf16[256,2048]{1,0:T(8,128)(2,1)S(1)} collective-permute-done((bf16[256,2048]{1,0:T(8,128)(2,1)S(1)}, bf16[256,2048]{1,0:T(8,128)(2,1)S(1)}, u32[]{:S(2)}, u32[]{:S(2)}) %collective-permute-start.19) | collective-permute-done | bytes 1048608 | tf_op jit(solution)/shard_map/ppermute | solution.py:289
  246.7 21.2 %collective-permute-done.22 = bf16[256,2048]{1,0:T(8,128)(2,1)S(1)} collective-permute-done((bf16[256,2048]{1,0:T(8,128)(2,1)S(1)}, bf16[256,2048]{1,0:T(8,128)(2,1)S(1)}, u32[]{:S(2)}, u32[]{:S(2)}) %collective-permute-start.22) | collective-permute-done | bytes 1048608 | tf_op jit(solution)/shard_map/ppermute | solution.py:289
  274.8 12.1 %collective-permute-done.25 = bf16[128,2048]{1,0:T(8,128)(2,1)} collective-permute-done((bf16[128,2048]{1,0:T(8,128)(2,1)}, bf16[128,2048]{1,0:T(8,128)(2,1)}, u32[]{:S(2)}, u32[]{:S(2)}) %collective-permute-start.25) | collective-permute-done | bytes 524320 | tf_op jit(solution)/shard_map/ppermute | solution.py:289
  331.3 21.3 %all-gather.13.cloned.1.call-done = bf16[32,64,1024]{2,1,0:T(8,128)(2,1)} async-done(((bf16[8,64,1024]{2,1,0:T(8,128)(2,1)}), bf16[32,64,1024]{2,1,0:T(8,128)(2,1)}) %all-gather.13.cloned.1.call-update) | async-done | bytes 4194320 | tf_op jit(solution)/shard_map/all_gather | solution.py:531
  352.7 11.8 %multiply_convert_fusion.2 = (bf16[1024,1024]{1,0:T(8,128)(2,1)S(1)}, bf16[1024,1024]{1,0:T(8,128)(2,1)S(1)}) fusion(f32[1024,1024]{1,0:T(8,128)} %copy-done.85, f32[1024,1024]{1,0:T(8,128)} %get-tuple-element.511, bf16[1024,2048]{1,0:T(8,128)(2,1)} %copy-done.48, bf16[2048,1024]{1,0:T(8,128)(2,1)} %bitcast.190), kind=kOutput, calls=%fused_computation.18 | convolution fusion | flops 4308598784 | bytes 20971520 | tf_op jit(solution)/shard_map/dot_general | solution.py:39
  380.1 9.8 %multiply_convert_fusion = (bf16[1024,1024]{1,0:T(8,128)(2,1)}, bf16[1024,1024]{1,0:T(8,128)(2,1)}) fusion(f32[1024,1024]{1,0:T(8,128)} %copy-done.84, f32[1024,1024]{1,0:T(8,128)} %get-tuple-element.520, bf16[1024,2048]{1,0:T(8,128)(2,1)S(1)} %copy-done.47, bf16[2048,1024]{1,0:T(8,128)(2,1)S(1)} %bitcast.192), kind=kOutput, calls=%fused_computation.15 | convolution fusion | flops 4308598784 | bytes 20971520 | tf_op jit(solution)/shard_map/dot_general | solution.py:39
  389.9 8.5 %fusion.38 = f32[1024,2048]{1,0:T(8,128)} fusion(bf16[1024,1024]{1,0:T(8,128)(2,1)} %get-tuple-element.531, bf16[1024,2048]{1,0:T(8,128)(2,1)S(1)} %bitcast.185), kind=kOutput, calls=%fused_computation.184 | convolution fusion | flops 4294967296 | bytes 14680064 | tf_op jit(solution)/shard_map/dot_general | solution.py:39
  416.0 8.0 %add_convert_fusion.3 = bf16[1024,2048]{1,0:T(8,128)(2,1)} fusion(f32[1024,2048]{1,0:T(8,128)S(1)} %fusion.39, bf16[1024,1024]{1,0:T(8,128)(2,1)} %copy-done.88, bf16[1024,2048]{1,0:T(8,128)(2,1)S(1)} %copy-done.54), kind=kOutput, calls=%fused_computation.5 | convolution fusion | flops 4299161600 | bytes 18874368 | tf_op jit(solution)/shard_map/dot_general | solution.py:33
  442.7 8.4 %convolution_convert_fusion.3 = bf16[1024,2048]{1,0:T(8,128)(2,1)} fusion(bf16[1024,1024]{1,0:T(8,128)(2,1)S(1)} %copy-done.90, bf16[2048,1024]{1,0:T(8,128)(2,1)} %bitcast.191), kind=kOutput, calls=%fused_computation.26 | convolution fusion | flops 4297064448 | bytes 10485760 | tf_op jit(solution)/shard_map/dot_general | solution.py:27
  467.1 22.7 %collective-permute-done.34.refs_1_ = bf16[256,2048]{1,0:T(8,128)(2,1)S(1)} collective-permute-done((bf16[256,2048]{1,0:T(8,128)(2,1)}, bf16[256,2048]{1,0:T(8,128)(2,1)S(1)}, u32[]{:S(2)}, u32[]{:S(2)}) %collective-permute-start.34) | collective-permute-done | bytes 1048608 | tf_op jit(solution)/shard_map/ppermute | solution.py:289
  495.8 12.3 %collective-permute-done.38 = bf16[128,2048]{1,0:T(8,128)(2,1)S(1)} collective-permute-done((bf16[128,2048]{1,0:T(8,128)(2,1)S(1)}, bf16[128,2048]{1,0:T(8,128)(2,1)S(1)}, u32[]{:S(2)}, u32[]{:S(2)}) %collective-permute-start.38) | collective-permute-done | bytes 524320 | tf_op jit(solution)/shard_map/ppermute | solution.py:289
  525.8 27.1 %shard_map.406 = (bf16[1024,2048]{1,0:T(8,128)(2,1)}, f32[768,2048]{1,0:T(8,128)}, f32[256,2048]{1,0:T(8,128)}, f32[1,2048]{1,0:T(1,128)}) custom-call(bf16[256,2048]{1,0:T(8,128)(2,1)} %get-tuple-element.580.refs_0_, bf16[256,2048]{1,0:T(8,128)(2,1)} %copy-done.28, bf16[256,2048]{1,0:T(8,128)(2,1)} %collective-permute-done.35.refs_2_, ...), custom_call_target="tpu_custom_call" | custom-call | tf_op jit(solution)/shard_map/pallas_call | solution.py:223
  567.0 30.0 %shard_map.407 = (bf16[1024,2048]{1,0:T(8,128)(2,1)}, f32[768,2048]{1,0:T(8,128)}, f32[256,2048]{1,0:T(8,128)}, f32[1,2048]{1,0:T(1,128)}) custom-call(bf16[256,2048]{1,0:T(8,128)(2,1)} %collective-permute-done.36.refs_0_, bf16[256,2048]{1,0:T(8,128)(2,1)} %get-tuple-element.611.refs_1_, bf16[256,2048]{1,0:T(8,128)(2,1)} %get-tuple-element.612.refs_2_, ...), custom_call_target="tpu_custom_call" | custom-call | tf_op jit(solution)/shard_map/pallas_call | solution.py:223
  614.1 14.7 %all-to-all-done.1 = bf16[8,64,1024]{2,1,0:T(8,128)(2,1)S(1)} async-done(((bf16[8,64,1024]{2,1,0:T(8,128)(2,1)}), bf16[8,64,1024]{2,1,0:T(8,128)(2,1)S(1)}, u32[]{:S(2)}, u32[]{:S(2)}) %all-to-all-start.1) | async-done | bytes 1048608 | tf_op jit(solution)/shard_map/all_to_all | solution.py:417
  670.3 10.6 %all-to-all-done.2 = bf16[8,64,256]{2,1,0:T(8,128)(2,1)S(1)} async-done(((bf16[8,64,256]{2,1,0:T(8,128)(2,1)}), bf16[8,64,256]{2,1,0:T(8,128)(2,1)S(1)}, u32[]{:S(2)}, u32[]{:S(2)}) %all-to-all-start.2) | async-done | bytes 262176 | tf_op jit(solution)/shard_map/all_to_all | solution.py:417
  (523 shorter events, 339.8 us)
Async XLA Ops:
  7.2 102.1 %all-gather.9.cloned.1.call-start = ((), (), s32[]{:S(2)}) async-start(), calls=%async_computation.8 | async-start | bytes 3932160 | tf_op jit(solution)/shard_map/all_gather | solution.py:482
  31.6 98.0 %all-gather.11.cloned.1.call-start = ((), (), s32[]{:S(2)}) async-start(), calls=%async_computation.9 | async-start | bytes 1310720 | tf_op jit(solution)/shard_map/all_gather | solution.py:526
  31.7 39.7 %collective-permute-start = (bf16[256,2048]{1,0:T(8,128)(2,1)S(1)}, bf16[256,2048]{1,0:T(8,128)(2,1)S(1)}, u32[]{:S(2)}, u32[]{:S(2)}) collective-permute-start(bf16[256,2048]{1,0:T(8,128)(2,1)S(1)} %copy-done.19), channel_id=1, source_target_pairs={{0,2},{1,3},{2,0},{3,1},{4,6},{5,7},{6,4},{7,5},{8,10},{9,11},{10,... | collective-permute-start | bytes 3145736 | tf_op jit(solution)/shard_map/ppermute | solution.py:289
  33.6 37.8 %collective-permute-start.1 = (bf16[256,2048]{1,0:T(8,128)(2,1)S(1)}, bf16[256,2048]{1,0:T(8,128)(2,1)S(1)}, u32[]{:S(2)}, u32[]{:S(2)}) collective-permute-start(bf16[256,2048]{1,0:T(8,128)(2,1)S(1)} %copy-done.19), channel_id=1, source_target_pairs={{0,4},{1,5},{2,6},{3,7},{4,0},{5,1},{6,2},{7,3},{8,12},{9,13},{10,... | collective-permute-start | bytes 3145736 | tf_op jit(solution)/shard_map/ppermute | solution.py:289
  35.1 36.3 %collective-permute-start.2 = (bf16[256,2048]{1,0:T(8,128)(2,1)S(1)}, bf16[256,2048]{1,0:T(8,128)(2,1)}, u32[]{:S(2)}, u32[]{:S(2)}) collective-permute-start(bf16[256,2048]{1,0:T(8,128)(2,1)S(1)} %copy-done.19), channel_id=1, source_target_pairs={{0,1},{1,0},{2,3},{3,2},{4,5},{5,4},{6,7},{7,6},{8,9},{9,8},{10,11... | collective-permute-start | bytes 3145736 | tf_op jit(solution)/shard_map/ppermute | solution.py:289
  35.1 36.3 %collective-permute-start.3 = (s32[1,256]{1,0:T(1,128)S(1)}, s32[1,256]{1,0:T(1,128)S(1)}, u32[]{:S(2)}, u32[]{:S(2)}) collective-permute-start(s32[1,256]{1,0:T(1,128)S(1)} %bitcast.179), channel_id=1, source_target_pairs={{0,2},{1,3},{2,0},{3,1},{4,6},{5,7},{6,4},{7,5},{8,10},{9,11},{10,... | collective-permute-start | bytes 3080 | tf_op jit(solution)/shard_map/ppermute | solution.py:289
  73.8 120.4 %all-gather.15.cloned.1.call-start = ((), (), s32[]{:S(2)}) async-start(), calls=%async_computation.16 | async-start | bytes 5242880 | tf_op jit(solution)/shard_map/all_gather | solution.py:524
  80.2 194.6 %all-gather.17.cloned.1.call-start = ((), (), s32[]{:S(2)}) async-start(), calls=%async_computation.17 | async-start | bytes 5242880 | tf_op jit(solution)/shard_map/all_gather | solution.py:530
  134.5 62.1 %collective-permute-start.13 = (bf16[1024,2048]{1,0:T(8,128)(2,1)}, bf16[1024,2048]{1,0:T(8,128)(2,1)}, u32[]{:S(2)}, u32[]{:S(2)}) collective-permute-start(bf16[1024,2048]{1,0:T(8,128)(2,1)} %convolution_convert_fusion.1), channel_id=1, source_target_pairs={{0,1},{1,0},{2,3},{3,2},{4,5},{5,4},{6,7},{7,6},{8,9},{9,8},{10,11... | collective-permute-start | bytes 12582920 | tf_op jit(solution)/shard_map/ppermute | solution.py:289
  165.2 29.0 %collective-permute-start.18 = (bf16[512,2048]{1,0:T(8,128)(2,1)}, bf16[512,2048]{1,0:T(8,128)(2,1)}, u32[]{:S(2)}, u32[]{:S(2)}) collective-permute-start(bf16[512,2048]{1,0:T(8,128)(2,1)} %constant_dynamic-update-slice_fusion.4), channel_id=1, source_target_pairs={{0,1},{1,0},{2,3},{3,2},{4,5},{5,4},{6,7},{7,6},{8,9},{9,8},{10,11... | collective-permute-start | bytes 6291464 | tf_op jit(solution)/shard_map/ppermute | solution.py:289
  171.1 181.6 %all-gather.13.cloned.1.call-start = ((), (), s32[]{:S(2)}) async-start(), calls=%async_computation.10 | async-start | bytes 5242880 | tf_op jit(solution)/shard_map/all_gather | solution.py:531
  274.2 183.1 %reduce-scatter.6.cloned.1.call-start = ((), (), s32[]{:S(2)}) async-start(), calls=%async_computation.11 | async-start | bytes 5242880 | tf_op jit(solution)/shard_map/reduce_scatter | solution.py:590
  331.3 221.8 %reduce-scatter.8.cloned.1.call-start = ((), (), s32[]{:S(2)}) async-start(), calls=%async_computation.12 | async-start | bytes 5242880 | tf_op jit(solution)/shard_map/reduce_scatter | solution.py:630
  425.3 174.8 %reduce-scatter.10.cloned.1.call-start = ((), (), s32[]{:S(2)}) async-start(), calls=%async_computation.13 | async-start | bytes 5242880 | tf_op jit(solution)/shard_map/reduce_scatter | solution.py:631
  467.0 195.8 %reduce-scatter.12.cloned.1.call-start = ((), (), s32[]{:S(2)}) async-start(), calls=%async_computation.14 | async-start | bytes 1310720 | tf_op jit(solution)/shard_map/reduce_scatter | solution.py:727
  517.3 35.7 %collective-permute-start.41 = (bf16[256,2048]{1,0:T(8,128)(2,1)}, bf16[256,2048]{1,0:T(8,128)(2,1)}, u32[]{:S(2)}, u32[]{:S(2)}) collective-permute-start(bf16[256,2048]{1,0:T(8,128)(2,1)} %constant_dynamic-update-slice_fusion.28.refs_3_), channel_id=1, source_target_pairs={{0,1},{1,0},{2,3},{3,2},{4,5},{5,4},{6,7},{7,6},{8,9},{9,8},{10,11... | collective-permute-start | bytes 3145736 | tf_op jit(solution)/shard_map/ppermute | solution.py:289
  517.3 35.7 %collective-permute-start.42 = (bf16[128,2048]{1,0:T(8,128)(2,1)}, bf16[128,2048]{1,0:T(8,128)(2,1)}, u32[]{:S(2)}, u32[]{:S(2)}) collective-permute-start(bf16[128,2048]{1,0:T(8,128)(2,1)} %get-tuple-element.578), channel_id=1, source_target_pairs={{0,2},{1,3},{2,0},{3,1},{4,6},{5,7},{6,4},{7,5},{8,10},{9,11},{10,... | collective-permute-start | bytes 1572872 | tf_op jit(solution)/shard_map/ppermute | solution.py:289
  518.8 34.2 %collective-permute-start.43 = (bf16[128,2048]{1,0:T(8,128)(2,1)}, bf16[128,2048]{1,0:T(8,128)(2,1)}, u32[]{:S(2)}, u32[]{:S(2)}) collective-permute-start(bf16[128,2048]{1,0:T(8,128)(2,1)} %get-tuple-element.579), channel_id=1, source_target_pairs={{0,4},{1,5},{2,6},{3,7},{4,0},{5,1},{6,2},{7,3},{8,12},{9,13},{10,... | collective-permute-start | bytes 1572872 | tf_op jit(solution)/shard_map/ppermute | solution.py:289
  558.6 38.4 %collective-permute-start.44 = (bf16[256,2048]{1,0:T(8,128)(2,1)}, bf16[256,2048]{1,0:T(8,128)(2,1)}, u32[]{:S(2)}, u32[]{:S(2)}) collective-permute-start(bf16[256,2048]{1,0:T(8,128)(2,1)} %pad_maximum_fusion.6), channel_id=1, source_target_pairs={{0,2},{1,3},{2,0},{3,1},{4,6},{5,7},{6,4},{7,5},{8,10},{9,11},{10,... | collective-permute-start | bytes 3145736 | tf_op jit(solution)/shard_map/ppermute | solution.py:289
  559.2 37.8 %collective-permute-start.45 = (bf16[256,2048]{1,0:T(8,128)(2,1)}, bf16[256,2048]{1,0:T(8,128)(2,1)}, u32[]{:S(2)}, u32[]{:S(2)}) collective-permute-start(bf16[256,2048]{1,0:T(8,128)(2,1)} %pad_maximum_fusion.7), channel_id=1, source_target_pairs={{0,4},{1,5},{2,6},{3,7},{4,0},{5,1},{6,2},{7,3},{8,12},{9,13},{10,... | collective-permute-start | bytes 3145736 | tf_op jit(solution)/shard_map/ppermute | solution.py:289
  600.2 31.4 %collective-permute-start.46 = (bf16[1024,2048]{1,0:T(8,128)(2,1)}, bf16[1024,2048]{1,0:T(8,128)(2,1)}, u32[]{:S(2)}, u32[]{:S(2)}) collective-permute-start(bf16[1024,2048]{1,0:T(8,128)(2,1)} %get-tuple-element.639), channel_id=1, source_target_pairs={{0,1},{1,0},{2,3},{3,2},{4,5},{5,4},{6,7},{7,6},{8,9},{9,8},{10,11... | collective-permute-start | bytes 12582920 | tf_op jit(solution)/shard_map/ppermute | solution.py:289
  613.5 91.4 %reduce-scatter.14.cloned.1.call-start = ((), (), s32[]{:S(2)}) async-start(), calls=%async_computation.15 | async-start | bytes 3932160 | tf_op jit(solution)/shard_map/reduce_scatter | solution.py:728
  653.7 34.7 %collective-permute-start.50 = (bf16[256,2048]{1,0:T(8,128)(2,1)}, bf16[256,2048]{1,0:T(8,128)(2,1)S(1)}, u32[]{:S(2)}, u32[]{:S(2)}) collective-permute-start(bf16[256,2048]{1,0:T(8,128)(2,1)} %pad_maximum_fusion.8), channel_id=1, source_target_pairs={{0,2},{1,3},{2,0},{3,1},{4,6},{5,7},{6,4},{7,5},{8,10},{9,11},{10,... | collective-permute-start | bytes 3145736 | tf_op jit(solution)/shard_map/ppermute | solution.py:289
  654.0 34.3 %collective-permute-start.51 = (bf16[256,2048]{1,0:T(8,128)(2,1)}, bf16[256,2048]{1,0:T(8,128)(2,1)}, u32[]{:S(2)}, u32[]{:S(2)}) collective-permute-start(bf16[256,2048]{1,0:T(8,128)(2,1)} %pad_maximum_fusion.9), channel_id=1, source_target_pairs={{0,4},{1,5},{2,6},{3,7},{4,0},{5,1},{6,2},{7,3},{8,12},{9,13},{10,... | collective-permute-start | bytes 3145736 | tf_op jit(solution)/shard_map/ppermute | solution.py:289
  (140 other events, 1981.3 us)
Sparse Core Ops, SparseCore 0:
  10.2 66.1 all-gather.8
  78.5 26.6 all-gather.10
  107.4 80.2 all-gather.14
  189.1 79.2 all-gather.16
  274.3 78.2 all-gather.12
  354.8 75.2 reduce-scatter.5
  432.5 77.2 reduce-scatter.7
  512.1 77.2 reduce-scatter.9
  603.0 25.7 reduce-scatter.11
  631.0 58.8 reduce-scatter.13

commit v3 on v2

--- a/solution.py
+++ b/solution.py
@@ -131,12 +131,12 @@
     joint[:, 2 * span :] = mixed[:, 2 * span :].astype(BF16)
     query, keys, values = (joint[:, part * span : (part + 1) * span] for part in range(3))
     rows = query.shape[0]
-    probs = probs_of(by_head(query), keys, down[0], across[0], False).astype(BF16)
+    probs = probs_of(by_head(query), keys, down[0, :, :1], across[0, :1], False).astype(BF16)
     found = plain_product(probs.reshape(-1, rows), values)
     attended[...] = own_columns(found, rows).astype(BF16)
 
 
-def attend_blocks(blocks, gain, weight, cosine, sine, places):
+def attend_blocks(blocks, gain, weight, cosine, sine, down, across):
     group = len(blocks)
     rows, width = blocks[0].shape
     span = weight.shape[0] // 3
@@ -148,8 +148,8 @@
         in_specs=[whole(rows, width)] * group
         + [whole(1, width), whole(3 * span, width), by_row(span), by_row(span)]
         + [
-            pl.BlockSpec((1, rows, 1), lambda i: (i, 0, 0)),
-            pl.BlockSpec((1, 1, rows), lambda i: (i, 0, 0)),
+            pl.BlockSpec((1, rows, 128), lambda i: (i, 0, 0)),
+            pl.BlockSpec((1, 8, rows), lambda i: (i, 0, 0)),
         ],
         out_specs=[by_row(width), by_row(3 * span), by_row(span)],
         out_shape=[
@@ -158,14 +158,14 @@
         ],
         scratch_shapes=[pltpu.VMEM((rows, width), BF16)],
         compiler_params=pltpu.CompilerParams(vmem_limit_bytes=VMEM_BYTES),
-    )(*blocks, gain[None], weight, cosine, sine, places[:, :, None], places[:, None, :])
+    )(*blocks, gain[None], weight, cosine, sine, down, across)
 
 
 def attend_back_kernel(group, first, *refs):
     grads, blocks, refs = refs[:group], refs[group : 2 * group], refs[2 * group :]
     mixing, weight, joint, attended, normed, cosine, sine, down, across = refs[:9]
     earlier, refs = (None, refs[9:]) if first else (refs[9:12], refs[12:])
-    terms, entry_sum, mixing_sum, gain_sum, held, tokens, back = refs
+    terms, entry_sum, mixing_sum, gain_sum, held, tokens, back, mixing_total = refs
     step = pl.program_id(0)
     for k in range(group):
 
@@ -176,7 +176,7 @@
 
     @pl.when(step == 0)
     def _():
-        for k, sums in ((1, mixing_sum), (2, gain_sum)):
+        for k, sums in ((1, mixing_total), (2, gain_sum)):
             sums[...] = jnp.zeros_like(sums) if first else earlier[k][...]
 
     rows = held.shape[0]
@@ -185,7 +185,7 @@
     query, keys, values = (joint[:, part * span : (part + 1) * span] for part in range(3))
     grad = plain_product(held[...], mixing[...]).astype(BF16)
     key_heads = by_head(keys)
-    probs = probs_of(key_heads, query, down[0], across[0], True)
+    probs = probs_of(key_heads, query, down[0, :, :1], across[0, :1], True)
     prob_grad = contract_last(by_head(values), grad).reshape(probs.shape)
     delta = jnp.sum(probs * prob_grad, axis=1, keepdims=True)
     score_grad = (probs * (prob_grad - delta)).astype(BF16).reshape(-1, rows)
@@ -203,17 +203,20 @@
     value = tokens[...].astype(F32)
     scale = lax.rsqrt(jnp.mean(value * value, axis=-1, keepdims=True) + EPS)
     gain_sum[...] += jnp.sum(term * (value * scale), axis=0, keepdims=True)
-    mixing_sum[...] += contract_first(attended[...], held[...])
+    mixing_total[...] += contract_first(attended[...], held[...])
 
     @pl.when(step == group - 1)
     def _():
         for part in range(3):
             part = slice(part * span, (part + 1) * span)
             found = contract_first(back[:, part], normed[...])
-            entry_sum[part, :] = found if first else earlier[0][part, :] + found
-
-
-def attend_back_blocks(grads, blocks, mixing, weight, joint, attended, normed, turn, places, earlier):
+            if not first:
+                found += earlier[0][part, :]
+            entry_sum[part, :] = found.astype(entry_sum.dtype)
+        mixing_sum[...] = mixing_total[...].astype(mixing_sum.dtype)
+
+
+def attend_back_blocks(grads, blocks, mixing, weight, joint, attended, normed, turn, earlier):
     group = len(blocks)
     rows, width = blocks[0].shape
     span = weight.shape[0] // 3
@@ -227,17 +230,20 @@
         + [whole(width, span), whole(3 * span, width)]
         + [by_row(3 * span), by_row(span), whole(group * rows, width), by_row(span), by_row(span)]
         + [
-            pl.BlockSpec((1, rows, 1), lambda i: (i, 0, 0)),
-            pl.BlockSpec((1, 1, rows), lambda i: (i, 0, 0)),
+            pl.BlockSpec((1, rows, 128), lambda i: (i, 0, 0)),
+            pl.BlockSpec((1, 8, rows), lambda i: (i, 0, 0)),
         ]
         + [whole(*shape) for shape in sums if earlier],
         out_specs=[by_row(width)] + [whole(*shape) for shape in sums],
         out_shape=[jax.ShapeDtypeStruct((group * rows, width), BF16)]
-        + [jax.ShapeDtypeStruct(shape, F32) for shape in sums],
+        + [
+            jax.ShapeDtypeStruct(shape, BF16 if earlier and shape[0] > 1 else F32) for shape in sums
+        ],
         scratch_shapes=[
             pltpu.VMEM((rows, width), BF16),
             pltpu.VMEM((rows, width), BF16),
             pltpu.VMEM((group * rows, 3 * span), BF16),
+            pltpu.VMEM((span, width), F32),
         ],
         compiler_params=pltpu.CompilerParams(vmem_limit_bytes=VMEM_BYTES),
     )(
@@ -249,8 +255,6 @@
         attended,
         normed,
         *turn,
-        places[:, :, None],
-        places[:, None, :],
         *earlier,
     )
 
@@ -260,7 +264,104 @@
     return (
         jnp.tile(jnp.concatenate([cosine, cosine], axis=1), (1, heads)),
         jnp.tile(jnp.concatenate([-sine, sine], axis=1), (1, heads)),
-    )
+        jnp.broadcast_to(places[:, :, None], (*places.shape, 128)),
+        jnp.broadcast_to(places[:, None, :], (places.shape[0], 8, places.shape[1])),
+    )
+
+
+def expand_kernel(group, *refs):
+    blocks, weight, joined, gate, upward, hidden = refs[:group], *refs[group:]
+    rows = blocks[0].shape[0]
+
+    @pl.when(pl.program_id(0) == 0)
+    def _():
+        for k in range(group):
+            joined[k * rows : (k + 1) * rows, :] = blocks[k][...]
+
+    gate[...] = contract_last(joined[...], weight[0])
+    upward[...] = contract_last(joined[...], weight[1])
+    hidden[...] = (gate[...] * jax.nn.sigmoid(gate[...]) * upward[...]).astype(BF16)
+
+
+def expand_blocks(blocks, weight):
+    group = len(blocks)
+    rows, width = blocks[0].shape
+    units = weight.shape[1]
+    tile = min(units, 256)
+    by_unit = pl.BlockSpec((group * rows, tile), lambda j: (0, j))
+    shape = group * rows, units
+    return pl.pallas_call(
+        functools.partial(expand_kernel, group),
+        grid=(units // tile,),
+        in_specs=[pl.BlockSpec((rows, width), lambda j: (0, 0))] * group
+        + [pl.BlockSpec((2, tile, width), lambda j: (0, j, 0))],
+        out_specs=[pl.BlockSpec((group * rows, width), lambda j: (0, 0))] + [by_unit] * 3,
+        out_shape=[
+            jax.ShapeDtypeStruct((group * rows, width), BF16),
+            jax.ShapeDtypeStruct(shape, F32),
+            jax.ShapeDtypeStruct(shape, F32),
+            jax.ShapeDtypeStruct(shape, BF16),
+        ],
+        compiler_params=pltpu.CompilerParams(vmem_limit_bytes=VMEM_BYTES),
+    )(*blocks, weight)
+
+
+def expand_back_kernel(tiles, grads, gate, upward, shrink, weight, gate_grad, up_grad, terms, both):
+    step = pl.program_id(0)
+    tile = gate.shape[1]
+
+    @pl.when(step < tiles)
+    def _():
+        sigma = jax.nn.sigmoid(gate[...])
+        swish = gate[...] * sigma
+        hidden_grad = plain_product(grads[...], shrink[...])
+        slope = sigma * (1.0 + gate[...] * (1.0 - sigma))
+        gate_grad[...] = (hidden_grad * upward[...] * slope).astype(BF16)
+        up_grad[...] = (hidden_grad * swish).astype(BF16)
+        both[step] = gate_grad[...]
+        both[tiles + step] = up_grad[...]
+
+    @pl.when(step >= tiles)
+    def _():
+        total = jnp.zeros(terms.shape, F32)
+        for k in range(2 * tiles):
+            part, first = k // tiles, k % tiles * tile
+            total += plain_product(both[k], weight[part, first : first + tile, :])
+        terms[...] = total.astype(BF16)
+
+
+def expand_back_blocks(grads, gate, upward, shrink, weight):
+    rows, width = grads.shape
+    units = gate.shape[1]
+    tile = min(units, 256)
+    tiles = units // tile
+    cuts = 4
+    early = lambda j: jnp.minimum(j, tiles - 1)
+    late = lambda j: jnp.maximum(j - tiles, 0)
+    by_unit = pl.BlockSpec((rows, tile), lambda j: (0, early(j)))
+    return pl.pallas_call(
+        functools.partial(expand_back_kernel, tiles),
+        grid=(tiles + cuts,),
+        in_specs=[
+            pl.BlockSpec((rows, width), lambda j: (0, 0)),
+            by_unit,
+            by_unit,
+            pl.BlockSpec((width, tile), lambda j: (0, early(j))),
+            pl.BlockSpec((2, units, width // cuts), lambda j: (0, 0, late(j))),
+        ],
+        out_specs=[
+            by_unit,
+            by_unit,
+            pl.BlockSpec((rows, width // cuts), lambda j: (0, late(j))),
+        ],
+        out_shape=[
+            jax.ShapeDtypeStruct((rows, units), BF16),
+            jax.ShapeDtypeStruct((rows, units), BF16),
+            jax.ShapeDtypeStruct((rows, width), BF16),
+        ],
+        scratch_shapes=[pltpu.VMEM((2 * tiles, rows, tile), BF16)],
+        compiler_params=pltpu.CompilerParams(vmem_limit_bytes=VMEM_BYTES),
+    )(grads, gate, upward, shrink, weight)
 
 
 class Plan:
@@ -326,9 +427,10 @@
                 lambda a, b: (a[:half], b[half:], jnp.concatenate([b, a])), above, beside
             )
             (first, second, pair, *got), found = self.window(
-                [(upper, 2), (lower, 4), (pair, 1)] + [(marks, 4)] * small, *works[1]
+                [(upper, 2), (lower, 4), (pair, 1)] + [(marks, 4)] * small + added(1), *works[1]
             )
             gave += found
+            more.append(got)
             across = self.step(lambda a, b: jnp.concatenate([a, b]), first, second)
             if small:
                 marks = self.step(lambda a, b: jnp.concatenate([a, b]), marks, *got)
@@ -355,7 +457,7 @@
         )
         return near, got[: len(near)], (marks, *got[len(near) :]), gave + found
 
-    def settle(self, near, far, rows, works=((), (), ()), small=None, got=None):
+    def settle(self, near, far, rows, works=((), (), ()), small=None, got=None, finish=None):
         gave = []
 
         def sends(bit):
@@ -379,7 +481,10 @@
             if small is not None:
                 for bit in sorted(self.bits, reverse=True):
                     small = sum_small(self.window(sends(bit))[0], bit)
-            return (terms, jnp.zeros_like(terms), jnp.zeros_like(terms)), gave, small
+            parts = terms, jnp.zeros_like(terms), jnp.zeros_like(terms)
+            if finish is not None:
+                finish(*parts)
+            return parts, gave, small
         half = rows // 2
         if got is None:
             (got,), (near, *found) = self.window([(far, 1)], near, *works[0])
@@ -398,7 +503,7 @@
         (beside, above, *more), found = self.window([(beside, 2), (above, 4)] + sends(2), *works[2])
         small = sum_small(more, 2)
         if small is not None:
-            (more,), _ = self.window(sends(1))
+            (more,), _ = self.window(sends(1), lambda: finish(sums[:rows], beside, above))
             small = sum_small([more], 1)
         return (sums[:rows], beside, above), gave + found, small
 
@@ -411,14 +516,16 @@
     def exchange(self, blocks):
         return lax.all_to_all(blocks, "fsdp", 0, 0, tiled=True)
 
-    def columns_back(self, blocks):
-        rows = blocks.shape[0] // self.fsdp
-        width = blocks.shape[1] // self.dp
-        blocks = lax.all_to_all(
-            blocks.reshape(self.fsdp, rows, self.dp * width), "fsdp", 0, 0, tiled=True
-        )
-        blocks = blocks.reshape(self.fsdp, rows, self.dp, width).transpose(1, 2, 0, 3)
-        return blocks.reshape(rows, self.dp * self.fsdp * width)
+    def columns_back(self, *sums):
+        rows = sums[0].shape[0] // self.fsdp
+        blocks = [value.reshape(self.fsdp, rows, -1) for value in sums]
+        blocks = self.exchange(jnp.concatenate(blocks, axis=-1))
+        found, last = [], 0
+        for value in sums:
+            first, last = last, last + value.shape[1]
+            block = blocks[..., first:last].reshape(self.fsdp, rows, self.dp, -1)
+            found.append(block.transpose(1, 2, 0, 3).reshape(rows, self.fsdp * value.shape[1]))
+        return found
 
 
 def local(
@@ -512,8 +619,7 @@
                 ),
             ],
             [
-                store("gate_low", lambda a: a[0].astype(BF16), expand_weight),
-                store("up_low", lambda a: a[1].astype(BF16), expand_weight),
+                store("expand_low", low_of, expand_weight),
                 lambda: state.update(gains=step(gains_fsdp, state["gains_dp"])),
             ],
             [],
@@ -521,13 +627,12 @@
     )
     gain_one, gain_two = state["gains"][0], state["gains"][1]
     shrink_blocks, mixing_blocks = state["columns"]
-    gate_role = lax.all_gather(state["gate_low"], "dp", axis=0, tiled=True)
     if whole_heads:
         mixing_role = lax.all_gather(mixing_blocks, "dp", axis=0, tiled=True).reshape(width, span)
     else:
         mixing_all = lax.all_gather(state["mixing_low"], AXES, axis=0, tiled=True)
         mixing_role = lax.dynamic_slice_in_dim(mixing_all, role * span, span, axis=1)
-    up_role = lax.all_gather(state["up_low"], "dp", axis=0, tiled=True)
+    expand_role = lax.all_gather(state["expand_low"], "dp", axis=1, tiled=True)
     shrink_role = lax.all_gather(shrink_blocks, "dp", axis=0, tiled=True).reshape(width, -1)
 
     inputs = tokens.astype(F32)
@@ -538,10 +643,10 @@
     state["turn near"] = step(lambda a: turn_tables(a, heads), near_places)
     state["turn far"] = step(lambda a: turn_tables(a, heads), far_places)
 
-    def attend_work(name, blocks, places):
+    def attend_work(name, blocks):
         def run(*_):
             state["attend " + name] = step(
-                attend_blocks, blocks, gain_one, entry_role, *state["turn " + name], places
+                attend_blocks, blocks, gain_one, entry_role, *state["turn " + name]
             )
 
         return run
@@ -550,10 +655,9 @@
         grad_low,
         None,
         (
-            [attend_work("far", far_tokens, far_places)],
+            [attend_work("far", far_tokens)],
             [
-                attend_work("near", spread_tokens, near_places),
-                lambda: state.update(gate=wait(gate_role)),
+                attend_work("near", spread_tokens),
             ],
             [],
         ),
@@ -572,45 +676,38 @@
 
     low_two, middle, scale_two = step(norm_middle, inputs, gain_two, *parts)
 
-    def expand(normed, gate_role, up_role):
-        gate = contract_last(normed, gate_role)
-        upward = contract_last(normed, up_role)
-        return gate, upward, (gate * jax.nn.sigmoid(gate) * upward).astype(BF16)
-
     def expand_near(near):
-        state["two near"] = step(join, *near)
-        state["up near"] = step(expand, state["two near"], gate_role, up_role)
-
-    _, far_two, _, _ = plan.spread(low_two, None, ([], [lambda: wait(up_role)], [expand_near]))
-    state["two far"] = step(join, *far_two)
-    state["up far"] = step(expand, state["two far"], gate_role, up_role)
+        state["up near"] = step(expand_blocks, near, expand_role)
+
+    _, far_two, _, _ = plan.spread(
+        low_two, None, ([], [lambda: wait(expand_role)], [expand_near])
+    )
+    state["up far"] = step(expand_blocks, far_two, expand_role)
     shrink_grad = step(
-        product_pairs, state["grad near"], state["up near"][2], state["grad far"], state["up far"][2]
+        product_pairs, state["grad near"], state["up near"][3], state["grad far"], state["up far"][3]
     )
     shrink_summed = lax.psum_scatter(shrink_grad, "dp", scatter_dimension=0, tiled=True)
     shrink_role = wait(shrink_role)
 
-    def back(gate, upward, grad_group, shrink_role):
-        sigma = jax.nn.sigmoid(gate)
-        swish = gate * sigma
-        hidden_grad = plain_product(grad_group, shrink_role)
-        gate_grad = hidden_grad * upward * (sigma * (1.0 + gate * (1.0 - sigma)))
-        upward_grad = hidden_grad * swish
-        return gate_grad.astype(BF16), upward_grad.astype(BF16)
-
-    def back_terms(gate_grad, up_grad, gate_role, up_role):
-        return (plain_product(gate_grad, gate_role) + plain_product(up_grad, up_role)).astype(BF16)
-
-    far_back = step(back, *state["up far"][:2], state["grad far"], shrink_role)
-    far = step(back_terms, *far_back, gate_role, up_role)
+    def expand_back(name):
+        return step(
+            expand_back_blocks,
+            state["grad " + name],
+            *state["up " + name][1:3],
+            shrink_role,
+            expand_role,
+        )
+
+    far_back = expand_back("far")
+    far = far_back[2]
 
     def near_terms():
-        state["back"] = step(back, *state["up near"][:2], state["grad near"], shrink_role)
-        return step(back_terms, *state["back"], gate_role, up_role)
+        state["back"] = expand_back("near")
+        return state["back"][2]
 
     def expand_grad(index):
         return lambda: step(
-            product_pairs, state["back"][index], state["two near"], far_back[index], state["two far"]
+            product_pairs, state["back"][index], state["up near"][0], far_back[index], state["up far"][0]
         )
 
     parts, (gate_grad, up_grad, far_output, near_output), _ = plan.settle(
@@ -622,8 +719,8 @@
             [expand_grad(0)],
             [
                 expand_grad(1),
-                work(product_last, state["up far"][2], shrink_role),
-                work(product_last, state["up near"][2], shrink_role),
+                work(product_last, state["up far"][3], shrink_role),
+                work(product_last, state["up near"][3], shrink_role),
             ],
         ),
     )
@@ -631,15 +728,6 @@
     up_summed = lax.psum_scatter(up_grad, "dp", scatter_dimension=0, tiled=True)
 
     shrink_summed = wait(shrink_summed)
-
-    def shrink_update(gradient, *values):
-        gradient = gradient[None].astype(F32)
-        return gradient, *adamw(values[0], gradient, *values[1:], RATE, DECAY)
-
-    def shrink_work():
-        state["shrink"] = step(
-            shrink_update, state["shrink back"], shrink_weight, shrink_moment, shrink_square
-        )
 
     def expand_update(gate, up, weight, moment, square):
         gradient = jnp.stack([gate, up]).astype(F32)
@@ -655,7 +743,7 @@
         back_two, middle, scale_two, gain_two, grad_out, *parts
     )
 
-    def attend_back(name, grads, blocks, places, earlier):
+    def attend_back(name, grads, blocks, earlier):
         normed, joint, attended = state["attend " + name]
         return step(
             attend_back_blocks,
@@ -667,7 +755,6 @@
             attended,
             normed,
             state["turn " + name],
-            places,
             earlier,
         )
 
@@ -680,28 +767,32 @@
         if k == 0:
             return [(far_output, 1)]
         if k == 1:
+            state["came"] = came[0][0]
             return []
-        state["sums"] = step(add_low, near_output, came[0][0])
         across = state["sums"][3 * rows :]
         return [(across[: rows // 2], 2), (across[rows // 2 :], 4)]
 
     def back_near(near_branch):
-        state["near back"] = attend_back("near", near_branch, spread_tokens, near_places, [])
+        state["near back"] = attend_back("near", near_branch, spread_tokens, [])
 
     def back_far():
         state["far back"] = attend_back(
-            "far", far_branch, far_tokens, far_places, state["near back"][1:]
+            "far", far_branch, far_tokens, state["near back"][1:]
         )
 
     _, far_branch, came, _ = plan.spread(
         branch_low,
         None,
-        ([], [], [back_near]),
+        (
+            [],
+            [lambda: state.update(sums=step(add_low, near_output, state["came"]))] * plan.short,
+            [back_near],
+        ),
         extra_output,
     )
     gate_summed = wait(gate_summed)
     if plan.short:
-        beside, above = step(functools.partial(plan.merge, rows), state["sums"], *came[2])
+        beside, above = step(functools.partial(plan.merge, rows), state["sums"], *came[3])
         parts, _ = window([(beside, 2), (above, 4)], back_far)
         parts = [state["sums"][:rows], *parts]
     else:
@@ -712,17 +803,8 @@
     near, far = state["near back"][0], state["far back"][0]
     up_summed = wait(up_summed)
 
-    def lower_sums():
-        _, entry_grad, mixing_grad, gain_grad = state["far back"]
-        state["entry"], state["mixing"] = step(
-            lambda a, b: (low_of(a), low_of(b.T)), entry_grad, mixing_grad
-        )
-        state["gain"] = step(order_gains, gain_grad, gain_two_grad)
-
-    (got,), _ = window(
-        [(far, 1)], lower_sums, store("shrink back", plan.columns_back, shrink_summed)
-    )
-    entry_grad, mixing_grad, gains = state["entry"], state["mixing"], state["gain"]
+    _, entry_grad, mixing_grad, gain_grad = state["far back"]
+    mixing_grad = step(lambda a: a.T, mixing_grad)
     if whole_heads:
         mixing_summed = lax.psum_scatter(mixing_grad, "dp", scatter_dimension=0, tiled=True)
         entry_gradient = lax.psum_scatter(
@@ -741,19 +823,35 @@
         entry_gradient = lax.psum_scatter(entry_full, AXES, scatter_dimension=1, tiled=True)
         mixing_summed = lax.psum_scatter(mixing_full, AXES, scatter_dimension=0, tiled=True)
 
-    def mixing_update(gradient, *values):
+    gains = step(order_gains, gain_grad, gain_two_grad)
+    (got,), ((shrink_back,),) = window([(far, 1)], work(plan.columns_back, shrink_summed))
+
+    def back_input(inputs, gain, middle_grad, *parts):
+        scale = lax.rsqrt(jnp.mean(inputs * inputs, axis=-1, keepdims=True) + EPS)
+        grad = sum(value.astype(F32) for value in parts)
+        return middle_grad + norm_back(inputs, scale, gain, grad)[0]
+
+    def finish(*parts):
+        state["input"] = step(back_input, inputs, gain_one, middle_grad, *parts)
+
+    def columns_update(shrink_back, mixing_summed, shrink, mixing):
         if whole_heads:
-            gradient = plan.columns_back(gradient)
-        gradient = gradient[None].astype(F32)
-        return gradient, *adamw(values[0], gradient, *values[1:], MIXING_RATE, DECAY)
-
-    parts, _, gains = plan.settle(
+            (mixing_summed,) = plan.columns_back(mixing_summed)
+        found = []
+        for gradient, values, rate in (
+            (shrink_back, shrink, RATE),
+            (mixing_summed, mixing, MIXING_RATE),
+        ):
+            gradient = gradient[None].astype(F32)
+            found.append((gradient, adamw(values[0], gradient, *values[1:], rate, DECAY)))
+        return found
+
+    _, _, gains = plan.settle(
         lambda: near,
         far,
         rows,
         (
             [],
-            [lambda: shrink_work()],
             [
                 store(
                     "expand",
@@ -763,28 +861,24 @@
                     expand_weight,
                     expand_moment,
                     expand_square,
-                ),
+                )
+            ],
+            [
                 store(
-                    "mixing new",
-                    mixing_update,
+                    "columns",
+                    columns_update,
+                    shrink_back,
                     mixing_summed,
-                    mixing_weight,
-                    mixing_moment,
-                    mixing_square,
-                ),
+                    (shrink_weight, shrink_moment, shrink_square),
+                    (mixing_weight, mixing_moment, mixing_square),
+                )
             ],
         ),
         gains,
         got,
-    )
-    mixing_gradient, *mixing_new = state["mixing new"]
-    def back_input(inputs, gain, middle_grad, *parts):
-        scale = lax.rsqrt(jnp.mean(inputs * inputs, axis=-1, keepdims=True) + EPS)
-        grad = sum(value.astype(F32) for value in parts)
-        return middle_grad + norm_back(inputs, scale, gain, grad)[0]
-
-    input_gradient = step(back_input, inputs, gain_one, middle_grad, *parts)
-
+        finish,
+    )
+    input_gradient = state["input"]
     def order_dp(gains):
         return jnp.take(gains[0], jnp.arange(dp) ^ lax.axis_index("dp"), axis=0)
 
@@ -794,7 +888,7 @@
         gains = step(lambda a, b: a[:bit] + b, gains, got)
     gain_grads = gains[0]
     attention_gradient, feedforward_gradient = gain_grads[:1], gain_grads[1:]
-    shrink_gradient, *shrink_new = state["shrink"]
+    (shrink_gradient, shrink_new), (mixing_gradient, mixing_new) = state["columns"]
     expand_gradient, *expand_new = state["expand"]
     entry_gradient = entry_gradient.astype(F32)
     entry_new = adamw(entry_weight, entry_gradient, entry_moment, entry_square, RATE, DECAY)

time: 724 us -> 687 us (0.949)
  Pallas kernels: 83.1 us -> 157 us
  matrix products: 132 us -> 61.5 us
  waiting for transfers between devices: 231 us -> 204 us
  local copies, waits for them, and re-layouts: 95 us -> 79 us
    pallas_call x0 -> x4, Pallas kernels: none -> 74 us  [the longest x2 44.9 us: expand_back_blocks(): pl.pallas_call(functools.partial(expand_back_kernel, tiles), grid=(tiles...]
    dot_general x6 -> x0, matrix products: 51.7 us -> none  [plain_product(): return jnp.dot(left, right, preferred_element_type=jnp.float32)]
    all_to_all x2 -> x0, waiting for transfers between devices: 25.4 us -> none  [columns_back(): lax.all_to_all(blocks.reshape(self.fsdp, rows, self.dp * width), 'fsdp',...]
    dot_general x8 -> x4, matrix products: 45.9 us -> 22.7 us  [contract_last(): lax.dot_general(left, right, (((1,), (1,)), ((), ())), preferred_element_...]
    all_to_all x1 -> x3, waiting for transfers between devices: 14.7 us -> 29.4 us  [exchange(): return lax.all_to_all(blocks, 'fsdp', 0, 0, tiled=True)]
    all_gather x1, waiting for transfers between devices: 21.3 us -> 11 us  [local(): lax.all_gather(shrink_blocks, 'dp', axis=0, tiled=True).reshape(width, -1)]
    all_to_all x1 -> x3, starting transfers between devices: 4.27 us -> 11.5 us  [exchange(): return lax.all_to_all(blocks, 'fsdp', 0, 0, tiled=True)]
    unnamed x211 -> x170, local copies, waits for them, and re-layouts: 21.3 us -> 16.6 us
  transfers between devices with their start and end apart: 69 -> 68, of which waited for: 23 -> 22; matrix products, arithmetic and copies ran while one was open for 41% -> 31% of each run, Pallas kernels for 12% -> 23%
where the time goes in v3:
time: 687 us; the launch traced here: 681 us
  waiting for transfers between devices  204 us (30%)
  Pallas kernels  157 us (23%)
  other arithmetic  84.3 us (12%)
  local copies, waits for them, and re-layouts  79 us (11%)
  matrix products  61.5 us (9%)
  starting transfers between devices  57.9 us (8%)
  blocking collectives  21.1 us (3%)
  between operations  16 us (2%)
    ppermute x56, waiting for transfers between devices, window(): came.append(lax.ppermute(value, axis, pairs))  163 us
    pallas_call x2, Pallas kernels, attend_back_blocks(): pl.pallas_call(functools.partial(attend_back_kernel, group, not earlier),...  56.1 us
    ppermute x56, starting transfers between devices, window(): came.append(lax.ppermute(value, axis, pairs))  45.2 us
    pallas_call x2, Pallas kernels, expand_back_blocks(): pl.pallas_call(functools.partial(expand_back_kernel, tiles), grid=(tiles...  44.9 us
    dot_general x6, matrix products, contract_first(): lax.dot_general(left, right, (((0,), (0,)), ((), ())), preferred_element_...  38.7 us
    all_to_all x3, waiting for transfers between devices, exchange(): return lax.all_to_all(blocks, 'fsdp', 0, 0, tiled=True)  29.4 us
    pallas_call x2, Pallas kernels, expand_blocks(): pl.pallas_call(functools.partial(expand_kernel, group), grid=(units // ti...  29.2 us
    pallas_call x2, Pallas kernels, attend_blocks(): pl.pallas_call(functools.partial(attend_kernel, group), grid=(group,), in...  26.8 us
  transfers between devices with their start and end apart: 68, of which 22 were waited for; matrix products, arithmetic and copies ran while one was open for 31% of the time, Pallas kernels for 23%

profile of v3, /device:TPU:0, one launch (start us, length us, event | category | flops | bytes accessed | tf_op | source)
XLA Modules:
  0.0 681.1 jit_solution(12464270234459433636)
XLA Ops:
  10.5 12.6 %all_gather.18 = bf16[2,4,64]{2,0,1:T(2,128)(2,1)S(1)} all-gather(bf16[2,1,64]{2,0,1:T(2,128)(2,1)S(1)} %copy.100), channel_id=1, replica_groups=mesh['dp'=4,'fsdp'=8] {'dp'}, dimensions={1}, use_global_device_ids=true | all-gather | bytes 1280 | tf_op jit(solution)/shard_map/all_gather | solution.py:596
  35.1 14.7 %all-to-all-done = bf16[8,64,1280]{2,1,0:T(8,128)(2,1)} async-done(((bf16[8,64,1280]{2,1,0:T(8,128)(2,1)}), bf16[8,64,1280]{2,1,0:T(8,128)(2,1)}, u32[]{:S(2)}, u32[]{:S(2)}) %all-to-all-start) | async-done | bytes 1310752 | tf_op jit(solution)/shard_map/all_to_all | solution.py:517
  53.8 17.1 %collective-permute-done.3 = s32[1,256]{1,0:T(1,128)S(1)} collective-permute-done((s32[1,256]{1,0:T(1,128)S(1)}, s32[1,256]{1,0:T(1,128)S(1)}, u32[]{:S(2)}, u32[]{:S(2)}) %collective-permute-start.3) | collective-permute-done | bytes 1056 | tf_op jit(solution)/shard_map/ppermute | solution.py:390
  82.1 8.2 %collective-permute-done.7 = s32[2,256]{1,0:T(2,128)S(1)} collective-permute-done((s32[2,256]{1,0:T(2,128)S(1)}, s32[2,256]{1,0:T(2,128)S(1)}, u32[]{:S(2)}, u32[]{:S(2)}) %collective-permute-start.7) | collective-permute-done | bytes 2080 | tf_op jit(solution)/shard_map/ppermute | solution.py:390
  93.3 8.6 %all-gather = bf16[2,4,512]{1,0,2:T(2,128)(2,1)S(1)} all-gather(bf16[2,4,64]{1,0,2:T(2,128)(2,1)S(1)} %copy.103), channel_id=2, replica_groups=mesh['dp'=4,'fsdp'=8] {'fsdp'}, dimensions={2}, use_global_device_ids=true | all-gather | bytes 9216 | tf_op jit(solution)/shard_map/all_gather | solution.py:599
  115.7 13.6 %shard_map.404 = (bf16[1024,2048]{1,0:T(8,128)(2,1)}, bf16[1024,768]{1,0:T(8,128)(2,1)}, bf16[1024,256]{1,0:T(8,128)(2,1)}) custom-call(bf16[256,2048]{1,0:T(8,128)(2,1)} %collective-permute-done.2.refs_0_.refs_4_, bf16[256,2048]{1,0:T(8,128)(2,1)} %get-tuple-element.627.refs_1_.refs_5_, bf16[256,2048]{1,0:T(8,128)(2,1)} %get-tuple-element.628.refs_2_.refs_6_, ...), custom_call_target="tpu_custom_call" | custom-call | tf_op jit(solution)/shard_map/pallas_call | solution.py:145
  136.5 23.2 %collective-permute-done.10 = bf16[256,2048]{1,0:T(8,128)(2,1)S(1)} collective-permute-done((bf16[256,2048]{1,0:T(8,128)(2,1)S(1)}, bf16[256,2048]{1,0:T(8,128)(2,1)S(1)}, u32[]{:S(2)}, u32[]{:S(2)}) %collective-permute-start.10) | collective-permute-done | bytes 1048608 | tf_op jit(solution)/shard_map/ppermute | solution.py:390
  171.2 13.2 %shard_map.405 = (bf16[1024,2048]{1,0:T(8,128)(2,1)}, bf16[1024,768]{1,0:T(8,128)(2,1)}, bf16[1024,256]{1,0:T(8,128)(2,1)}) custom-call(bf16[256,2048]{1,0:T(8,128)(2,1)} %refs_4_, bf16[256,2048]{1,0:T(8,128)(2,1)} %copy-done.10, bf16[256,2048]{1,0:T(8,128)(2,1)} %copy-done.11, bf16[256,2048]{1,0:T(8,128)(2,1)} %copy-done.34, f32[1,2048]{1,0:T(1,128)} %bitcast.131, ...), custom_call_target="tpu_custom_call" | custom-call | tf_op jit(solution)/shard_map/pallas_call | solution.py:145
  196.9 10.9 %collective-permute-done.14 = bf16[128,2048]{1,0:T(8,128)(2,1)S(1)} collective-permute-done((bf16[128,2048]{1,0:T(8,128)(2,1)S(1)}, bf16[128,2048]{1,0:T(8,128)(2,1)S(1)}, u32[]{:S(2)}, u32[]{:S(2)}) %collective-permute-start.14) | collective-permute-done | bytes 524320 | tf_op jit(solution)/shard_map/ppermute | solution.py:390
  214.2 19.3 %collective-permute-done.19 = bf16[256,2048]{1,0:T(8,128)(2,1)S(1)} collective-permute-done((bf16[256,2048]{1,0:T(8,128)(2,1)S(1)}, bf16[256,2048]{1,0:T(8,128)(2,1)S(1)}, u32[]{:S(2)}, u32[]{:S(2)}) %collective-permute-start.19) | collective-permute-done | bytes 1048608 | tf_op jit(solution)/shard_map/ppermute | solution.py:390
  238.7 21.6 %collective-permute-done.22.refs_1_ = bf16[256,2048]{1,0:T(8,128)(2,1)S(1)} collective-permute-done((bf16[256,2048]{1,0:T(8,128)(2,1)}, bf16[256,2048]{1,0:T(8,128)(2,1)S(1)}, u32[]{:S(2)}, u32[]{:S(2)}) %collective-permute-start.22) | collective-permute-done | bytes 1048608 | tf_op jit(solution)/shard_map/ppermute | solution.py:390
  265.4 12.4 %collective-permute-done.25 = bf16[128,2048]{1,0:T(8,128)(2,1)S(1)} collective-permute-done((bf16[128,2048]{1,0:T(8,128)(2,1)S(1)}, bf16[128,2048]{1,0:T(8,128)(2,1)S(1)}, u32[]{:S(2)}, u32[]{:S(2)}) %collective-permute-start.25) | collective-permute-done | bytes 524320 | tf_op jit(solution)/shard_map/ppermute | solution.py:390
  280.0 14.7 %shard_map.406 = (bf16[1024,2048]{1,0:T(8,128)(2,1)}, f32[1024,1024]{1,0:T(8,128)}, f32[1024,1024]{1,0:T(8,128)}, bf16[1024,1024]{1,0:T(8,128)(2,1)}) custom-call(bf16[256,2048]{1,0:T(8,128)(2,1)} %multiply_convert_fusion.refs_0_, bf16[256,2048]{1,0:T(8,128)(2,1)} %copy-done.27, bf16[256,2048]{1,0:T(8,128)(2,1)} %collective-permute-done.23.refs_2_, ...), custom_call_target="tpu_custom_call" | custom-call | tf_op jit(solution)/shard_map/pallas_call | solution.py:293
  298.8 14.4 %shard_map.407 = (bf16[1024,2048]{1,0:T(8,128)(2,1)}, f32[1024,1024]{1,0:T(8,128)}, f32[1024,1024]{1,0:T(8,128)}, bf16[1024,1024]{1,0:T(8,128)(2,1)}) custom-call(bf16[256,2048]{1,0:T(8,128)(2,1)} %collective-permute-done.24.refs_0_, bf16[256,2048]{1,0:T(8,128)(2,1)} %get-tuple-element.508.refs_1_, bf16[256,2048]{1,0:T(8,128)(2,1)} %get-tuple-element.509.refs_2_, ...), custom_call_target="tpu_custom_call" | custom-call | tf_op jit(solution)/shard_map/pallas_call | solution.py:293
  325.9 11.0 %all-gather.12.cloned.1.call-done = bf16[32,64,1024]{2,1,0:T(8,128)(2,1)} async-done(((bf16[8,64,1024]{2,1,0:T(8,128)(2,1)}), bf16[32,64,1024]{2,1,0:T(8,128)(2,1)}) %all-gather.12.cloned.1.call-update) | async-done | bytes 4194320 | tf_op jit(solution)/shard_map/all_gather | solution.py:636
  336.9 22.8 %shard_map.408 = (bf16[1024,1024]{1,0:T(8,128)(2,1)}, bf16[1024,1024]{1,0:T(8,128)(2,1)}, bf16[1024,2048]{1,0:T(8,128)(2,1)}) custom-call(bf16[1024,2048]{1,0:T(8,128)(2,1)} %copy-done.30, f32[1024,1024]{1,0:T(8,128)} %get-tuple-element.521.gate, f32[1024,1024]{1,0:T(8,128)} %get-tuple-element.522.upward, bf16[2048,1024]{1,0:T(8,128)(2,1)} %bitcast.100, ...), custom_call_target="tpu_custom_call" | custom-call | tf_op jit(solution)/shard_map/pallas_call | solution.py:342
  359.7 22.1 %shard_map.409 = (bf16[1024,1024]{1,0:T(8,128)(2,1)}, bf16[1024,1024]{1,0:T(8,128)(2,1)}, bf16[1024,2048]{1,0:T(8,128)(2,1)}) custom-call(bf16[1024,2048]{1,0:T(8,128)(2,1)} %copy-done.28, f32[1024,1024]{1,0:T(8,128)} %get-tuple-element.529.gate, f32[1024,1024]{1,0:T(8,128)} %get-tuple-element.530.upward, bf16[2048,1024]{1,0:T(8,128)(2,1)} %bitcast.101, ...), custom_call_target="tpu_custom_call" | custom-call | tf_op jit(solution)/shard_map/pallas_call | solution.py:342
  397.2 8.5 %add_convert_fusion.3 = bf16[1024,2048]{1,0:T(8,128)(2,1)} fusion(f32[1024,2048]{1,0:T(8,128)} %fusion.35, bf16[1024,1024]{1,0:T(8,128)(2,1)S(1)} %copy-done.73, bf16[1024,2048]{1,0:T(8,128)(2,1)S(1)} %copy-done.67), kind=kOutput, calls=%fused_computation.5 | convolution fusion | flops 4299161600 | bytes 18874368 | tf_op jit(solution)/shard_map/dot_general | solution.py:33
  426.1 9.5 %convolution_convert_fusion.3 = bf16[1024,2048]{1,0:T(8,128)(2,1)} fusion(bf16[1024,1024]{1,0:T(8,128)(2,1)} %get-tuple-element.555, bf16[2048,1024]{1,0:T(8,128)(2,1)} %bitcast.102), kind=kOutput, calls=%fused_computation.16 | convolution fusion | flops 4297064448 | bytes 10485760 | tf_op jit(solution)/shard_map/dot_general | solution.py:27
  451.6 23.1 %collective-permute-done.34.refs_1_ = bf16[256,2048]{1,0:T(8,128)(2,1)S(1)} collective-permute-done((bf16[256,2048]{1,0:T(8,128)(2,1)S(1)}, bf16[256,2048]{1,0:T(8,128)(2,1)S(1)}, u32[]{:S(2)}, u32[]{:S(2)}) %collective-permute-start.34) | collective-permute-done | bytes 1048608 | tf_op jit(solution)/shard_map/ppermute | solution.py:390
  499.2 27.6 %shard_map.410 = (bf16[1024,2048]{1,0:T(8,128)(2,1)}, f32[768,2048]{1,0:T(8,128)}, f32[256,2048]{1,0:T(8,128)}, f32[1,2048]{1,0:T(1,128)}) custom-call(bf16[256,2048]{1,0:T(8,128)(2,1)} %get-tuple-element.591.refs_0_, bf16[256,2048]{1,0:T(8,128)(2,1)} %copy-done.32, bf16[256,2048]{1,0:T(8,128)(2,1)} %copy-done.33, ...), custom_call_target="tpu_custom_call" | custom-call | tf_op jit(solution)/shard_map/pallas_call | solution.py:226
  542.0 28.5 %shard_map.411 = (bf16[1024,2048]{1,0:T(8,128)(2,1)}, bf16[768,2048]{1,0:T(8,128)(2,1)}, bf16[256,2048]{1,0:T(8,128)(2,1)}, f32[1,2048]{1,0:T(1,128)}) custom-call(bf16[256,2048]{1,0:T(8,128)(2,1)} %copy-done.49, bf16[256,2048]{1,0:T(8,128)(2,1)} %get-tuple-element.623.refs_1_, bf16[256,2048]{1,0:T(8,128)(2,1)} %get-tuple-element.624.refs_2_, ...), custom_call_target="tpu_custom_call" | custom-call | tf_op jit(solution)/shard_map/pallas_call | solution.py:226
  580.2 14.7 %all-to-all-done.1 = bf16[8,64,1024]{2,1,0:T(8,128)(2,1)S(1)} async-done(((bf16[8,64,1024]{2,1,0:T(8,128)(2,1)}), bf16[8,64,1024]{2,1,0:T(8,128)(2,1)S(1)}, u32[]{:S(2)}, u32[]{:S(2)}) %all-to-all-start.1) | async-done | bytes 1048608 | tf_op jit(solution)/shard_map/all_to_all | solution.py:517
  644.4 10.3 %collective-permute-done.52 = f32[2,4,2,64]{3,1,2,0:T(4,128)S(1)} collective-permute-done((f32[2,4,2,64]{3,1,2,0:T(4,128)S(1)}, f32[2,4,2,64]{3,1,2,0:T(4,128)S(1)}, u32[]{:S(2)}, u32[]{:S(2)}) %collective-permute-start.52) | collective-permute-done | bytes 4128 | tf_op jit(solution)/shard_map/ppermute | solution.py:390
  (464 shorter events, 282.5 us)
Async XLA Ops:
  7.2 99.6 %all-gather.6.cloned.1.call-start = ((), (), s32[]{:S(2)}) async-start(), calls=%async_computation.8 | async-start | bytes 3932160 | tf_op jit(solution)/shard_map/all_gather | solution.py:589
  31.1 98.3 %all-gather.8.cloned.1.call-start = ((), (), s32[]{:S(2)}) async-start(), calls=%async_computation.9 | async-start | bytes 1310720 | tf_op jit(solution)/shard_map/all_gather | solution.py:631
  31.1 39.7 %collective-permute-start = (bf16[256,2048]{1,0:T(8,128)(2,1)S(1)}, bf16[256,2048]{1,0:T(8,128)(2,1)S(1)}, u32[]{:S(2)}, u32[]{:S(2)}) collective-permute-start(bf16[256,2048]{1,0:T(8,128)(2,1)S(1)} %copy-done.18), channel_id=1, source_target_pairs={{0,2},{1,3},{2,0},{3,1},{4,6},{5,7},{6,4},{7,5},{8,10},{9,11},{10,... | collective-permute-start | bytes 3145736 | tf_op jit(solution)/shard_map/ppermute | solution.py:390
  33.0 37.8 %collective-permute-start.1 = (bf16[256,2048]{1,0:T(8,128)(2,1)S(1)}, bf16[256,2048]{1,0:T(8,128)(2,1)S(1)}, u32[]{:S(2)}, u32[]{:S(2)}) collective-permute-start(bf16[256,2048]{1,0:T(8,128)(2,1)S(1)} %copy-done.18), channel_id=1, source_target_pairs={{0,4},{1,5},{2,6},{3,7},{4,0},{5,1},{6,2},{7,3},{8,12},{9,13},{10,... | collective-permute-start | bytes 3145736 | tf_op jit(solution)/shard_map/ppermute | solution.py:390
  34.5 36.3 %collective-permute-start.2 = (bf16[256,2048]{1,0:T(8,128)(2,1)S(1)}, bf16[256,2048]{1,0:T(8,128)(2,1)}, u32[]{:S(2)}, u32[]{:S(2)}) collective-permute-start(bf16[256,2048]{1,0:T(8,128)(2,1)S(1)} %copy-done.18), channel_id=1, source_target_pairs={{0,1},{1,0},{2,3},{3,2},{4,5},{5,4},{6,7},{7,6},{8,9},{9,8},{10,11... | collective-permute-start | bytes 3145736 | tf_op jit(solution)/shard_map/ppermute | solution.py:390
  34.5 36.3 %collective-permute-start.3 = (s32[1,256]{1,0:T(1,128)S(1)}, s32[1,256]{1,0:T(1,128)S(1)}, u32[]{:S(2)}, u32[]{:S(2)}) collective-permute-start(s32[1,256]{1,0:T(1,128)S(1)} %bitcast.143), channel_id=1, source_target_pairs={{0,2},{1,3},{2,0},{3,1},{4,6},{5,7},{6,4},{7,5},{8,10},{9,11},{10,... | collective-permute-start | bytes 3080 | tf_op jit(solution)/shard_map/ppermute | solution.py:390
  78.2 200.7 %all-gather.10.cloned.1.call-start = ((), (), s32[]{:S(2)}) async-start(), calls=%async_computation.10 | async-start | bytes 10485760 | tf_op jit(solution)/shard_map/all_gather | solution.py:635
  103.0 233.9 %all-gather.12.cloned.1.call-start = ((), (), s32[]{:S(2)}) async-start(), calls=%async_computation.11 | async-start | bytes 5242880 | tf_op jit(solution)/shard_map/all_gather | solution.py:636
  134.2 54.9 %collective-permute-start.13 = (bf16[1024,2048]{1,0:T(8,128)(2,1)}, bf16[1024,2048]{1,0:T(8,128)(2,1)}, u32[]{:S(2)}, u32[]{:S(2)}) collective-permute-start(bf16[1024,2048]{1,0:T(8,128)(2,1)} %convolution_convert_fusion.1), channel_id=1, source_target_pairs={{0,1},{1,0},{2,3},{3,2},{4,5},{5,4},{6,7},{7,6},{8,9},{9,8},{10,11... | collective-permute-start | bytes 12582920 | tf_op jit(solution)/shard_map/ppermute | solution.py:390
  238.7 203.1 %reduce-scatter.6.cloned.1.call-start = ((), (), s32[]{:S(2)}) async-start(), calls=%async_computation.12 | async-start | bytes 5242880 | tf_op jit(solution)/shard_map/reduce_scatter | solution.py:689
  325.8 201.0 %reduce-scatter.8.cloned.1.call-start = ((), (), s32[]{:S(2)}) async-start(), calls=%async_computation.13 | async-start | bytes 5242880 | tf_op jit(solution)/shard_map/reduce_scatter | solution.py:727
  407.0 166.7 %reduce-scatter.10.cloned.1.call-start = ((), (), s32[]{:S(2)}) async-start(), calls=%async_computation.14 | async-start | bytes 5242880 | tf_op jit(solution)/shard_map/reduce_scatter | solution.py:728
  413.1 28.6 %collective-permute-start.32 = (bf16[256,2048]{1,0:T(8,128)(2,1)}, bf16[256,2048]{1,0:T(8,128)(2,1)}, u32[]{:S(2)}, u32[]{:S(2)}) collective-permute-start(bf16[256,2048]{1,0:T(8,128)(2,1)} %pad_maximum_fusion.3), channel_id=1, source_target_pairs={{0,2},{1,3},{2,0},{3,1},{4,6},{5,7},{6,4},{7,5},{8,10},{9,11},{10,... | collective-permute-start | bytes 3145736 | tf_op jit(solution)/shard_map/ppermute | solution.py:390
  413.8 27.9 %collective-permute-start.33 = (bf16[256,2048]{1,0:T(8,128)(2,1)}, bf16[256,2048]{1,0:T(8,128)(2,1)}, u32[]{:S(2)}, u32[]{:S(2)}) collective-permute-start(bf16[256,2048]{1,0:T(8,128)(2,1)} %pad_maximum_fusion.4), channel_id=1, source_target_pairs={{0,4},{1,5},{2,6},{3,7},{4,0},{5,1},{6,2},{7,3},{8,12},{9,13},{10,... | collective-permute-start | bytes 3145736 | tf_op jit(solution)/shard_map/ppermute | solution.py:390
  448.5 27.6 %collective-permute-start.37 = (bf16[1024,2048]{1,0:T(8,128)(2,1)}, bf16[1024,2048]{1,0:T(8,128)(2,1)}, u32[]{:S(2)}, u32[]{:S(2)}) collective-permute-start(bf16[1024,2048]{1,0:T(8,128)(2,1)} %convolution_convert_fusion.3), channel_id=1, source_target_pairs={{0,1},{1,0},{2,3},{3,2},{4,5},{5,4},{6,7},{7,6},{8,9},{9,8},{10,11... | collective-permute-start | bytes 12582920 | tf_op jit(solution)/shard_map/ppermute | solution.py:390
  448.5 172.2 %reduce-scatter.12.cloned.1.call-start = ((), (), s32[]{:S(2)}) async-start(), calls=%async_computation.15 | async-start | bytes 1310720 | tf_op jit(solution)/shard_map/reduce_scatter | solution.py:809
  493.8 33.0 %collective-permute-start.41 = (bf16[256,2048]{1,0:T(8,128)(2,1)}, bf16[256,2048]{1,0:T(8,128)(2,1)}, u32[]{:S(2)}, u32[]{:S(2)}) collective-permute-start(bf16[256,2048]{1,0:T(8,128)(2,1)} %constant_dynamic-update-slice_fusion.22.refs_3_), channel_id=1, source_target_pairs={{0,1},{1,0},{2,3},{3,2},{4,5},{5,4},{6,7},{7,6},{8,9},{9,8},{10,11... | collective-permute-start | bytes 3145736 | tf_op jit(solution)/shard_map/ppermute | solution.py:390
  493.8 33.0 %collective-permute-start.42 = (bf16[128,2048]{1,0:T(8,128)(2,1)}, bf16[128,2048]{1,0:T(8,128)(2,1)}, u32[]{:S(2)}, u32[]{:S(2)}) collective-permute-start(bf16[128,2048]{1,0:T(8,128)(2,1)} %get-tuple-element.589), channel_id=1, source_target_pairs={{0,2},{1,3},{2,0},{3,1},{4,6},{5,7},{6,4},{7,5},{8,10},{9,11},{10,... | collective-permute-start | bytes 1572872 | tf_op jit(solution)/shard_map/ppermute | solution.py:390
  494.4 32.4 %collective-permute-start.43 = (bf16[128,2048]{1,0:T(8,128)(2,1)}, bf16[128,2048]{1,0:T(8,128)(2,1)}, u32[]{:S(2)}, u32[]{:S(2)}) collective-permute-start(bf16[128,2048]{1,0:T(8,128)(2,1)} %get-tuple-element.590), channel_id=1, source_target_pairs={{0,4},{1,5},{2,6},{3,7},{4,0},{5,1},{6,2},{7,3},{8,12},{9,13},{10,... | collective-permute-start | bytes 1572872 | tf_op jit(solution)/shard_map/ppermute | solution.py:390
  532.2 38.3 %collective-permute-start.44 = (bf16[256,2048]{1,0:T(8,128)(2,1)}, bf16[256,2048]{1,0:T(8,128)(2,1)}, u32[]{:S(2)}, u32[]{:S(2)}) collective-permute-start(bf16[256,2048]{1,0:T(8,128)(2,1)} %pad_maximum_fusion.5), channel_id=1, source_target_pairs={{0,2},{1,3},{2,0},{3,1},{4,6},{5,7},{6,4},{7,5},{8,10},{9,11},{10,... | collective-permute-start | bytes 3145736 | tf_op jit(solution)/shard_map/ppermute | solution.py:390
  533.3 37.3 %collective-permute-start.45 = (bf16[256,2048]{1,0:T(8,128)(2,1)}, bf16[256,2048]{1,0:T(8,128)(2,1)}, u32[]{:S(2)}, u32[]{:S(2)}) collective-permute-start(bf16[256,2048]{1,0:T(8,128)(2,1)} %pad_maximum_fusion.6), channel_id=1, source_target_pairs={{0,4},{1,5},{2,6},{3,7},{4,0},{5,1},{6,2},{7,3},{8,12},{9,13},{10,... | collective-permute-start | bytes 3145736 | tf_op jit(solution)/shard_map/ppermute | solution.py:390
  579.4 88.7 %reduce-scatter.14.cloned.1.call-start = ((), (), s32[]{:S(2)}) async-start(), calls=%async_computation.16 | async-start | bytes 3932160 | tf_op jit(solution)/shard_map/reduce_scatter | solution.py:810
  626.2 28.6 %collective-permute-start.50 = (bf16[256,2048]{1,0:T(8,128)(2,1)}, bf16[256,2048]{1,0:T(8,128)(2,1)S(1)}, u32[]{:S(2)}, u32[]{:S(2)}) collective-permute-start(bf16[256,2048]{1,0:T(8,128)(2,1)} %pad_maximum_fusion.7), channel_id=1, source_target_pairs={{0,2},{1,3},{2,0},{3,1},{4,6},{5,7},{6,4},{7,5},{8,10},{9,11},{10,... | collective-permute-start | bytes 3145736 | tf_op jit(solution)/shard_map/ppermute | solution.py:390
  628.2 26.6 %collective-permute-start.51 = (bf16[256,2048]{1,0:T(8,128)(2,1)}, bf16[256,2048]{1,0:T(8,128)(2,1)}, u32[]{:S(2)}, u32[]{:S(2)}) collective-permute-start(bf16[256,2048]{1,0:T(8,128)(2,1)} %pad_maximum_fusion.8), channel_id=1, source_target_pairs={{0,4},{1,5},{2,6},{3,7},{4,0},{5,1},{6,2},{7,3},{8,12},{9,13},{10,... | collective-permute-start | bytes 3145736 | tf_op jit(solution)/shard_map/ppermute | solution.py:390
  (121 other events, 1360.7 us)
Sparse Core Ops, SparseCore 0:
  10.2 66.1 all-gather.5
  78.6 26.5 all-gather.7
  107.3 149.1 all-gather.9
  257.9 78.9 all-gather.11
  339.1 75.2 reduce-scatter.5
  416.6 77.2 reduce-scatter.7
  496.2 77.2 reduce-scatter.9
  576.0 27.6 reduce-scatter.11
  605.9 58.8 reduce-scatter.13

commit v4 on v3

--- a/solution.py
+++ b/solution.py
@@ -136,10 +136,9 @@
     attended[...] = own_columns(found, rows).astype(BF16)
 
 
-def attend_blocks(blocks, gain, weight, cosine, sine, down, across):
+def attend_blocks(span, blocks, gain, weight, cosine, sine, down, across):
     group = len(blocks)
     rows, width = blocks[0].shape
-    span = weight.shape[0] // 3
     whole = lambda *shape: pl.BlockSpec(shape, lambda i: (0,) * len(shape))
     by_row = lambda columns: pl.BlockSpec((rows, columns), lambda i: (i, 0))
     return pl.pallas_call(
@@ -216,10 +215,9 @@
         mixing_sum[...] = mixing_total[...].astype(mixing_sum.dtype)
 
 
-def attend_back_blocks(grads, blocks, mixing, weight, joint, attended, normed, turn, earlier):
+def attend_back_blocks(span, grads, blocks, mixing, weight, joint, attended, normed, turn, earlier):
     group = len(blocks)
     rows, width = blocks[0].shape
-    span = weight.shape[0] // 3
     whole = lambda *shape: pl.BlockSpec(shape, lambda i: (0,) * len(shape))
     by_row = lambda columns: pl.BlockSpec((rows, columns), lambda i: (i, 0))
     sums = [(3 * span, width), (span, width), (1, width)]
@@ -269,6 +267,24 @@
     )
 
 
+def split_kernel(fsdp, rows_held, blocks):
+    width = blocks.shape[2] // HEAD
+    for role in range(fsdp):
+        for k in range(width):
+            first = (k * fsdp + role) * HEAD
+            blocks[role, :, k * HEAD : (k + 1) * HEAD] = rows_held[:, first : first + HEAD]
+
+
+def split_heads(weight, dp, fsdp, span):
+    return pl.pallas_call(
+        functools.partial(split_kernel, fsdp),
+        grid=(1,),
+        in_specs=[pl.BlockSpec((span, weight.shape[1]), lambda i: (3, 0))],
+        out_specs=pl.BlockSpec((fsdp, span, dp * HEAD), lambda i: (0, 0, 0)),
+        out_shape=jax.ShapeDtypeStruct((fsdp, span, dp * HEAD), BF16),
+    )(weight)
+
+
 def expand_kernel(group, *refs):
     blocks, weight, joined, gate, upward, hidden = refs[:group], *refs[group:]
     rows = blocks[0].shape[0]
@@ -306,7 +322,59 @@
     )(*blocks, weight)
 
 
-def expand_back_kernel(tiles, grads, gate, upward, shrink, weight, gate_grad, up_grad, terms, both):
+def pairs_kernel(left, right, left_other, right_other, out):
+    total = contract_first(left[...], right[...])
+    total += contract_first(left_other[...], right_other[...])
+    out[...] = total.astype(BF16)
+
+
+def product_pairs(left, right, left_other, right_other):
+    rows, units = left.shape
+    width = right.shape[1]
+    tile = min(units, 256)
+    whole = pl.BlockSpec((rows, width), lambda j: (0, 0))
+    part = pl.BlockSpec((rows, tile), lambda j: (0, j))
+    return pl.pallas_call(
+        pairs_kernel,
+        grid=(units // tile,),
+        in_specs=[part, whole, part, whole],
+        out_specs=pl.BlockSpec((tile, width), lambda j: (j, 0)),
+        out_shape=jax.ShapeDtypeStruct((units, width), BF16),
+        compiler_params=pltpu.CompilerParams(vmem_limit_bytes=VMEM_BYTES),
+    )(left, right, left_other, right_other)
+
+
+def output_kernel(hidden, shrink, head, tail):
+    total = contract_last(hidden[...], shrink[...]).astype(BF16)
+    head[...] = total[: head.shape[0]]
+    tail[...] = total[head.shape[0] :]
+
+
+def output_blocks(cut, hidden, shrink):
+    rows, units = hidden.shape
+    width = shrink.shape[0]
+    cuts = 4
+    return pl.pallas_call(
+        output_kernel,
+        grid=(cuts,),
+        in_specs=[
+            pl.BlockSpec((rows, units), lambda j: (0, 0)),
+            pl.BlockSpec((width // cuts, units), lambda j: (j, 0)),
+        ],
+        out_specs=[
+            pl.BlockSpec((cut, width // cuts), lambda j: (0, j)),
+            pl.BlockSpec((rows - cut, width // cuts), lambda j: (0, j)),
+        ],
+        out_shape=[
+            jax.ShapeDtypeStruct((cut, width), BF16),
+            jax.ShapeDtypeStruct((rows - cut, width), BF16),
+        ],
+        compiler_params=pltpu.CompilerParams(vmem_limit_bytes=VMEM_BYTES),
+    )(hidden, shrink)
+
+
+def expand_back_kernel(tiles, *refs):
+    grads, gate, upward, shrink, weight, gate_grad, up_grad, head, tail, both = refs
     step = pl.program_id(0)
     tile = gate.shape[1]
 
@@ -323,14 +391,15 @@
 
     @pl.when(step >= tiles)
     def _():
-        total = jnp.zeros(terms.shape, F32)
+        total = jnp.zeros((grads.shape[0], head.shape[1]), F32)
         for k in range(2 * tiles):
             part, first = k // tiles, k % tiles * tile
             total += plain_product(both[k], weight[part, first : first + tile, :])
-        terms[...] = total.astype(BF16)
-
-
-def expand_back_blocks(grads, gate, upward, shrink, weight):
+        head[...] = total[: head.shape[0]].astype(BF16)
+        tail[...] = total[head.shape[0] :].astype(BF16)
+
+
+def expand_back_blocks(cut, grads, gate, upward, shrink, weight):
     rows, width = grads.shape
     units = gate.shape[1]
     tile = min(units, 256)
@@ -352,12 +421,14 @@
         out_specs=[
             by_unit,
             by_unit,
-            pl.BlockSpec((rows, width // cuts), lambda j: (0, late(j))),
+            pl.BlockSpec((cut, width // cuts), lambda j: (0, late(j))),
+            pl.BlockSpec((rows - cut, width // cuts), lambda j: (0, late(j))),
         ],
         out_shape=[
             jax.ShapeDtypeStruct((rows, units), BF16),
             jax.ShapeDtypeStruct((rows, units), BF16),
-            jax.ShapeDtypeStruct((rows, width), BF16),
+            jax.ShapeDtypeStruct((cut, width), BF16),
+            jax.ShapeDtypeStruct((rows - cut, width), BF16),
         ],
         scratch_shapes=[pltpu.VMEM((2 * tiles, rows, tile), BF16)],
         compiler_params=pltpu.CompilerParams(vmem_limit_bytes=VMEM_BYTES),
@@ -407,7 +478,7 @@
             jnp.concatenate([add_low(above[:half], first), above[half:]]),
         )
 
-    def spread(self, block, marks=None, works=((), (), ()), extra=None):
+    def spread(self, block, marks=None, works=((), (), ()), extra=None, pause=None):
         small = marks is not None
         gave, more = [], []
 
@@ -421,13 +492,16 @@
             )
             gave += found
             more.append(got)
+            if pause is not None:
+                pause()
             if small:
                 marks = self.step(lambda a, b: jnp.concatenate([a, b]), marks, *got)
             upper, lower, pair = self.step(
                 lambda a, b: (a[:half], b[half:], jnp.concatenate([b, a])), above, beside
             )
             (first, second, pair, *got), found = self.window(
-                [(upper, 2), (lower, 4), (pair, 1)] + [(marks, 4)] * small + added(1), *works[1]
+                [(upper, 2), (lower, 4), (pair, 1)] + [(marks, 4)] * small + added(1),
+                *[functools.partial(w, [block, beside, above, other]) for w in works[1]],
             )
             gave += found
             more.append(got)
@@ -449,7 +523,7 @@
             if small:
                 marks = jnp.concatenate([marks, got[-1]])
             near = near + got[: len(near)]
-        for work in [*works[0], *works[1]]:
+        for work in [*works[0], *([pause] if pause else []), *works[1]]:
             gave.append(work())
         got, found = self.window(
             [(piece, 1) for piece in near] + [(marks, 1)] * small,
@@ -506,6 +580,24 @@
             (more,), _ = self.window(sends(1), lambda: finish(sums[:rows], beside, above))
             small = sum_small([more], 1)
         return (sums[:rows], beside, above), gave + found, small
+
+    def sum_pair(self, rows, near, across, got):
+        return add_low(near[rows:], got[: 2 * rows]), add_low(across, got[2 * rows :])
+
+    def merge_pair(self, rows, pair, first, second):
+        return self.merge(rows, jnp.concatenate([pair[:rows], pair]), first, second)
+
+    def settle_mixed(self, first, across, others, rows, works):
+        half = rows // 2
+        (got,), ((near, other), *gave) = self.window([(others, 1)], first, *works[0])
+        pair, across = self.step(functools.partial(self.sum_pair, rows), near, across, got)
+        (upper, lower, own), found = self.window(
+            [(across[:half], 2), (across[half:], 4), (other, 1)], *works[1]
+        )
+        gave += found
+        beside, above = self.step(functools.partial(self.merge_pair, rows), pair, upper, lower)
+        (beside, above), found = self.window([(beside, 2), (above, 4)], *works[2])
+        return (near[:rows], own, beside, above), gave + found
 
     def columns_split(self, shard):
         rows, columns = shard.shape
@@ -580,150 +672,175 @@
     product_last = lambda a, b: contract_last(a, b).astype(BF16)
     product_plain = lambda a, b: plain_product(a, b).astype(BF16)
 
-    def product_pairs(a, b, c, d):
-        return (contract_first(a, b) + contract_first(c, d)).astype(BF16)
-
-    entry_low = step(low_of, entry_weight)
+    attention_low = step(
+        lambda a, b: jnp.concatenate([a, b]).astype(BF16), entry_weight, mixing_weight
+    )
     role = lax.axis_index("fsdp")
     if whole_heads:
-        entry_role = lax.all_gather(entry_low, "dp", axis=1, tiled=True)
+        attention_all = lax.all_gather(attention_low, "dp", axis=1, tiled=True)
     else:
-        entry_all = lax.all_gather(entry_low, AXES, axis=1, tiled=True)
-        entry_role = lax.dynamic_slice_in_dim(entry_all, role * span, span, axis=1)
+        attention_all = lax.all_gather(attention_low, AXES, axis=1, tiled=True)
 
     def gains_dp(*gains):
         gains = jnp.concatenate(gains).astype(BF16)[:, None]
         return lax.all_gather(gains, "dp", axis=1, tiled=True)
 
     def gains_fsdp(gains):
-        gains = lax.all_gather(gains[:, :, None], "fsdp", axis=2, tiled=True)
-        return gains.reshape(2, width).astype(F32)
-
-    def columns_work(shrink_low, mixing_low):
-        blocks = plan.exchange(
-            jnp.concatenate([plan.columns_split(shrink_low), plan.columns_split(mixing_low)], -1)
-        )
-        size = shrink_low.shape[1] // fsdp
-        return blocks[..., :size], blocks[..., size:]
+        return lax.all_gather(gains[:, :, None], "fsdp", axis=2, tiled=True)
+
+    def columns_work(rows_held):
+        return plan.exchange(plan.columns_split(rows_held))
 
     spread_tokens, far_tokens, (near_places, far_places), _ = plan.spread(
         tokens,
         positions[None],
         (
             [
-                store("mixing_low", low_of, mixing_weight[0]),
-                store("shrink_low", low_of, shrink_weight[0]),
                 store("gains_dp", gains_dp, attention_gain, feedforward_gain),
-                lambda: state.update(
-                    columns=step(columns_work, state["shrink_low"], state["mixing_low"])
-                ),
+                store("expand_low", low_of, expand_weight),
             ],
-            [
-                store("expand_low", low_of, expand_weight),
-                lambda: state.update(gains=step(gains_fsdp, state["gains_dp"])),
-            ],
+            [lambda *_: state.update(gains=step(gains_fsdp, state["gains_dp"]))],
             [],
         ),
     )
-    gain_one, gain_two = state["gains"][0], state["gains"][1]
-    shrink_blocks, mixing_blocks = state["columns"]
-    if whole_heads:
-        mixing_role = lax.all_gather(mixing_blocks, "dp", axis=0, tiled=True).reshape(width, span)
-    else:
-        mixing_all = lax.all_gather(state["mixing_low"], AXES, axis=0, tiled=True)
-        mixing_role = lax.dynamic_slice_in_dim(mixing_all, role * span, span, axis=1)
+    gains = state["gains"].reshape(2, width).astype(F32)
+    gain_one, gain_two = gains[0], gains[1]
     expand_role = lax.all_gather(state["expand_low"], "dp", axis=1, tiled=True)
-    shrink_role = lax.all_gather(shrink_blocks, "dp", axis=0, tiled=True).reshape(width, -1)
 
     inputs = tokens.astype(F32)
     live = (positions >= 0).astype(F32)[:, None]
     grad_out = cotangent.astype(F32) * live
     grad_low = step(low_of, grad_out)
-    entry_role = wait(entry_role).reshape(3 * span, width)
     state["turn near"] = step(lambda a: turn_tables(a, heads), near_places)
     state["turn far"] = step(lambda a: turn_tables(a, heads), far_places)
 
     def attend_work(name, blocks):
         def run(*_):
             state["attend " + name] = step(
-                attend_blocks, blocks, gain_one, entry_role, *state["turn " + name]
+                functools.partial(attend_blocks, span),
+                blocks,
+                gain_one,
+                state["entry"],
+                *state["turn " + name],
             )
 
         return run
+
+    def attention_weights():
+        found = wait(attention_all)
+        if whole_heads:
+            state["entry"] = found.reshape(4 * span, width)
+            (held,) = plan.tie([split_heads(state["entry"], dp, fsdp, span)])
+            mixing_role = plan.exchange(held).reshape(fsdp, dp, HEAD, span)
+            state["mixing"] = mixing_role.transpose(1, 0, 2, 3).reshape(width, span)
+        else:
+            own = lax.dynamic_slice_in_dim(found[:3], role * span, span, axis=1)
+            state["entry"] = own.reshape(3 * span, width)
+            state["mixing"] = lax.dynamic_slice_in_dim(found[3], role * span, span, axis=1)
+        attend_work("far", far_tokens)()
 
     near_grad, far_grad, _, _ = plan.spread(
         grad_low,
         None,
+        ([], [attend_work("near", spread_tokens)], []),
+        pause=attention_weights,
+    )
+    mixing_role = wait(state["mixing"])
+    entry_role = state["entry"]
+    far = step(product_last, state["attend far"][2], mixing_role)
+    near = work(product_last, state["attend near"][2], mixing_role)
+    shrink_low = step(low_of, shrink_weight[0])
+    parts, (shrink_blocks, *_), _ = plan.settle(
+        near,
+        far,
+        rows,
         (
-            [attend_work("far", far_tokens)],
-            [
-                attend_work("near", spread_tokens),
-            ],
+            [work(columns_work, shrink_low)],
+            [],
             [],
         ),
     )
-    mixing_role = wait(mixing_role)
-    far = step(product_last, state["attend far"][2], mixing_role)
-    near = work(product_last, state["attend near"][2], mixing_role)
-    parts, _, _ = plan.settle(
-        near, far, rows, ([], [store("grad near", join, *near_grad)], [store("grad far", join, *far_grad)])
-    )
+    shrink_role = lax.all_gather(shrink_blocks, "dp", axis=0, tiled=True).reshape(width, -1)
 
     def norm_middle(inputs, gain, own, beside, above):
         middle = inputs + own.astype(F32) + beside.astype(F32) + above.astype(F32)
         scale = lax.rsqrt(jnp.mean(middle * middle, axis=-1, keepdims=True) + EPS)
         return (middle * scale * gain).astype(BF16), middle, scale
 
+    expand_role = wait(expand_role)
     low_two, middle, scale_two = step(norm_middle, inputs, gain_two, *parts)
 
-    def expand_near(near):
-        state["up near"] = step(expand_blocks, near, expand_role)
-
-    _, far_two, _, _ = plan.spread(
-        low_two, None, ([], [lambda: wait(expand_role)], [expand_near])
-    )
-    state["up far"] = step(expand_blocks, far_two, expand_role)
+    def grouped(near, far):
+        if not plan.short:
+            return near, far
+        return [*near[:3], far[0]], [near[3], *far[1:]]
+
+    first_grad, second_grad = grouped(near_grad, far_grad)
+
+    def expand_first(blocks):
+        state["up first"] = step(expand_blocks, blocks, expand_role)
+
+    near_two, far_two, _, _ = plan.spread(
+        low_two,
+        None,
+        (
+            [store("grad first", join, *first_grad), store("grad second", join, *second_grad)],
+            [expand_first] * plan.short,
+            [expand_first] * (not plan.short),
+        ),
+    )
+    state["up second"] = step(expand_blocks, grouped(near_two, far_two)[1], expand_role)
     shrink_grad = step(
-        product_pairs, state["grad near"], state["up near"][3], state["grad far"], state["up far"][3]
+        product_pairs,
+        state["grad first"],
+        state["up first"][3],
+        state["grad second"],
+        state["up second"][3],
     )
     shrink_summed = lax.psum_scatter(shrink_grad, "dp", scatter_dimension=0, tiled=True)
     shrink_role = wait(shrink_role)
 
-    def expand_back(name):
+    def expand_back(name, cut):
         return step(
-            expand_back_blocks,
+            functools.partial(expand_back_blocks, cut * rows),
             state["grad " + name],
             *state["up " + name][1:3],
             shrink_role,
             expand_role,
         )
 
-    far_back = expand_back("far")
-    far = far_back[2]
-
-    def near_terms():
-        state["back"] = expand_back("near")
-        return state["back"][2]
+    second_back = expand_back("second", 1)
+
+    def first_terms():
+        state["back"] = expand_back("first", 3)
+        return state["back"][2:]
 
     def expand_grad(index):
-        return lambda: step(
-            product_pairs, state["back"][index], state["up near"][0], far_back[index], state["up far"][0]
-        )
-
-    parts, (gate_grad, up_grad, far_output, near_output), _ = plan.settle(
-        near_terms,
-        far,
-        rows,
-        (
-            [],
-            [expand_grad(0)],
-            [
-                expand_grad(1),
-                work(product_last, state["up far"][3], shrink_role),
-                work(product_last, state["up near"][3], shrink_role),
-            ],
-        ),
-    )
+        return lambda *_: step(
+            product_pairs,
+            state["back"][index],
+            state["up first"][0],
+            second_back[index],
+            state["up second"][0],
+        )
+
+    works = ([], [expand_grad(0)], [expand_grad(1)])
+    if plan.short:
+        parts, gave = plan.settle_mixed(first_terms, *second_back[2:], rows, works)
+    else:
+        parts, gave, _ = plan.settle(
+            lambda: join(*first_terms()), join(*second_back[2:]), rows, works
+        )
+    gate_grad, up_grad = gave
+
+    def output_work(name, cut):
+        return store(
+            "out " + name,
+            functools.partial(output_blocks, cut * rows),
+            state["up " + name][3],
+            shrink_role,
+        )
+
     gate_summed = lax.psum_scatter(gate_grad, "dp", scatter_dimension=0, tiled=True)
     up_summed = lax.psum_scatter(up_grad, "dp", scatter_dimension=0, tiled=True)
 
@@ -733,8 +850,8 @@
         gradient = jnp.stack([gate, up]).astype(F32)
         return gradient, *adamw(weight, gradient, moment, square, RATE, DECAY)
 
-    def back_two(middle, scale, gain, grad_out, own, beside, above):
-        grad = own.astype(F32) + beside.astype(F32) + above.astype(F32)
+    def back_two(middle, scale, gain, grad_out, *parts):
+        grad = sum(value.astype(F32) for value in parts)
         middle_back, gain_grad = norm_back(middle, scale, gain, grad)
         middle_grad = grad_out + middle_back
         return middle_grad.astype(BF16), middle_grad, gain_grad
@@ -746,7 +863,7 @@
     def attend_back(name, grads, blocks, earlier):
         normed, joint, attended = state["attend " + name]
         return step(
-            attend_back_blocks,
+            functools.partial(attend_back_blocks, span),
             grads,
             blocks,
             mixing_role,
@@ -765,11 +882,16 @@
 
     def extra_output(k, came):
         if k == 0:
-            return [(far_output, 1)]
+            return []
         if k == 1:
-            state["came"] = came[0][0]
-            return []
-        across = state["sums"][3 * rows :]
+            return [(state["out second"][1], 1), (state["out first"][1], 1)]
+        state["sums"] = step(
+            functools.partial(plan.sum_pair, rows),
+            state["out first"][0],
+            state["out second"][0],
+            came[1][0],
+        )
+        across = state["sums"][1]
         return [(across[: rows // 2], 2), (across[rows // 2 :], 4)]
 
     def back_near(near_branch):
@@ -784,23 +906,30 @@
         branch_low,
         None,
         (
+            [output_work("second", 1), output_work("first", 3)],
             [],
-            [lambda: state.update(sums=step(add_low, near_output, state["came"]))] * plan.short,
             [back_near],
         ),
         extra_output,
     )
-    gate_summed = wait(gate_summed)
     if plan.short:
-        beside, above = step(functools.partial(plan.merge, rows), state["sums"], *came[3])
+        beside, above = step(
+            functools.partial(plan.merge_pair, rows), state["sums"][0], *came[3]
+        )
         parts, _ = window([(beside, 2), (above, 4)], back_far)
-        parts = [state["sums"][:rows], *parts]
+        parts = [state["out first"][0][:rows], came[2][1], *parts]
     else:
-        parts, _, _ = plan.settle(lambda: near_output, far_output, rows, ([], [back_far], []))
+        parts, _, _ = plan.settle(
+            lambda: join(*state["out first"]),
+            join(*state["out second"]),
+            rows,
+            ([], [back_far], []),
+        )
     layer_output = step(
         lambda *a: sum((value.astype(F32) for value in a[1:]), a[0]).astype(BF16), middle, *parts
     )
     near, far = state["near back"][0], state["far back"][0]
+    gate_summed = wait(gate_summed)
     up_summed = wait(up_summed)
 
     _, entry_grad, mixing_grad, gain_grad = state["far back"]

time: 687 us -> 684 us (level)
  Pallas kernels: 157 us -> 217 us
  matrix products: 61.5 us -> 7.74 us
  waiting for transfers between devices: 204 us -> 176 us
  blocking collectives: 21.1 us -> 28.2 us
    pallas_call x0 -> x6, Pallas kernels: none -> 62.7 us  [the longest x3 43.2 us: product_pairs(): pl.pallas_call(pairs_kernel, grid=(units // tile,), in_specs=[part, whole...]
    dot_general x6 -> x0, matrix products: 38.7 us -> none  [contract_first(): lax.dot_general(left, right, (((0,), (0,)), ((), ())), preferred_element_...]
    ppermute x56 -> x58, waiting for transfers between devices: 163 us -> 138 us  [window(): came.append(lax.ppermute(value, axis, pairs))]
    dot_general x4 -> x2, matrix products: 22.7 us -> 7.74 us  [contract_last(): lax.dot_general(left, right, (((1,), (1,)), ((), ())), preferred_element_...]
    all_gather x1, waiting for transfers between devices: 11 us -> 0.02 us  [local(): lax.all_gather(shrink_blocks, 'dp', axis=0, tiled=True).reshape(width, -1)]
    all_gather x1, waiting for transfers between devices: 0.01 us -> 10.9 us  [local(): expand_role = lax.all_gather(state['expand_low'], 'dp', axis=1, tiled=True)]
    all_gather x1, blocking collectives: 8.57 us -> 17 us  [gains_fsdp(): return lax.all_gather(gains[:, :, None], 'fsdp', axis=2, tiled=True)]
    all_to_all x3 -> x4, starting transfers between devices: 11.5 us -> 15.9 us  [exchange(): return lax.all_to_all(blocks, 'fsdp', 0, 0, tiled=True)]
  transfers between devices with their start and end apart: 68 -> 70, of which waited for: 22 -> 26; matrix products, arithmetic and copies ran while one was open for 31% -> 25% of each run, Pallas kernels for 23% -> 32%
where the time goes in v4:
time: 684 us; the launch traced here: 678 us
  Pallas kernels  217 us (32%)
  waiting for transfers between devices  176 us (26%)
  other arithmetic  88.6 us (13%)
  local copies, waits for them, and re-layouts  82.6 us (12%)
  starting transfers between devices  62 us (9%)
  blocking collectives  28.2 us (4%)
  between operations  16 us (2%)
  matrix products  7.74 us (1%)
    ppermute x58, waiting for transfers between devices, window(): came.append(lax.ppermute(value, axis, pairs))  138 us
    pallas_call x2, Pallas kernels, attend_back_blocks(): pl.pallas_call(functools.partial(attend_back_kernel, group, not earlier),...  55.5 us
    ppermute x58, starting transfers between devices, window(): came.append(lax.ppermute(value, axis, pairs))  44.8 us
    pallas_call x2, Pallas kernels, expand_back_blocks(): pl.pallas_call(functools.partial(expand_back_kernel, tiles), grid=(tiles...  44.4 us
    pallas_call x3, Pallas kernels, product_pairs(): pl.pallas_call(pairs_kernel, grid=(units // tile,), in_specs=[part, whole...  43.2 us
    pallas_call x2, Pallas kernels, expand_blocks(): pl.pallas_call(functools.partial(expand_kernel, group), grid=(units // ti...  28.5 us
    all_to_all x4, waiting for transfers between devices, exchange(): return lax.all_to_all(blocks, 'fsdp', 0, 0, tiled=True)  26.6 us
    pallas_call x2, Pallas kernels, attend_blocks(): pl.pallas_call(functools.partial(attend_kernel, group), grid=(group,), in...  25.9 us
  transfers between devices with their start and end apart: 70, of which 26 were waited for; matrix products, arithmetic and copies ran while one was open for 25% of the time, Pallas kernels for 32%

profile of v4, /device:TPU:0, one launch (start us, length us, event | category | flops | bytes accessed | tf_op | source)
XLA Modules:
  0.0 678.0 jit_solution(12396510193888691386)
XLA Ops:
  15.4 11.2 %all_gather.15 = bf16[2,4,64]{2,0,1:T(2,128)(2,1)S(1)} all-gather(bf16[2,1,64]{2,0,1:T(2,128)(2,1)S(1)} %copy.100), channel_id=1, replica_groups=mesh['dp'=4,'fsdp'=8] {'dp'}, dimensions={1}, use_global_device_ids=true | all-gather | bytes 1280 | tf_op jit(solution)/shard_map/all_gather | solution.py:686
  44.4 17.0 %all-gather = bf16[2,4,512]{1,0,2:T(2,128)(2,1)S(1)} all-gather(bf16[2,4,64]{1,0,2:T(2,128)(2,1)S(1)} %copy.101), channel_id=2, replica_groups=mesh['dp'=4,'fsdp'=8] {'fsdp'}, dimensions={2}, use_global_device_ids=true | all-gather | bytes 9216 | tf_op jit(solution)/shard_map/all_gather | solution.py:689
  74.7 23.5 %collective-permute-done.10 = bf16[256,2048]{1,0:T(8,128)(2,1)} collective-permute-done((bf16[256,2048]{1,0:T(8,128)(2,1)S(1)}, bf16[256,2048]{1,0:T(8,128)(2,1)}, u32[]{:S(2)}, u32[]{:S(2)}) %collective-permute-start.10) | collective-permute-done | bytes 1048608 | tf_op jit(solution)/shard_map/ppermute | solution.py:461
  113.4 12.9 %shard_map.404 = (bf16[1024,2048]{1,0:T(8,128)(2,1)}, bf16[1024,768]{1,0:T(8,128)(2,1)}, bf16[1024,256]{1,0:T(8,128)(2,1)}) custom-call(bf16[256,2048]{1,0:T(8,128)(2,1)} %collective-permute-done.2.refs_0_.refs_4_, bf16[256,2048]{1,0:T(8,128)(2,1)} %get-tuple-element.656.refs_1_.refs_5_, bf16[256,2048]{1,0:T(8,128)(2,1)} %get-tuple-element.657.refs_2_.refs_6_, ...), custom_call_target="tpu_custom_call" | custom-call | tf_op jit(solution)/shard_map/pallas_call | solution.py:144
  143.7 12.9 %shard_map.405 = (bf16[1024,2048]{1,0:T(8,128)(2,1)}, bf16[1024,768]{1,0:T(8,128)(2,1)}, bf16[1024,256]{1,0:T(8,128)(2,1)}) custom-call(bf16[256,2048]{1,0:T(8,128)(2,1)} %refs_4_, bf16[256,2048]{1,0:T(8,128)(2,1)} %copy-done.7, bf16[256,2048]{1,0:T(8,128)(2,1)} %copy-done.8, bf16[256,2048]{1,0:T(8,128)(2,1)} %copy-done.22, f32[1,2048]{1,0:T(1,128)} %bitcast.115, ...), custom_call_target="tpu_custom_call" | custom-call | tf_op jit(solution)/shard_map/pallas_call | solution.py:144
  171.1 12.0 %all-to-all-done.1 = bf16[8,64,1024]{2,1,0:T(8,128)(2,1)S(1)} async-done(((bf16[8,64,1024]{2,1,0:T(8,128)(2,1)}), bf16[8,64,1024]{2,1,0:T(8,128)(2,1)S(1)}, u32[]{:S(2)}, u32[]{:S(2)}) %all-to-all-start.1) | async-done | bytes 1048608 | tf_op jit(solution)/shard_map/all_to_all | solution.py:609
  193.6 10.6 %collective-permute-done.14 = bf16[128,2048]{1,0:T(8,128)(2,1)S(1)} collective-permute-done((bf16[128,2048]{1,0:T(8,128)(2,1)S(1)}, bf16[128,2048]{1,0:T(8,128)(2,1)S(1)}, u32[]{:S(2)}, u32[]{:S(2)}) %collective-permute-start.14) | collective-permute-done | bytes 524320 | tf_op jit(solution)/shard_map/ppermute | solution.py:461
  213.7 18.3 %collective-permute-done.16 = bf16[256,2048]{1,0:T(8,128)(2,1)} collective-permute-done((bf16[256,2048]{1,0:T(8,128)(2,1)}, bf16[256,2048]{1,0:T(8,128)(2,1)}, u32[]{:S(2)}, u32[]{:S(2)}) %collective-permute-start.16) | collective-permute-done | bytes 1048608 | tf_op jit(solution)/shard_map/ppermute | solution.py:461
  233.2 10.9 %all-gather.7.cloned.1.call-done.refs_4_ = bf16[2,1024,2048]{2,1,0:T(8,128)(2,1)} async-done(((bf16[2,256,2048]{2,1,0:T(8,128)(2,1)}), bf16[2,1024,2048]{2,1,0:T(8,128)(2,1)}) %all-gather.7.cloned.1.call-update) | async-done | bytes 8388624 | tf_op jit(solution)/shard_map/all_gather | solution.py:708
  260.6 11.7 %collective-permute-done.18.refs_1_ = bf16[256,2048]{1,0:T(8,128)(2,1)S(1)} collective-permute-done((bf16[256,2048]{1,0:T(8,128)(2,1)S(1)}, bf16[256,2048]{1,0:T(8,128)(2,1)S(1)}, u32[]{:S(2)}, u32[]{:S(2)}) %collective-permute-start.18) | collective-permute-done | bytes 1048608 | tf_op jit(solution)/shard_map/ppermute | solution.py:461
  278.4 14.3 %shard_map.407 = (bf16[1024,2048]{1,0:T(8,128)(2,1)}, f32[1024,1024]{1,0:T(8,128)}, f32[1024,1024]{1,0:T(8,128)}, bf16[1024,1024]{1,0:T(8,128)(2,1)}) custom-call(bf16[256,2048]{1,0:T(8,128)(2,1)} %copy-done.33, bf16[256,2048]{1,0:T(8,128)(2,1)} %copy-done.25, bf16[256,2048]{1,0:T(8,128)(2,1)} %copy-done.26, bf16[256,2048]{1,0:T(8,128)(2,1)} %copy-done.51, ...), custom_call_target="tpu_custom_call" | custom-call | tf_op jit(solution)/shard_map/pallas_call | solution.py:309
  296.5 14.3 %shard_map.408 = (bf16[1024,2048]{1,0:T(8,128)(2,1)}, f32[1024,1024]{1,0:T(8,128)}, f32[1024,1024]{1,0:T(8,128)}, bf16[1024,1024]{1,0:T(8,128)(2,1)}) custom-call(bf16[256,2048]{1,0:T(8,128)(2,1)} %copy-done.42, bf16[256,2048]{1,0:T(8,128)(2,1)} %get-tuple-element.524.refs_1_, bf16[256,2048]{1,0:T(8,128)(2,1)} %get-tuple-element.525.refs_2_, ...), custom_call_target="tpu_custom_call" | custom-call | tf_op jit(solution)/shard_map/pallas_call | solution.py:309
  310.7 14.1 %shard_map.409 = bf16[2048,1024]{1,0:T(8,128)(2,1)} custom-call(bf16[1024,2048]{1,0:T(8,128)(2,1)} %copy-done.2, bf16[1024,1024]{1,0:T(8,128)(2,1)} %get-tuple-element.592.right.hidden, bf16[1024,2048]{1,0:T(8,128)(2,1)} %constant_dynamic-update-slice_fusion.12.left_other.refs_0_, bf16[1024,1024]{1,0:T(8,128)(2,1)} %get-tuple-element.588.right_other.hidden), custom_call_target="tpu_custom_call" | custom-call | tf_op jit(solution)/shard_map/pallas_call | solution.py:337
  325.2 22.3 %shard_map.410 = (bf16[1024,1024]{1,0:T(8,128)(2,1)}, bf16[1024,1024]{1,0:T(8,128)(2,1)}, bf16[256,2048]{1,0:T(8,128)(2,1)}, bf16[768,2048]{1,0:T(8,128)(2,1)}) custom-call(bf16[1024,2048]{1,0:T(8,128)(2,1)} %constant_dynamic-update-slice_fusion.12.left_other.refs_0_, f32[1024,1024]{1,0:T(8,128)} %get-tuple-element.537.refs_1_, ...), custom_call_target="tpu_custom_call" | custom-call | tf_op jit(solution)/shard_map/pallas_call | solution.py:411
  347.9 22.1 %shard_map.411 = (bf16[1024,1024]{1,0:T(8,128)(2,1)}, bf16[1024,1024]{1,0:T(8,128)(2,1)}, bf16[768,2048]{1,0:T(8,128)(2,1)}, bf16[256,2048]{1,0:T(8,128)(2,1)}) custom-call(bf16[1024,2048]{1,0:T(8,128)(2,1)} %copy-done.2, f32[1024,1024]{1,0:T(8,128)} %get-tuple-element.546.refs_1_, f32[1024,1024]{1,0:T(8,128)} %get-tuple-element.547.refs_2_, ...), custom_call_target="tpu_custom_call" | custom-call | tf_op jit(solution)/shard_map/pallas_call | solution.py:411
  374.1 14.4 %shard_map.412 = bf16[1024,2048]{1,0:T(8,128)(2,1)} custom-call(bf16[1024,1024]{1,0:T(8,128)(2,1)} %get-tuple-element.562.left, bf16[1024,2048]{1,0:T(8,128)(2,1)} %get-tuple-element.575.right, bf16[1024,1024]{1,0:T(8,128)(2,1)} %get-tuple-element.564.left_other, bf16[1024,2048]{1,0:T(8,128)(2,1)} %get-tuple-element.577.right_other), custom_call_target="tpu_custom_call" | custom-call | tf_op jit(solution)/shard_map/pallas_call | solution.py:337
  392.3 11.2 %collective-permute-done.30 = bf16[128,2048]{1,0:T(8,128)(2,1)S(1)} collective-permute-done((bf16[128,2048]{1,0:T(8,128)(2,1)S(1)}, bf16[128,2048]{1,0:T(8,128)(2,1)S(1)}, u32[]{:S(2)}, u32[]{:S(2)}) %collective-permute-start.30) | collective-permute-done | bytes 524320 | tf_op jit(solution)/shard_map/ppermute | solution.py:461
  410.5 14.7 %shard_map.413 = bf16[1024,2048]{1,0:T(8,128)(2,1)} custom-call(bf16[1024,1024]{1,0:T(8,128)(2,1)} %get-tuple-element.574.left, bf16[1024,2048]{1,0:T(8,128)(2,1)} %get-tuple-element.575.right, bf16[1024,1024]{1,0:T(8,128)(2,1)} %get-tuple-element.576.left_other, bf16[1024,2048]{1,0:T(8,128)(2,1)} %get-tuple-element.577.right_other), custom_call_target="tpu_custom_call" | custom-call | tf_op jit(solution)/shard_map/pallas_call | solution.py:337
  450.2 8.4 %shard_map.415 = (bf16[768,2048]{1,0:T(8,128)(2,1)}, bf16[256,2048]{1,0:T(8,128)(2,1)}) custom-call(bf16[1024,1024]{1,0:T(8,128)(2,1)} %get-tuple-element.592.right.hidden, bf16[2048,1024]{1,0:T(8,128)(2,1)} %bitcast.88), custom_call_target="tpu_custom_call" | custom-call | tf_op jit(solution)/shard_map/pallas_call | solution.py:357
  469.5 12.9 %collective-permute-done.38 = bf16[128,2048]{1,0:T(8,128)(2,1)S(1)} collective-permute-done((bf16[128,2048]{1,0:T(8,128)(2,1)}, bf16[128,2048]{1,0:T(8,128)(2,1)S(1)}, u32[]{:S(2)}, u32[]{:S(2)}) %collective-permute-start.38) | collective-permute-done | bytes 524320 | tf_op jit(solution)/shard_map/ppermute | solution.py:461
  497.1 27.0 %shard_map.416 = (bf16[1024,2048]{1,0:T(8,128)(2,1)}, f32[768,2048]{1,0:T(8,128)}, f32[256,2048]{1,0:T(8,128)}, f32[1,2048]{1,0:T(1,128)}) custom-call(bf16[256,2048]{1,0:T(8,128)(2,1)} %copy-done.30, bf16[256,2048]{1,0:T(8,128)(2,1)} %copy-done.23, bf16[256,2048]{1,0:T(8,128)(2,1)} %copy-done.24, ...), custom_call_target="tpu_custom_call" | custom-call | tf_op jit(solution)/shard_map/pallas_call | solution.py:224
  539.3 28.5 %shard_map.417 = (bf16[1024,2048]{1,0:T(8,128)(2,1)}, bf16[768,2048]{1,0:T(8,128)(2,1)}, bf16[256,2048]{1,0:T(8,128)(2,1)}, f32[1,2048]{1,0:T(1,128)}) custom-call(bf16[256,2048]{1,0:T(8,128)(2,1)} %copy-done.49, bf16[256,2048]{1,0:T(8,128)(2,1)} %get-tuple-element.652.refs_1_, bf16[256,2048]{1,0:T(8,128)(2,1)} %get-tuple-element.653.refs_2_, ...), custom_call_target="tpu_custom_call" | custom-call | tf_op jit(solution)/shard_map/pallas_call | solution.py:224
  578.0 14.6 %all-to-all-done.2 = bf16[8,64,1024]{2,1,0:T(8,128)(2,1)S(1)} async-done(((bf16[8,64,1024]{2,1,0:T(8,128)(2,1)}), bf16[8,64,1024]{2,1,0:T(8,128)(2,1)S(1)}, u32[]{:S(2)}, u32[]{:S(2)}) %all-to-all-start.2) | async-done | bytes 1048608 | tf_op jit(solution)/shard_map/all_to_all | solution.py:609
  640.8 11.7 %collective-permute-done.54 = f32[2,4,2,64]{3,1,2,0:T(4,128)S(1)} collective-permute-done((f32[2,4,2,64]{3,1,2,0:T(4,128)S(1)}, f32[2,4,2,64]{3,1,2,0:T(4,128)S(1)}, u32[]{:S(2)}, u32[]{:S(2)}) %collective-permute-start.54) | collective-permute-done | bytes 4128 | tf_op jit(solution)/shard_map/ppermute | solution.py:461
  (446 shorter events, 290.4 us)
Async XLA Ops:
  7.2 92.0 %all-gather.5.cloned.1.call-start = ((), (), s32[]{:S(2)}) async-start(), calls=%async_computation.9 | async-start | bytes 5242880 | tf_op jit(solution)/shard_map/all_gather | solution.py:680
  10.0 234.0 %all-gather.7.cloned.1.call-start = ((), (), s32[]{:S(2)}) async-start(), calls=%async_computation.10 | async-start | bytes 10485760 | tf_op jit(solution)/shard_map/all_gather | solution.py:708
  10.4 26.2 %collective-permute-start = (bf16[256,2048]{1,0:T(8,128)(2,1)S(1)}, bf16[256,2048]{1,0:T(8,128)(2,1)S(1)}, u32[]{:S(2)}, u32[]{:S(2)}) collective-permute-start(bf16[256,2048]{1,0:T(8,128)(2,1)S(1)} %copy-done.9), channel_id=1, source_target_pairs={{0,2},{1,3},{2,0},{3,1},{4,6},{5,7},{6,4},{7,5},{8,10},{9,11},{10,... | collective-permute-start | bytes 3145736 | tf_op jit(solution)/shard_map/ppermute | solution.py:461
  72.6 25.5 %collective-permute-start.10 = (bf16[256,2048]{1,0:T(8,128)(2,1)S(1)}, bf16[256,2048]{1,0:T(8,128)(2,1)}, u32[]{:S(2)}, u32[]{:S(2)}) collective-permute-start(bf16[256,2048]{1,0:T(8,128)(2,1)S(1)} %convert_element_type.279), channel_id=1, source_target_pairs={{0,2},{1,3},{2,0},{3,1},{4,6},{5,7},{6,4},{7,5},{8,10},{9,11},{10,... | collective-permute-start | bytes 3145736 | tf_op jit(solution)/shard_map/ppermute | solution.py:461
  73.9 25.2 %collective-permute-start.11 = (bf16[256,2048]{1,0:T(8,128)(2,1)S(1)}, bf16[256,2048]{1,0:T(8,128)(2,1)}, u32[]{:S(2)}, u32[]{:S(2)}) collective-permute-start(bf16[256,2048]{1,0:T(8,128)(2,1)S(1)} %convert_element_type.279), channel_id=1, source_target_pairs={{0,4},{1,5},{2,6},{3,7},{4,0},{5,1},{6,2},{7,3},{8,12},{9,13},{10,... | collective-permute-start | bytes 3145736 | tf_op jit(solution)/shard_map/ppermute | solution.py:461
  132.2 50.9 %collective-permute-start.13 = (bf16[1024,2048]{1,0:T(8,128)(2,1)}, bf16[1024,2048]{1,0:T(8,128)(2,1)}, u32[]{:S(2)}, u32[]{:S(2)}) collective-permute-start(bf16[1024,2048]{1,0:T(8,128)(2,1)} %convolution_convert_fusion.1), channel_id=1, source_target_pairs={{0,1},{1,0},{2,3},{3,2},{4,5},{5,4},{6,7},{7,6},{8,9},{9,8},{10,11... | collective-permute-start | bytes 12582920 | tf_op jit(solution)/shard_map/ppermute | solution.py:461
  167.2 158.0 %all-gather.9.cloned.1.call-start = ((), (), s32[]{:S(2)}) async-start(), calls=%async_computation.11 | async-start | bytes 5242880 | tf_op jit(solution)/shard_map/all_gather | solution.py:763
  167.4 26.0 %collective-permute-start.23 = (bf16[512,2048]{1,0:T(8,128)(2,1)}, bf16[512,2048]{1,0:T(8,128)(2,1)}, u32[]{:S(2)}, u32[]{:S(2)}) collective-permute-start(bf16[512,2048]{1,0:T(8,128)(2,1)} %constant_dynamic-update-slice_fusion.4), channel_id=1, source_target_pairs={{0,1},{1,0},{2,3},{3,2},{4,5},{5,4},{6,7},{7,6},{8,9},{9,8},{10,11... | collective-permute-start | bytes 6291464 | tf_op jit(solution)/shard_map/ppermute | solution.py:461
  167.9 25.5 %collective-permute-start.21 = (bf16[128,2048]{1,0:T(8,128)(2,1)S(1)}, bf16[128,2048]{1,0:T(8,128)(2,1)S(1)}, u32[]{:S(2)}, u32[]{:S(2)}) collective-permute-start(bf16[128,2048]{1,0:T(8,128)(2,1)S(1)} %copy-done.56), channel_id=1, source_target_pairs={{0,2},{1,3},{2,0},{3,1},{4,6},{5,7},{6,4},{7,5},{8,10},{9,11},{10,... | collective-permute-start | bytes 1572872 | tf_op jit(solution)/shard_map/ppermute | solution.py:461
  206.9 25.1 %collective-permute-start.16 = (bf16[256,2048]{1,0:T(8,128)(2,1)}, bf16[256,2048]{1,0:T(8,128)(2,1)}, u32[]{:S(2)}, u32[]{:S(2)}) collective-permute-start(bf16[256,2048]{1,0:T(8,128)(2,1)} %pad_maximum_fusion.2), channel_id=1, source_target_pairs={{0,2},{1,3},{2,0},{3,1},{4,6},{5,7},{6,4},{7,5},{8,10},{9,11},{10,... | collective-permute-start | bytes 3145736 | tf_op jit(solution)/shard_map/ppermute | solution.py:461
  210.6 221.7 %reduce-scatter.6.cloned.1.call-start = ((), (), s32[]{:S(2)}) async-start(), calls=%async_computation.12 | async-start | bytes 5242880 | tf_op jit(solution)/shard_map/reduce_scatter | solution.py:800
  247.2 25.2 %collective-permute-start.18 = (bf16[256,2048]{1,0:T(8,128)(2,1)S(1)}, bf16[256,2048]{1,0:T(8,128)(2,1)S(1)}, u32[]{:S(2)}, u32[]{:S(2)}) collective-permute-start(bf16[256,2048]{1,0:T(8,128)(2,1)S(1)} %multiply_convert_fusion.refs_0_), channel_id=1, source_target_pairs={{0,2},{1,3},{2,0},{3,1},{4,6},{5,7},{6,4},{7,5},{8,10},{9,11},{10,... | collective-permute-start | bytes 3145736 | tf_op jit(solution)/shard_map/ppermute | solution.py:461
  324.9 246.6 %reduce-scatter.8.cloned.1.call-start = ((), (), s32[]{:S(2)}) async-start(), calls=%async_computation.13 | async-start | bytes 5242880 | tf_op jit(solution)/shard_map/reduce_scatter | solution.py:844
  388.5 183.0 %reduce-scatter.10.cloned.1.call-start = ((), (), s32[]{:S(2)}) async-start(), calls=%async_computation.14 | async-start | bytes 5242880 | tf_op jit(solution)/shard_map/reduce_scatter | solution.py:845
  467.5 150.9 %reduce-scatter.12.cloned.1.call-start = ((), (), s32[]{:S(2)}) async-start(), calls=%async_computation.15 | async-start | bytes 1310720 | tf_op jit(solution)/shard_map/reduce_scatter | solution.py:938
  491.1 33.0 %collective-permute-start.43 = (bf16[256,2048]{1,0:T(8,128)(2,1)}, bf16[256,2048]{1,0:T(8,128)(2,1)}, u32[]{:S(2)}, u32[]{:S(2)}) collective-permute-start(bf16[256,2048]{1,0:T(8,128)(2,1)} %constant_dynamic-update-slice_fusion.20.refs_3_), channel_id=1, source_target_pairs={{0,1},{1,0},{2,3},{3,2},{4,5},{5,4},{6,7},{7,6},{8,9},{9,8},{10,11... | collective-permute-start | bytes 3145736 | tf_op jit(solution)/shard_map/ppermute | solution.py:461
  491.1 33.0 %collective-permute-start.44 = (bf16[128,2048]{1,0:T(8,128)(2,1)}, bf16[128,2048]{1,0:T(8,128)(2,1)}, u32[]{:S(2)}, u32[]{:S(2)}) collective-permute-start(bf16[128,2048]{1,0:T(8,128)(2,1)} %get-tuple-element.618), channel_id=1, source_target_pairs={{0,2},{1,3},{2,0},{3,1},{4,6},{5,7},{6,4},{7,5},{8,10},{9,11},{10,... | collective-permute-start | bytes 1572872 | tf_op jit(solution)/shard_map/ppermute | solution.py:461
  492.3 31.8 %collective-permute-start.45 = (bf16[128,2048]{1,0:T(8,128)(2,1)}, bf16[128,2048]{1,0:T(8,128)(2,1)}, u32[]{:S(2)}, u32[]{:S(2)}) collective-permute-start(bf16[128,2048]{1,0:T(8,128)(2,1)} %get-tuple-element.619), channel_id=1, source_target_pairs={{0,4},{1,5},{2,6},{3,7},{4,0},{5,1},{6,2},{7,3},{8,12},{9,13},{10,... | collective-permute-start | bytes 1572872 | tf_op jit(solution)/shard_map/ppermute | solution.py:461
  528.0 39.8 %collective-permute-start.46 = (bf16[256,2048]{1,0:T(8,128)(2,1)}, bf16[256,2048]{1,0:T(8,128)(2,1)}, u32[]{:S(2)}, u32[]{:S(2)}) collective-permute-start(bf16[256,2048]{1,0:T(8,128)(2,1)} %pad_maximum_fusion.6), channel_id=1, source_target_pairs={{0,2},{1,3},{2,0},{3,1},{4,6},{5,7},{6,4},{7,5},{8,10},{9,11},{10,... | collective-permute-start | bytes 3145736 | tf_op jit(solution)/shard_map/ppermute | solution.py:461
  528.7 39.2 %collective-permute-start.47 = (bf16[256,2048]{1,0:T(8,128)(2,1)}, bf16[256,2048]{1,0:T(8,128)(2,1)}, u32[]{:S(2)}, u32[]{:S(2)}) collective-permute-start(bf16[256,2048]{1,0:T(8,128)(2,1)} %pad_maximum_fusion.7), channel_id=1, source_target_pairs={{0,4},{1,5},{2,6},{3,7},{4,0},{5,1},{6,2},{7,3},{8,12},{9,13},{10,... | collective-permute-start | bytes 3145736 | tf_op jit(solution)/shard_map/ppermute | solution.py:461
  577.2 87.0 %reduce-scatter.14.cloned.1.call-start = ((), (), s32[]{:S(2)}) async-start(), calls=%async_computation.16 | async-start | bytes 3932160 | tf_op jit(solution)/shard_map/reduce_scatter | solution.py:939
  624.0 28.6 %collective-permute-start.52 = (bf16[256,2048]{1,0:T(8,128)(2,1)}, bf16[256,2048]{1,0:T(8,128)(2,1)}, u32[]{:S(2)}, u32[]{:S(2)}) collective-permute-start(bf16[256,2048]{1,0:T(8,128)(2,1)} %pad_maximum_fusion.8), channel_id=1, source_target_pairs={{0,2},{1,3},{2,0},{3,1},{4,6},{5,7},{6,4},{7,5},{8,10},{9,11},{10,... | collective-permute-start | bytes 3145736 | tf_op jit(solution)/shard_map/ppermute | solution.py:461
  626.0 26.6 %collective-permute-start.53 = (bf16[256,2048]{1,0:T(8,128)(2,1)}, bf16[256,2048]{1,0:T(8,128)(2,1)}, u32[]{:S(2)}, u32[]{:S(2)}) collective-permute-start(bf16[256,2048]{1,0:T(8,128)(2,1)} %pad_maximum_fusion.9), channel_id=1, source_target_pairs={{0,4},{1,5},{2,6},{3,7},{4,0},{5,1},{6,2},{7,3},{8,12},{9,13},{10,... | collective-permute-start | bytes 3145736 | tf_op jit(solution)/shard_map/ppermute | solution.py:461
  627.5 25.1 %collective-permute-start.54 = (f32[2,4,2,64]{3,1,2,0:T(4,128)S(1)}, f32[2,4,2,64]{3,1,2,0:T(4,128)S(1)}, u32[]{:S(2)}, u32[]{:S(2)}) collective-permute-start(f32[2,4,2,64]{3,1,2,0:T(4,128)S(1)} %slice.313), channel_id=1, source_target_pairs={{0,2},{1,3},{2,0},{3,1},{4,6},{5,7},{6,4},{7,5},{8,10},{9,11},{10,... | collective-permute-start | bytes 12296 | tf_op jit(solution)/shard_map/ppermute | solution.py:461
  (115 other events, 1424.1 us)
Sparse Core Ops, SparseCore 0:
  10.2 83.4 all-gather.4
  95.8 148.1 all-gather.6
  245.6 78.9 all-gather.8
  326.7 75.2 reduce-scatter.5
  404.3 77.2 reduce-scatter.7
  484.3 77.2 reduce-scatter.9
  573.8 25.0 reduce-scatter.11
  601.1 58.8 reduce-scatter.13

commit v5 on v4

--- a/solution.py
+++ b/solution.py
@@ -459,6 +459,7 @@
             axis, count = ("fsdp", self.fsdp) if mask > 0 else ("dp", self.dp)
             pairs = [(i, i ^ abs(mask)) for i in range(count)]
             came.append(lax.ppermute(value, axis, pairs))
+        self.came = came
         gave, done = [], []
         for work in works:
             gave.append(work())
@@ -591,8 +592,10 @@
         half = rows // 2
         (got,), ((near, other), *gave) = self.window([(others, 1)], first, *works[0])
         pair, across = self.step(functools.partial(self.sum_pair, rows), near, across, got)
-        (upper, lower, own), found = self.window(
-            [(across[:half], 2), (across[half:], 4), (other, 1)], *works[1]
+        (upper, lower, own), (_, *found) = self.window(
+            [(across[:half], 2), (across[half:], 4), (other, 1)],
+            lambda: self.wait(self.came[2]),
+            *works[1],
         )
         gave += found
         beside, above = self.step(functools.partial(self.merge_pair, rows), pair, upper, lower)

time: 684 us -> 692 us (1.012)
    unnamed x153 -> x155, local copies, waits for them, and re-layouts: 18.1 us -> 17.8 us
  transfers between devices with their start and end apart: 70 -> 70, of which waited for: 26 -> 24; matrix products, arithmetic and copies ran while one was open for 25% -> 25% of each run, Pallas kernels for 32% -> 32%
where the time goes in v5:
time: 692 us; the launch traced here: 686 us
  Pallas kernels  217 us (31%)
  waiting for transfers between devices  181 us (26%)
  other arithmetic  90.1 us (13%)
  local copies, waits for them, and re-layouts  84.4 us (12%)
  starting transfers between devices  61.9 us (9%)
  blocking collectives  28.2 us (4%)
  between operations  15.7 us (2%)
  matrix products  7.74 us (1%)
    ppermute x58, waiting for transfers between devices, window(): came.append(lax.ppermute(value, axis, pairs))  143 us
    pallas_call x2, Pallas kernels, attend_back_blocks(): pl.pallas_call(functools.partial(attend_back_kernel, group, not earlier),...  55.7 us
    ppermute x58, starting transfers between devices, window(): came.append(lax.ppermute(value, axis, pairs))  45.1 us
    pallas_call x2, Pallas kernels, expand_back_blocks(): pl.pallas_call(functools.partial(expand_back_kernel, tiles), grid=(tiles...  44.5 us
    pallas_call x3, Pallas kernels, product_pairs(): pl.pallas_call(pairs_kernel, grid=(units // tile,), in_specs=[part, whole...  42.7 us
    pallas_call x2, Pallas kernels, expand_blocks(): pl.pallas_call(functools.partial(expand_kernel, group), grid=(units // ti...  28.5 us
    all_to_all x4, waiting for transfers between devices, exchange(): return lax.all_to_all(blocks, 'fsdp', 0, 0, tiled=True)  26.3 us
    pallas_call x2, Pallas kernels, attend_blocks(): pl.pallas_call(functools.partial(attend_kernel, group), grid=(group,), in...  25.9 us
  transfers between devices with their start and end apart: 70, of which 24 were waited for; matrix products, arithmetic and copies ran while one was open for 25% of the time, Pallas kernels for 32%

profile of v5, /device:TPU:0, one launch (start us, length us, event | category | flops | bytes accessed | tf_op | source)
XLA Modules:
  0.0 685.6 jit_solution(2884792606966714838)
XLA Ops:
  15.4 11.2 %all_gather.15 = bf16[2,4,64]{2,0,1:T(2,128)(2,1)S(1)} all-gather(bf16[2,1,64]{2,0,1:T(2,128)(2,1)S(1)} %copy.100), channel_id=1, replica_groups=mesh['dp'=4,'fsdp'=8] {'dp'}, dimensions={1}, use_global_device_ids=true | all-gather | bytes 1280 | tf_op jit(solution)/shard_map/all_gather | solution.py:689
  44.4 17.0 %all-gather = bf16[2,4,512]{1,0,2:T(2,128)(2,1)S(1)} all-gather(bf16[2,4,64]{1,0,2:T(2,128)(2,1)S(1)} %copy.101), channel_id=2, replica_groups=mesh['dp'=4,'fsdp'=8] {'fsdp'}, dimensions={2}, use_global_device_ids=true | all-gather | bytes 9216 | tf_op jit(solution)/shard_map/all_gather | solution.py:692
  74.6 23.5 %collective-permute-done.10 = bf16[256,2048]{1,0:T(8,128)(2,1)} collective-permute-done((bf16[256,2048]{1,0:T(8,128)(2,1)S(1)}, bf16[256,2048]{1,0:T(8,128)(2,1)}, u32[]{:S(2)}, u32[]{:S(2)}) %collective-permute-start.10) | collective-permute-done | bytes 1048608 | tf_op jit(solution)/shard_map/ppermute | solution.py:461
  113.1 12.9 %shard_map.404 = (bf16[1024,2048]{1,0:T(8,128)(2,1)}, bf16[1024,768]{1,0:T(8,128)(2,1)}, bf16[1024,256]{1,0:T(8,128)(2,1)}) custom-call(bf16[256,2048]{1,0:T(8,128)(2,1)} %collective-permute-done.2.refs_0_.refs_4_, bf16[256,2048]{1,0:T(8,128)(2,1)} %get-tuple-element.656.refs_1_.refs_5_, bf16[256,2048]{1,0:T(8,128)(2,1)} %get-tuple-element.657.refs_2_.refs_6_, ...), custom_call_target="tpu_custom_call" | custom-call | tf_op jit(solution)/shard_map/pallas_call | solution.py:144
  143.4 12.9 %shard_map.405 = (bf16[1024,2048]{1,0:T(8,128)(2,1)}, bf16[1024,768]{1,0:T(8,128)(2,1)}, bf16[1024,256]{1,0:T(8,128)(2,1)}) custom-call(bf16[256,2048]{1,0:T(8,128)(2,1)} %refs_4_, bf16[256,2048]{1,0:T(8,128)(2,1)} %copy-done.7, bf16[256,2048]{1,0:T(8,128)(2,1)} %copy-done.8, bf16[256,2048]{1,0:T(8,128)(2,1)} %copy-done.22, f32[1,2048]{1,0:T(1,128)} %bitcast.115, ...), custom_call_target="tpu_custom_call" | custom-call | tf_op jit(solution)/shard_map/pallas_call | solution.py:144
  171.1 11.7 %all-to-all-done.1 = bf16[8,64,1024]{2,1,0:T(8,128)(2,1)S(1)} async-done(((bf16[8,64,1024]{2,1,0:T(8,128)(2,1)}), bf16[8,64,1024]{2,1,0:T(8,128)(2,1)S(1)}, u32[]{:S(2)}, u32[]{:S(2)}) %all-to-all-start.1) | async-done | bytes 1048608 | tf_op jit(solution)/shard_map/all_to_all | solution.py:612
  193.4 10.6 %collective-permute-done.14 = bf16[128,2048]{1,0:T(8,128)(2,1)S(1)} collective-permute-done((bf16[128,2048]{1,0:T(8,128)(2,1)S(1)}, bf16[128,2048]{1,0:T(8,128)(2,1)S(1)}, u32[]{:S(2)}, u32[]{:S(2)}) %collective-permute-start.14) | collective-permute-done | bytes 524320 | tf_op jit(solution)/shard_map/ppermute | solution.py:461
  213.5 18.3 %collective-permute-done.16 = bf16[256,2048]{1,0:T(8,128)(2,1)} collective-permute-done((bf16[256,2048]{1,0:T(8,128)(2,1)}, bf16[256,2048]{1,0:T(8,128)(2,1)}, u32[]{:S(2)}, u32[]{:S(2)}) %collective-permute-start.16) | collective-permute-done | bytes 1048608 | tf_op jit(solution)/shard_map/ppermute | solution.py:461
  232.9 11.1 %all-gather.7.cloned.1.call-done.refs_4_ = bf16[2,1024,2048]{2,1,0:T(8,128)(2,1)} async-done(((bf16[2,256,2048]{2,1,0:T(8,128)(2,1)}), bf16[2,1024,2048]{2,1,0:T(8,128)(2,1)}) %all-gather.7.cloned.1.call-update) | async-done | bytes 8388624 | tf_op jit(solution)/shard_map/all_gather | solution.py:711
  260.6 11.7 %collective-permute-done.18.refs_1_ = bf16[256,2048]{1,0:T(8,128)(2,1)S(1)} collective-permute-done((bf16[256,2048]{1,0:T(8,128)(2,1)S(1)}, bf16[256,2048]{1,0:T(8,128)(2,1)S(1)}, u32[]{:S(2)}, u32[]{:S(2)}) %collective-permute-start.18) | collective-permute-done | bytes 1048608 | tf_op jit(solution)/shard_map/ppermute | solution.py:461
  278.4 14.3 %shard_map.407 = (bf16[1024,2048]{1,0:T(8,128)(2,1)}, f32[1024,1024]{1,0:T(8,128)}, f32[1024,1024]{1,0:T(8,128)}, bf16[1024,1024]{1,0:T(8,128)(2,1)}) custom-call(bf16[256,2048]{1,0:T(8,128)(2,1)} %copy-done.33, bf16[256,2048]{1,0:T(8,128)(2,1)} %copy-done.25, bf16[256,2048]{1,0:T(8,128)(2,1)} %copy-done.26, bf16[256,2048]{1,0:T(8,128)(2,1)} %copy-done.51, ...), custom_call_target="tpu_custom_call" | custom-call | tf_op jit(solution)/shard_map/pallas_call | solution.py:309
  296.4 14.3 %shard_map.408 = (bf16[1024,2048]{1,0:T(8,128)(2,1)}, f32[1024,1024]{1,0:T(8,128)}, f32[1024,1024]{1,0:T(8,128)}, bf16[1024,1024]{1,0:T(8,128)(2,1)}) custom-call(bf16[256,2048]{1,0:T(8,128)(2,1)} %copy-done.42, bf16[256,2048]{1,0:T(8,128)(2,1)} %get-tuple-element.524.refs_1_, bf16[256,2048]{1,0:T(8,128)(2,1)} %get-tuple-element.525.refs_2_, ...), custom_call_target="tpu_custom_call" | custom-call | tf_op jit(solution)/shard_map/pallas_call | solution.py:309
  310.7 14.1 %shard_map.409 = bf16[2048,1024]{1,0:T(8,128)(2,1)} custom-call(bf16[1024,2048]{1,0:T(8,128)(2,1)} %copy-done.2, bf16[1024,1024]{1,0:T(8,128)(2,1)} %get-tuple-element.592.right.hidden, bf16[1024,2048]{1,0:T(8,128)(2,1)} %constant_dynamic-update-slice_fusion.12.left_other.refs_0_, bf16[1024,1024]{1,0:T(8,128)(2,1)} %get-tuple-element.588.right_other.hidden), custom_call_target="tpu_custom_call" | custom-call | tf_op jit(solution)/shard_map/pallas_call | solution.py:337
  325.1 22.4 %shard_map.410 = (bf16[1024,1024]{1,0:T(8,128)(2,1)}, bf16[1024,1024]{1,0:T(8,128)(2,1)}, bf16[256,2048]{1,0:T(8,128)(2,1)}, bf16[768,2048]{1,0:T(8,128)(2,1)}) custom-call(bf16[1024,2048]{1,0:T(8,128)(2,1)} %constant_dynamic-update-slice_fusion.12.left_other.refs_0_, f32[1024,1024]{1,0:T(8,128)} %get-tuple-element.537.refs_1_, ...), custom_call_target="tpu_custom_call" | custom-call | tf_op jit(solution)/shard_map/pallas_call | solution.py:411
  348.0 22.2 %shard_map.411 = (bf16[1024,1024]{1,0:T(8,128)(2,1)}, bf16[1024,1024]{1,0:T(8,128)(2,1)}, bf16[768,2048]{1,0:T(8,128)(2,1)}, bf16[256,2048]{1,0:T(8,128)(2,1)}) custom-call(bf16[1024,2048]{1,0:T(8,128)(2,1)} %copy-done.2, f32[1024,1024]{1,0:T(8,128)} %get-tuple-element.546.refs_1_, f32[1024,1024]{1,0:T(8,128)} %get-tuple-element.547.refs_2_, ...), custom_call_target="tpu_custom_call" | custom-call | tf_op jit(solution)/shard_map/pallas_call | solution.py:411
  377.5 14.3 %shard_map.412 = bf16[1024,2048]{1,0:T(8,128)(2,1)} custom-call(bf16[1024,1024]{1,0:T(8,128)(2,1)} %get-tuple-element.562.left, bf16[1024,2048]{1,0:T(8,128)(2,1)} %get-tuple-element.575.right, bf16[1024,1024]{1,0:T(8,128)(2,1)} %get-tuple-element.564.left_other, bf16[1024,2048]{1,0:T(8,128)(2,1)} %get-tuple-element.577.right_other), custom_call_target="tpu_custom_call" | custom-call | tf_op jit(solution)/shard_map/pallas_call | solution.py:337
  397.3 14.3 %shard_map.413 = bf16[1024,2048]{1,0:T(8,128)(2,1)} custom-call(bf16[1024,1024]{1,0:T(8,128)(2,1)} %get-tuple-element.574.left, bf16[1024,2048]{1,0:T(8,128)(2,1)} %get-tuple-element.575.right, bf16[1024,1024]{1,0:T(8,128)(2,1)} %get-tuple-element.576.left_other, bf16[1024,2048]{1,0:T(8,128)(2,1)} %get-tuple-element.577.right_other), custom_call_target="tpu_custom_call" | custom-call | tf_op jit(solution)/shard_map/pallas_call | solution.py:337
  415.5 21.5 %collective-permute-done.33 = bf16[256,2048]{1,0:T(8,128)(2,1)} collective-permute-done((bf16[256,2048]{1,0:T(8,128)(2,1)}, bf16[256,2048]{1,0:T(8,128)(2,1)}, u32[]{:S(2)}, u32[]{:S(2)}) %collective-permute-start.33) | collective-permute-done | bytes 1048608 | tf_op jit(solution)/shard_map/ppermute | solution.py:461
  455.8 8.3 %shard_map.415 = (bf16[768,2048]{1,0:T(8,128)(2,1)}, bf16[256,2048]{1,0:T(8,128)(2,1)}) custom-call(bf16[1024,1024]{1,0:T(8,128)(2,1)} %get-tuple-element.592.right.hidden, bf16[2048,1024]{1,0:T(8,128)(2,1)} %bitcast.88), custom_call_target="tpu_custom_call" | custom-call | tf_op jit(solution)/shard_map/pallas_call | solution.py:357
  477.3 12.0 %collective-permute-done.38 = bf16[128,2048]{1,0:T(8,128)(2,1)S(1)} collective-permute-done((bf16[128,2048]{1,0:T(8,128)(2,1)}, bf16[128,2048]{1,0:T(8,128)(2,1)S(1)}, u32[]{:S(2)}, u32[]{:S(2)}) %collective-permute-start.38) | collective-permute-done | bytes 524320 | tf_op jit(solution)/shard_map/ppermute | solution.py:461
  504.2 27.0 %shard_map.416 = (bf16[1024,2048]{1,0:T(8,128)(2,1)}, f32[768,2048]{1,0:T(8,128)}, f32[256,2048]{1,0:T(8,128)}, f32[1,2048]{1,0:T(1,128)}) custom-call(bf16[256,2048]{1,0:T(8,128)(2,1)} %copy-done.30, bf16[256,2048]{1,0:T(8,128)(2,1)} %copy-done.23, bf16[256,2048]{1,0:T(8,128)(2,1)} %copy-done.24, ...), custom_call_target="tpu_custom_call" | custom-call | tf_op jit(solution)/shard_map/pallas_call | solution.py:224
  547.2 28.7 %shard_map.417 = (bf16[1024,2048]{1,0:T(8,128)(2,1)}, bf16[768,2048]{1,0:T(8,128)(2,1)}, bf16[256,2048]{1,0:T(8,128)(2,1)}, f32[1,2048]{1,0:T(1,128)}) custom-call(bf16[256,2048]{1,0:T(8,128)(2,1)} %copy-done.49, bf16[256,2048]{1,0:T(8,128)(2,1)} %get-tuple-element.652.refs_1_, bf16[256,2048]{1,0:T(8,128)(2,1)} %get-tuple-element.653.refs_2_, ...), custom_call_target="tpu_custom_call" | custom-call | tf_op jit(solution)/shard_map/pallas_call | solution.py:224
  586.1 14.6 %all-to-all-done.2 = bf16[8,64,1024]{2,1,0:T(8,128)(2,1)S(1)} async-done(((bf16[8,64,1024]{2,1,0:T(8,128)(2,1)}), bf16[8,64,1024]{2,1,0:T(8,128)(2,1)S(1)}, u32[]{:S(2)}, u32[]{:S(2)}) %all-to-all-start.2) | async-done | bytes 1048608 | tf_op jit(solution)/shard_map/all_to_all | solution.py:612
  648.7 11.7 %collective-permute-done.54 = f32[2,4,2,64]{3,1,2,0:T(4,128)S(1)} collective-permute-done((f32[2,4,2,64]{3,1,2,0:T(4,128)S(1)}, f32[2,4,2,64]{3,1,2,0:T(4,128)S(1)}, u32[]{:S(2)}, u32[]{:S(2)}) %collective-permute-start.54) | collective-permute-done | bytes 4128 | tf_op jit(solution)/shard_map/ppermute | solution.py:461
  (448 shorter events, 289.2 us)
Async XLA Ops:
  7.2 91.9 %all-gather.5.cloned.1.call-start = ((), (), s32[]{:S(2)}) async-start(), calls=%async_computation.9 | async-start | bytes 5242880 | tf_op jit(solution)/shard_map/all_gather | solution.py:683
  10.0 234.0 %all-gather.7.cloned.1.call-start = ((), (), s32[]{:S(2)}) async-start(), calls=%async_computation.10 | async-start | bytes 10485760 | tf_op jit(solution)/shard_map/all_gather | solution.py:711
  10.4 26.2 %collective-permute-start = (bf16[256,2048]{1,0:T(8,128)(2,1)S(1)}, bf16[256,2048]{1,0:T(8,128)(2,1)S(1)}, u32[]{:S(2)}, u32[]{:S(2)}) collective-permute-start(bf16[256,2048]{1,0:T(8,128)(2,1)S(1)} %copy-done.9), channel_id=1, source_target_pairs={{0,2},{1,3},{2,0},{3,1},{4,6},{5,7},{6,4},{7,5},{8,10},{9,11},{10,... | collective-permute-start | bytes 3145736 | tf_op jit(solution)/shard_map/ppermute | solution.py:461
  72.6 25.5 %collective-permute-start.10 = (bf16[256,2048]{1,0:T(8,128)(2,1)S(1)}, bf16[256,2048]{1,0:T(8,128)(2,1)}, u32[]{:S(2)}, u32[]{:S(2)}) collective-permute-start(bf16[256,2048]{1,0:T(8,128)(2,1)S(1)} %convert_element_type.279), channel_id=1, source_target_pairs={{0,2},{1,3},{2,0},{3,1},{4,6},{5,7},{6,4},{7,5},{8,10},{9,11},{10,... | collective-permute-start | bytes 3145736 | tf_op jit(solution)/shard_map/ppermute | solution.py:461
  73.9 25.2 %collective-permute-start.11 = (bf16[256,2048]{1,0:T(8,128)(2,1)S(1)}, bf16[256,2048]{1,0:T(8,128)(2,1)}, u32[]{:S(2)}, u32[]{:S(2)}) collective-permute-start(bf16[256,2048]{1,0:T(8,128)(2,1)S(1)} %convert_element_type.279), channel_id=1, source_target_pairs={{0,4},{1,5},{2,6},{3,7},{4,0},{5,1},{6,2},{7,3},{8,12},{9,13},{10,... | collective-permute-start | bytes 3145736 | tf_op jit(solution)/shard_map/ppermute | solution.py:461
  131.9 50.9 %collective-permute-start.13 = (bf16[1024,2048]{1,0:T(8,128)(2,1)}, bf16[1024,2048]{1,0:T(8,128)(2,1)}, u32[]{:S(2)}, u32[]{:S(2)}) collective-permute-start(bf16[1024,2048]{1,0:T(8,128)(2,1)} %convolution_convert_fusion.1), channel_id=1, source_target_pairs={{0,1},{1,0},{2,3},{3,2},{4,5},{5,4},{6,7},{7,6},{8,9},{9,8},{10,11... | collective-permute-start | bytes 12582920 | tf_op jit(solution)/shard_map/ppermute | solution.py:461
  166.9 158.2 %all-gather.9.cloned.1.call-start = ((), (), s32[]{:S(2)}) async-start(), calls=%async_computation.11 | async-start | bytes 5242880 | tf_op jit(solution)/shard_map/all_gather | solution.py:766
  167.4 25.8 %collective-permute-start.23 = (bf16[512,2048]{1,0:T(8,128)(2,1)}, bf16[512,2048]{1,0:T(8,128)(2,1)}, u32[]{:S(2)}, u32[]{:S(2)}) collective-permute-start(bf16[512,2048]{1,0:T(8,128)(2,1)} %constant_dynamic-update-slice_fusion.4), channel_id=1, source_target_pairs={{0,1},{1,0},{2,3},{3,2},{4,5},{5,4},{6,7},{7,6},{8,9},{9,8},{10,11... | collective-permute-start | bytes 6291464 | tf_op jit(solution)/shard_map/ppermute | solution.py:461
  168.0 25.2 %collective-permute-start.21 = (bf16[128,2048]{1,0:T(8,128)(2,1)S(1)}, bf16[128,2048]{1,0:T(8,128)(2,1)S(1)}, u32[]{:S(2)}, u32[]{:S(2)}) collective-permute-start(bf16[128,2048]{1,0:T(8,128)(2,1)S(1)} %copy-done.56), channel_id=1, source_target_pairs={{0,2},{1,3},{2,0},{3,1},{4,6},{5,7},{6,4},{7,5},{8,10},{9,11},{10,... | collective-permute-start | bytes 1572872 | tf_op jit(solution)/shard_map/ppermute | solution.py:461
  210.3 228.2 %reduce-scatter.6.cloned.1.call-start = ((), (), s32[]{:S(2)}) async-start(), calls=%async_computation.12 | async-start | bytes 5242880 | tf_op jit(solution)/shard_map/reduce_scatter | solution.py:803
  247.2 25.2 %collective-permute-start.18 = (bf16[256,2048]{1,0:T(8,128)(2,1)S(1)}, bf16[256,2048]{1,0:T(8,128)(2,1)S(1)}, u32[]{:S(2)}, u32[]{:S(2)}) collective-permute-start(bf16[256,2048]{1,0:T(8,128)(2,1)S(1)} %multiply_convert_fusion.refs_0_), channel_id=1, source_target_pairs={{0,2},{1,3},{2,0},{3,1},{4,6},{5,7},{6,4},{7,5},{8,10},{9,11},{10,... | collective-permute-start | bytes 3145736 | tf_op jit(solution)/shard_map/ppermute | solution.py:461
  324.9 254.8 %reduce-scatter.10.cloned.1.call-start = ((), (), s32[]{:S(2)}) async-start(), calls=%async_computation.14 | async-start | bytes 5242880 | tf_op jit(solution)/shard_map/reduce_scatter | solution.py:848
  411.6 168.0 %reduce-scatter.8.cloned.1.call-start = ((), (), s32[]{:S(2)}) async-start(), calls=%async_computation.13 | async-start | bytes 5242880 | tf_op jit(solution)/shard_map/reduce_scatter | solution.py:847
  411.7 25.4 %collective-permute-start.33 = (bf16[256,2048]{1,0:T(8,128)(2,1)}, bf16[256,2048]{1,0:T(8,128)(2,1)}, u32[]{:S(2)}, u32[]{:S(2)}) collective-permute-start(bf16[256,2048]{1,0:T(8,128)(2,1)} %pad_maximum_fusion.4), channel_id=1, source_target_pairs={{0,2},{1,3},{2,0},{3,1},{4,6},{5,7},{6,4},{7,5},{8,10},{9,11},{10,... | collective-permute-start | bytes 3145736 | tf_op jit(solution)/shard_map/ppermute | solution.py:461
  413.1 25.4 %collective-permute-start.34 = (bf16[256,2048]{1,0:T(8,128)(2,1)}, bf16[256,2048]{1,0:T(8,128)(2,1)}, u32[]{:S(2)}, u32[]{:S(2)}) collective-permute-start(bf16[256,2048]{1,0:T(8,128)(2,1)} %pad_maximum_fusion.5), channel_id=1, source_target_pairs={{0,4},{1,5},{2,6},{3,7},{4,0},{5,1},{6,2},{7,3},{8,12},{9,13},{10,... | collective-permute-start | bytes 3145736 | tf_op jit(solution)/shard_map/ppermute | solution.py:461
  474.4 152.1 %reduce-scatter.12.cloned.1.call-start = ((), (), s32[]{:S(2)}) async-start(), calls=%async_computation.15 | async-start | bytes 1310720 | tf_op jit(solution)/shard_map/reduce_scatter | solution.py:941
  499.0 32.2 %collective-permute-start.43 = (bf16[256,2048]{1,0:T(8,128)(2,1)}, bf16[256,2048]{1,0:T(8,128)(2,1)}, u32[]{:S(2)}, u32[]{:S(2)}) collective-permute-start(bf16[256,2048]{1,0:T(8,128)(2,1)} %constant_dynamic-update-slice_fusion.20.refs_3_), channel_id=1, source_target_pairs={{0,1},{1,0},{2,3},{3,2},{4,5},{5,4},{6,7},{7,6},{8,9},{9,8},{10,11... | collective-permute-start | bytes 3145736 | tf_op jit(solution)/shard_map/ppermute | solution.py:461
  499.0 32.2 %collective-permute-start.44 = (bf16[128,2048]{1,0:T(8,128)(2,1)}, bf16[128,2048]{1,0:T(8,128)(2,1)}, u32[]{:S(2)}, u32[]{:S(2)}) collective-permute-start(bf16[128,2048]{1,0:T(8,128)(2,1)} %get-tuple-element.618), channel_id=1, source_target_pairs={{0,2},{1,3},{2,0},{3,1},{4,6},{5,7},{6,4},{7,5},{8,10},{9,11},{10,... | collective-permute-start | bytes 1572872 | tf_op jit(solution)/shard_map/ppermute | solution.py:461
  499.2 31.9 %collective-permute-start.45 = (bf16[128,2048]{1,0:T(8,128)(2,1)}, bf16[128,2048]{1,0:T(8,128)(2,1)}, u32[]{:S(2)}, u32[]{:S(2)}) collective-permute-start(bf16[128,2048]{1,0:T(8,128)(2,1)} %get-tuple-element.619), channel_id=1, source_target_pairs={{0,4},{1,5},{2,6},{3,7},{4,0},{5,1},{6,2},{7,3},{8,12},{9,13},{10,... | collective-permute-start | bytes 1572872 | tf_op jit(solution)/shard_map/ppermute | solution.py:461
  535.1 40.8 %collective-permute-start.46 = (bf16[256,2048]{1,0:T(8,128)(2,1)}, bf16[256,2048]{1,0:T(8,128)(2,1)}, u32[]{:S(2)}, u32[]{:S(2)}) collective-permute-start(bf16[256,2048]{1,0:T(8,128)(2,1)} %pad_maximum_fusion.6), channel_id=1, source_target_pairs={{0,2},{1,3},{2,0},{3,1},{4,6},{5,7},{6,4},{7,5},{8,10},{9,11},{10,... | collective-permute-start | bytes 3145736 | tf_op jit(solution)/shard_map/ppermute | solution.py:461
  536.9 39.0 %collective-permute-start.47 = (bf16[256,2048]{1,0:T(8,128)(2,1)}, bf16[256,2048]{1,0:T(8,128)(2,1)}, u32[]{:S(2)}, u32[]{:S(2)}) collective-permute-start(bf16[256,2048]{1,0:T(8,128)(2,1)} %pad_maximum_fusion.7), channel_id=1, source_target_pairs={{0,4},{1,5},{2,6},{3,7},{4,0},{5,1},{6,2},{7,3},{8,12},{9,13},{10,... | collective-permute-start | bytes 3145736 | tf_op jit(solution)/shard_map/ppermute | solution.py:461
  585.3 86.8 %reduce-scatter.14.cloned.1.call-start = ((), (), s32[]{:S(2)}) async-start(), calls=%async_computation.16 | async-start | bytes 3932160 | tf_op jit(solution)/shard_map/reduce_scatter | solution.py:942
  631.9 28.6 %collective-permute-start.52 = (bf16[256,2048]{1,0:T(8,128)(2,1)}, bf16[256,2048]{1,0:T(8,128)(2,1)}, u32[]{:S(2)}, u32[]{:S(2)}) collective-permute-start(bf16[256,2048]{1,0:T(8,128)(2,1)} %pad_maximum_fusion.8), channel_id=1, source_target_pairs={{0,2},{1,3},{2,0},{3,1},{4,6},{5,7},{6,4},{7,5},{8,10},{9,11},{10,... | collective-permute-start | bytes 3145736 | tf_op jit(solution)/shard_map/ppermute | solution.py:461
  633.9 26.6 %collective-permute-start.53 = (bf16[256,2048]{1,0:T(8,128)(2,1)}, bf16[256,2048]{1,0:T(8,128)(2,1)}, u32[]{:S(2)}, u32[]{:S(2)}) collective-permute-start(bf16[256,2048]{1,0:T(8,128)(2,1)} %pad_maximum_fusion.9), channel_id=1, source_target_pairs={{0,4},{1,5},{2,6},{3,7},{4,0},{5,1},{6,2},{7,3},{8,12},{9,13},{10,... | collective-permute-start | bytes 3145736 | tf_op jit(solution)/shard_map/ppermute | solution.py:461
  (116 other events, 1409.9 us)
Sparse Core Ops, SparseCore 0:
  10.2 83.4 all-gather.4
  95.8 148.1 all-gather.6
  245.6 78.9 all-gather.8
  326.7 75.2 reduce-scatter.5
  411.8 74.7 reduce-scatter.9
  488.7 77.2 reduce-scatter.7
  581.9 24.3 reduce-scatter.11
  608.5 58.9 reduce-scatter.13
